TPU v7x, 256 devices: a whole 4x4x8 slice. The times are simulated.
256 devices in a mesh: region: 8 (over x, core), slab: 32 (over y, z).
Axes of the slice: x: 4, y: 4, z: 8, core: 2. Of those that a mesh axis runs over, the one named last changes fastest.
Arguments:
- waveforms: bfloat16 [16384, 48, 128], P(('region', 'slab')), may hold values from -21 to 21, as said below
- neighbours: int32 [16384, 32], P(('region', 'slab')), may hold values from 0 to 16383, as said below
- masks: int32 [16, 16384], replicated, may hold values 0 or 1
- locations: float32 [4, 16384], replicated, may hold values from -5 to 30, as said below
- stations: float32 [3, 16], replicated, may hold values from -15 to 35, as said below
Outputs:
- lag_times: float32 [16384, 512], P(('region', 'slab'))
- gradient: float32 [4, 16384], P(None, ('region', 'slab'))
Inputs may be any that keep to these rules, and one draw needn't show every extreme that they name: `waveforms`: event amplitudes differ from event to event. `neighbours`: columns 0 to 23 name other events of the same device's block of 64 events. The next 6 columns name events on other devices of the same region; of the 384 such references of one device at most 25 lie on any one device, and exactly 25 on some device. Column 30 names an event at the same slab index in the region one index lower (one higher for region 0); the last column one at the same slab index in the region one index higher (one lower for the last region). `locations`: depths lie between 5 and 15. `stations`: depths lie between -1.5 and 0.
All inputs are finite; a program needn't handle non-finite values.
Results may differ from a plain program's by a relative error of at most 0.002.
Values may be sent and summed in bfloat16 or wider, within the bound.
No kernel may reach another device: no remote copies, remote signals or barrier semaphores. Data moves between devices by JAX's collectives and lax.ppermute only.
A program may use at most 128 MiB of HBM per device.

v0:
```python
import jax
import jax.numpy as jnp
from jax import lax
from jax.sharding import PartitionSpec as P

K_LOCAL = 24
K_REGION = 6


SHARPNESS = 0.1
WAVE_SPEED = 0.6


def with_halo(block, sides, width):
    for axis, dim in sides:
        count = lax.axis_size(axis)
        forward = [(i, i + 1) for i in range(count - 1)]
        backward = [(target, source) for source, target in forward]
        low = lax.ppermute(
            lax.slice_in_dim(block, block.shape[dim] - width, None, axis=dim), axis, forward
        )
        high = lax.ppermute(lax.slice_in_dim(block, 0, width, axis=dim), axis, backward)
        block = jnp.concatenate([low, block, high], axis=dim)
    return block


def shifted(block, axis, distance):
    devices = range(lax.axis_size(axis))
    route = [(i - distance, i) for i in devices if i - distance in devices]
    return lax.ppermute(block, axis, route)


def forward_table(samples):
    half_length = samples // 2
    sample_ids = jnp.arange(samples, dtype=jnp.int32)[:, None]
    cos_bins = jnp.arange(half_length + 1, dtype=jnp.int32)[None, :]
    sin_bins = jnp.arange(1, half_length, dtype=jnp.int32)[None, :]
    cos_angle = 2.0 * jnp.pi / samples * (sample_ids * cos_bins % samples).astype(jnp.float32)
    sin_angle = 2.0 * jnp.pi / samples * (sample_ids * sin_bins % samples).astype(jnp.float32)
    table = jnp.concatenate([jnp.cos(cos_angle), -jnp.sin(sin_angle)], axis=1)
    return table.astype(jnp.bfloat16)


def inverse_table(samples):
    half_length = samples // 2
    cos_bins = jnp.arange(half_length + 1, dtype=jnp.int32)[:, None]
    sin_bins = jnp.arange(1, half_length, dtype=jnp.int32)[:, None]
    lag_ids = jnp.arange(samples, dtype=jnp.int32)[None, :]
    factors = (
        jnp.where((cos_bins == 0) | (cos_bins == half_length), 1.0, 2.0).astype(jnp.float32)
        / samples
    )
    cos_angle = 2.0 * jnp.pi / samples * (cos_bins * lag_ids % samples).astype(jnp.float32)
    sin_angle = 2.0 * jnp.pi / samples * (sin_bins * lag_ids % samples).astype(jnp.float32)
    upper_rows = factors * jnp.cos(cos_angle)
    lower_rows = -(2.0 / samples) * jnp.sin(sin_angle)
    return jnp.concatenate([upper_rows, lower_rows], axis=0).astype(jnp.bfloat16)


def lag_values(samples):
    lag_ids = jnp.arange(samples, dtype=jnp.int32)
    return jnp.where(lag_ids < samples // 2, lag_ids, lag_ids - samples).astype(jnp.float32)


def cross_packed(own_spec, partner):
    half_length = own_spec.shape[-1] // 2
    own_values = own_spec.astype(jnp.float32)
    other_values = partner.astype(jnp.float32)
    own_real = own_values[..., : half_length + 1]
    own_imag = own_values[..., half_length + 1 :]
    other_real = other_values[..., : half_length + 1]
    other_imag = other_values[..., half_length + 1 :]
    imag_product = own_imag * other_imag
    widths = [(0, 0)] * (imag_product.ndim - 1) + [(1, 1)]
    real_part = own_real * other_real + jnp.pad(imag_product, widths)
    imag_part = (
        own_real[..., 1:half_length] * other_imag - own_imag * other_real[..., 1:half_length]
    )
    return jnp.concatenate([real_part, imag_part], axis=-1).astype(jnp.bfloat16)


def soft_lags(own_spec, partner, inverse):
    crossed = cross_packed(own_spec, partner)
    layout = crossed.shape
    correlation = jnp.dot(
        crossed.reshape(-1, layout[-1]), inverse, preferred_element_type=jnp.float32
    )
    correlation = correlation.reshape(layout[:-2] + (layout[-2] // 3, 3, layout[-1]))
    scores = SHARPNESS * jnp.sum(correlation, axis=-2)
    weights = jax.nn.softmax(scores, axis=-1)
    return jnp.sum(weights * lag_values(layout[-1]), axis=-1)


def geometry(places, stations):
    offsets = places[:3, :, None] - stations[:, None, :]
    distance = jnp.sqrt(jnp.sum(offsets * offsets, axis=0))
    arrival = places[3][:, None] + distance / WAVE_SPEED
    direction = offsets / (WAVE_SPEED * distance)
    return (arrival, direction)


def per_device(waveforms, neighbours, masks, locations, stations):
    events, channels, samples = waveforms.shape
    neighbour_count = neighbours.shape[1]
    station_count = stations.shape[1]
    slab_count = lax.axis_size("slab")
    region_index = lax.axis_index("region")
    slab_index = lax.axis_index("slab")
    block_start = (region_index * slab_count + slab_index) * events
    spectra = jnp.dot(
        waveforms.reshape(-1, samples), forward_table(samples), preferred_element_type=jnp.float32
    )
    spectra = spectra.astype(jnp.bfloat16).reshape(events, channels, samples)
    inverse = inverse_table(samples)
    border = with_halo(spectra, (("region", 0),), events)
    remote_ids = neighbours[:, K_LOCAL : K_LOCAL + K_REGION].reshape(-1)
    ref_count = remote_ids.shape[0]
    target = remote_ids // events % slab_count
    within = remote_ids % events
    region_rows = target * events + within
    region_pool = lax.all_gather(spectra, "slab", axis=0, tiled=True)
    fetched = jnp.take(region_pool, region_rows, axis=0)
    pool_rows = jnp.concatenate([border, fetched], axis=0)
    local_index = events + neighbours[:, :K_LOCAL] % events
    region_index_rows = 3 * events + jnp.arange(ref_count, dtype=jnp.int32).reshape(
        events, K_REGION
    )
    cross_ids = neighbours[:, K_LOCAL + K_REGION :]
    lower_side = cross_ids // (slab_count * events) < region_index
    cross_index = jnp.where(lower_side, 0, 2 * events) + cross_ids % events
    pool_index = jnp.concatenate([local_index, region_index_rows, cross_index], axis=1)
    group_index = pool_index.reshape(events, neighbour_count // 2, 2).transpose(1, 0, 2)

    def lag_group(row_index):
        partner = jnp.take(pool_rows, row_index.reshape(-1), axis=0).reshape(
            events, 2, channels, samples
        )
        return soft_lags(spectra[:, None], partner, inverse)

    lag_times = lax.map(lag_group, group_index)
    lag_times = lag_times.transpose(1, 0, 2, 3).reshape(events, neighbour_count, station_count)
    own_places = lax.dynamic_slice_in_dim(locations, block_start, events, 1)
    own_arrival, own_dir = geometry(own_places, stations)
    flat_ids = neighbours.reshape(-1)
    part_arrival, part_dir = geometry(jnp.take(locations, flat_ids, axis=1), stations)
    part_arrival = part_arrival.reshape(events, neighbour_count, station_count)
    part_dir = part_dir.reshape(3, events, neighbour_count, station_count)
    own_mask = lax.dynamic_slice_in_dim(masks, block_start, events, 1).astype(jnp.float32).T
    part_mask = (
        jnp.take(masks, flat_ids, axis=1)
        .astype(jnp.float32)
        .T.reshape(events, neighbour_count, station_count)
    )
    residual = (
        own_mask[:, None, :]
        * part_mask
        * (lag_times - (part_arrival - own_arrival[:, None, :]))
        / (neighbour_count * station_count)
    )
    own_sum = jnp.sum(residual, axis=1)
    own_grad = jnp.concatenate(
        [jnp.sum(own_dir * own_sum[None], axis=2), jnp.sum(own_sum, axis=1)[None]], axis=0
    )
    part_grad = -jnp.concatenate(
        [jnp.sum(part_dir * residual[None], axis=3), jnp.sum(residual, axis=2)[None]], axis=0
    )
    event_range = jnp.arange(events, dtype=jnp.int32)
    local_targets = (neighbours[:, :K_LOCAL] % events).reshape(-1)
    local_table = (local_targets[:, None] == event_range[None, :]).astype(jnp.float32)
    local_grad = jnp.dot(
        part_grad[:, :, :K_LOCAL].reshape(4, -1), local_table, precision=lax.Precision.HIGHEST
    )
    remote_grad = part_grad[:, :, K_LOCAL : K_LOCAL + K_REGION].reshape(4, -1).T
    term_table = (
        region_rows[:, None] == jnp.arange(events * lax.axis_size("slab"), dtype=jnp.int32)[None, :]
    ).astype(jnp.float32)
    remote_back = (
        lax.psum_scatter(
            lax.dot_general(
                term_table, remote_grad, (((0,), (0,)), ((), ())), precision=lax.Precision.HIGHEST
            ).astype(jnp.bfloat16),
            "slab",
            scatter_dimension=0,
            tiled=True,
        )
        .astype(jnp.float32)
        .T
    )
    cross_grad = part_grad[:, :, K_LOCAL + K_REGION :].reshape(4, -1)
    cross_targets = (cross_ids % events).reshape(-1)
    hit_table = (cross_targets[:, None] == event_range[None, :]).astype(jnp.float32)
    lower_weight = lower_side.reshape(-1).astype(jnp.float32)
    to_lower = jnp.dot(
        cross_grad * lower_weight[None, :], hit_table, precision=lax.Precision.HIGHEST
    )
    to_upper = jnp.dot(
        cross_grad * (1.0 - lower_weight)[None, :], hit_table, precision=lax.Precision.HIGHEST
    )
    from_upper = shifted(to_lower, "region", -1)
    from_lower = shifted(to_upper, "region", 1)
    gradient = own_grad + local_grad + remote_back + from_upper + from_lower
    return (lag_times.reshape(events, neighbour_count * station_count), gradient)


def solution(mesh):
    in_specs = (P(("region", "slab"), None, None), P(("region", "slab"), None), P(), P(), P())
    out_specs = (P(("region", "slab"), None), P(None, ("region", "slab")))
    return jax.shard_map(
        per_device, mesh=mesh, in_specs=in_specs, out_specs=out_specs, check_vma=False
    )
```

profile of v0, /device:TPU:1, one launch (start us, length us, event | category | flops | bytes accessed | tf_op | source)
XLA Modules:
  0.0 667.6 jit_solution(6596903940394889053)
XLA Ops:
  8.8 1.2 copy.146
  10.0 4.5 collective-permute-start
  14.6 2.8 collective-permute-start.1
  18.1 5.0 copy.153
  23.4 4.7 copy.151
  28.2 9.0 %gather_fusion.3 = f32[2048,4]{1,0:T(8,128)S(1)} fusion(f32[4,16384]{0,1:T(8,128)} %copy.153, s32[2048]{0:T(1024)S(1)} %broadcast_clamp_fusion), kind=kCustom, calls=%fused_computation.3 | custom fusion | bytes 73728 | tf_op jit(solution)/shard_map/jit(_take)/gather | solution.py:145
  38.1 1.3 copy.156
  39.4 11.0 %gather_fusion.2 = s32[2048,16]{1,0:T(8,128)} fusion(s32[16,16384]{0,1:T(8,128)} %copy.151, s32[2048]{0:T(1024)S(1)} %broadcast_clamp_fusion), kind=kCustom, calls=%fused_computation.2 | custom fusion | bytes 270336 | tf_op jit(solution)/shard_map/jit(_take)/gather | solution.py:150
  53.1 144.8 %all-gather.2.cloned.1.call-done = bf16[2048,48,128]{2,1,0:T(8,128)(2,1)} async-done(((bf16[64,48,128]{2,1,0:T(8,128)(2,1)}), bf16[2048,48,128]{2,1,0:T(8,128)(2,1)}) %all-gather.2.cloned.1.call-update) | async-done | bytes 25165840 | tf_op jit(solution)/shard_map/all_gather | solution.py:121
  197.9 11.5 %gather_fusion.1 = bf16[384,48,128]{2,1,0:T(8,128)(2,1)} fusion(bf16[2048,48,128]{2,1,0:T(8,128)(2,1)} %all-gather.2.cloned.1.call-done, s32[1024]{0:T(1024)S(1)} %pad_clamp_fusion.1), kind=kCustom, calls=%fused_computation.1 | custom fusion | bytes 9438720 | tf_op jit(solution)/shard_map/jit(_take)/gather | solution.py:122
  209.4 3.1 broadcast_select_fusion
  212.6 4.5 pad_maximum_fusion
  217.1 224.1 %while.12 = (s32[]{:T(128)}, f32[16,64,2,16]{1,3,2,0:T(8,128)S(1)}, bf16[3072,128]{1,0:T(8,128)(2,1)S(1)}, s32[16,64,2]{1,2,0:T(2,128)S(1)}, bf16[576,48,128]{2,...) while((s32[]{:T(128)}, f32[16,64,2,16]{1,3,2,0:T(8,128)S(1)}, bf16[3072,128]{1,0:T(8,128)(2,1)S(1)}, ...), condition=%wide.region_5.6_spmd, body=%wide.region_0.5_spmd.sunk | while | flops 211411840 | bytes 36690516 | solution.py:140
  217.4 3.9 gather_fusion
  222.6 1.7 slice_multiply_fusion.4
  224.4 1.1 fusion.123
  231.4 3.9 gather_fusion
  236.6 1.7 slice_multiply_fusion.4
  238.4 1.1 fusion.123
  245.4 3.9 gather_fusion
  250.6 1.7 slice_multiply_fusion.4
  252.4 1.1 fusion.123
  259.4 3.9 gather_fusion
  264.7 1.7 slice_multiply_fusion.4
  266.5 1.1 fusion.123
  273.4 3.9 gather_fusion
  278.7 1.7 slice_multiply_fusion.4
  280.5 1.1 fusion.123
  287.4 3.9 gather_fusion
  292.7 1.7 slice_multiply_fusion.4
  294.5 1.1 fusion.123
  301.4 3.9 gather_fusion
  306.7 1.7 slice_multiply_fusion.4
  308.5 1.1 fusion.123
  315.4 3.9 gather_fusion
  320.7 1.7 slice_multiply_fusion.4
  322.5 1.1 fusion.123
  329.4 3.9 gather_fusion
  334.7 1.7 slice_multiply_fusion.4
  336.5 1.1 fusion.123
  343.5 3.9 gather_fusion
  348.7 1.7 slice_multiply_fusion.4
  350.5 1.1 fusion.123
  357.5 3.9 gather_fusion
  362.7 1.7 slice_multiply_fusion.4
  364.5 1.1 fusion.123
  371.5 3.9 gather_fusion
  376.7 1.7 slice_multiply_fusion.4
  385.5 3.9 gather_fusion
  390.7 1.7 slice_multiply_fusion.4
  399.5 3.9 gather_fusion
  404.8 1.7 slice_multiply_fusion.4
  413.5 3.9 gather_fusion
  418.8 1.7 slice_multiply_fusion.4
  427.5 3.9 gather_fusion
  432.8 1.7 slice_multiply_fusion.4
  441.2 1.4 copy.159
  442.6 3.2 fusion.35
  445.8 1.8 copy.152
  447.5 1.3 copy.157
  451.2 1.1 fusion.27
  453.8 3.0 collective-permute-start.2
  457.0 3.0 collective-permute-start.3
  461.3 197.5 %reduce-scatter.4.cloned.1.call-done = bf16[64,4]{1,0:T(8,128)(2,1)} async-done(((bf16[2048,4]{1,0:T(8,128)(2,1)}), bf16[64,4]{1,0:T(8,128)(2,1)}) %reduce-scatter.4.cloned.1.call-update) | async-done | bytes 528
  (403 shorter events, 134.4 us)
Async XLA Ops:
  7.2 1.1 copy-start
  7.2 10.2 %slice-start = ((s32[64,32]{0,1:T(8,128)}), s32[64,6]{0,1:T(8,128)S(1)}, s32[]{:S(2)}) async-start(s32[64,32]{0,1:T(8,128)} %param.8), calls=%async_computation.3 | async-start | bytes 8192 | tf_op jit(solution)/shard_map/slice | solution.py:116
  7.2 10.6 %copy-start.5 = (s32[64,32]{0,1:T(8,128)S(1)}, s32[64,32]{0,1:T(8,128)}, u32[]{:S(2)}) copy-start(s32[64,32]{0,1:T(8,128)} %param.8) | copy-start | bytes 24580
  7.2 10.9 %copy-start.4 = (f32[4,16384]{1,0:T(4,128)S(1)}, f32[4,16384]{1,0:T(4,128)}, u32[]{:S(2)}) copy-start(f32[4,16384]{1,0:T(4,128)} %param.10) | copy-start | bytes 786436
  7.2 190.7 %all-gather.2.cloned.1.call-start = ((), (), s32[]{:S(2)}) async-start(), calls=%async_computation.1 | async-start | bytes 25952256 | tf_op jit(solution)/shard_map/all_gather | solution.py:121
  10.0 648.9 %reduce-scatter.4.cloned.1.call-start = ((), (), s32[]{:S(2)}) async-start(), calls=%async_computation.2 | async-start | bytes 540672
  10.0 202.5 %collective-permute-start = (bf16[64,48,128]{2,1,0:T(8,128)(2,1)}, bf16[64,48,128]{2,1,0:T(8,128)(2,1)}, u32[]{:S(2)}, u32[]{:S(2)}) collective-permute-start(bf16[64,48,128]{2,1,0:T(8,128)(2,1)} %bitcast.100), channel_id=1, source_target_pairs={{0,32},{32,64},{64,96},{96,128},{128,160},{160,192},{192,224},{1,3... | collective-permute-start | bytes 2359304 | tf_op jit(solution)/shard_map/ppermute | solution.py:19
  14.6 198.0 %collective-permute-start.1 = (bf16[64,48,128]{2,1,0:T(8,128)(2,1)}, bf16[64,48,128]{2,1,0:T(8,128)(2,1)}, u32[]{:S(2)}, u32[]{:S(2)}) collective-permute-start(bf16[64,48,128]{2,1,0:T(8,128)(2,1)} %bitcast.101), channel_id=1, source_target_pairs={{32,0},{64,32},{96,64},{128,96},{160,128},{192,160},{224,192},{33,... | collective-permute-start | bytes 2359304 | tf_op jit(solution)/shard_map/ppermute | solution.py:22
  18.1 5.1 copy-start.6
  18.1 5.3 copy-start.3
  209.4 3.1 copy-start.2
  448.8 211.9 %copy-start.1 = (bf16[64,48,128]{2,1,0:T(8,128)(2,1)S(1)}, bf16[64,48,128]{2,1,0:T(8,128)(2,1)}, u32[]{:S(2)}) copy-start(bf16[64,48,128]{2,1,0:T(8,128)(2,1)} %param.7) | copy-start | bytes 2359300
  453.8 205.8 %collective-permute-start.2 = (f32[4,64]{1,0:T(4,128)S(1)}, f32[4,64]{1,0:T(4,128)S(1)}, u32[]{:S(2)}, u32[]{:S(2)}) collective-permute-start(f32[4,64]{1,0:T(4,128)S(1)} %fusion.52), channel_id=1, source_target_pairs={{32,0},{64,32},{96,64},{128,96},{160,128},{192,160},{224,192},{33,... | collective-permute-start | bytes 3080 | tf_op jit(solution)/shard_map/ppermute | solution.py:30
  457.0 202.6 %collective-permute-start.3 = (f32[4,64]{1,0:T(4,128)S(1)}, f32[4,64]{1,0:T(4,128)S(1)}, u32[]{:S(2)}, u32[]{:S(2)}) collective-permute-start(f32[4,64]{1,0:T(4,128)S(1)} %fusion.50), channel_id=1, source_target_pairs={{0,32},{32,64},{64,96},{96,128},{128,160},{160,192},{192,224},{1,3... | collective-permute-start | bytes 3080 | tf_op jit(solution)/shard_map/ppermute | solution.py:30
Sparse Core Ops, SparseCore 0:
  10.6 187.2 all-gather.1
  453.5 205.2 reduce-scatter.3
where the time goes:
time: 673 us; the launch traced here: 668 us
  waiting for transfers between devices  342 us (51%)
  local copies, waits for them, and re-layouts  192 us (29%)
  other arithmetic  83.9 us (12%)
  matrix products  19.5 us (3%)
  between operations  14.4 us (2%)
  starting transfers between devices  13.4 us (2%)
    unnamed x3, waiting for transfers between devices  198 us
    all_gather x1, waiting for transfers between devices, per_device(): region_pool = lax.all_gather(spectra, 'slab', axis=0, tiled=True)  145 us
    gather x16, local copies, waits for them, and re-layouts, lag_group(): jnp.take(pool_rows, row_index.reshape(-1), axis=0)  61.8 us
    concatenate x32, local copies, waits for them, and re-layouts, cross_packed(): return jnp.concatenate([real_part, imag_part], axis=-1).astype(jnp.bfloat16)  32.6 us
    mul x16, other arithmetic, cross_packed(): imag_product = own_imag * other_imag  27 us
    another operation x32, local copies, waits for them, and re-layouts  19.5 us
    another operation x20, other arithmetic  19.1 us
    div x16, other arithmetic, soft_lags(): weights = jax.nn.softmax(scores, axis=-1)  18.1 us
  transfers between devices with their start and end apart: 6, of which 2 were waited for; matrix products, arithmetic and copies ran while one was open for 8% of the time, Pallas kernels for 0%

commit v1 on v0

v1 whole, which is shorter than its diff:
```python
import functools

import jax
import jax.numpy as jnp
import ml_dtypes
import numpy as np
from jax import lax
from jax.experimental import pallas as pl
from jax.experimental.pallas import tpu as pltpu
from jax.sharding import PartitionSpec as P

K_LOCAL = 24
K_REGION = 6
K_CROSS = 2
K_HOME = K_LOCAL + K_CROSS
COMPONENTS = 3
LANES = 128

SHARPNESS = 0.1
WAVE_SPEED = 0.6
EXPONENT_SCALE = SHARPNESS * 1.4426950408889634

F32 = jnp.float32
BF16 = jnp.bfloat16
BY_LAST = (((1,), (1,)), ((), ()))
VMEM_BYTES = 56 * 1024 * 1024


def forward_table(samples):
    half_length = samples // 2
    sample_ids = np.arange(samples)[:, None]
    cos_bins = np.arange(half_length + 1)[None, :]
    sin_bins = np.arange(1, half_length)[None, :]
    cos_angle = 2.0 * np.pi / samples * (sample_ids * cos_bins % samples)
    sin_angle = 2.0 * np.pi / samples * (sample_ids * sin_bins % samples)
    table = np.concatenate([np.cos(cos_angle), -np.sin(sin_angle)], axis=1)
    return table.astype(np.float32).astype(ml_dtypes.bfloat16)


def inverse_table(samples):
    half_length = samples // 2
    cos_bins = np.arange(half_length + 1)[:, None]
    sin_bins = np.arange(1, half_length)[:, None]
    lag_ids = np.arange(samples)[None, :]
    factors = np.where((cos_bins == 0) | (cos_bins == half_length), 1.0, 2.0) / samples
    cos_angle = 2.0 * np.pi / samples * (cos_bins * lag_ids % samples)
    sin_angle = 2.0 * np.pi / samples * (sin_bins * lag_ids % samples)
    table = np.concatenate(
        [factors * np.cos(cos_angle), -(2.0 / samples) * np.sin(sin_angle)], axis=0
    )
    return table.astype(np.float32).astype(ml_dtypes.bfloat16)


def inverse_rows(samples):
    table = inverse_table(samples).T
    real, imag = table[:, : samples // 2], table[:, samples // 2 :]
    return np.concatenate([real, real, imag, imag, table], axis=1)


def lag_values(samples):
    lag_ids = np.arange(samples)
    values = np.where(lag_ids < samples // 2, lag_ids, lag_ids - samples)
    return np.broadcast_to(values[:, None], (samples, LANES)).astype(np.float32)


def arrange(first, second):
    half = first.shape[-1] // 2
    lane = lax.broadcasted_iota(jnp.int32, first.shape, first.ndim - 1)
    real = jnp.where(lane < half, first, pltpu.roll(second, half, second.ndim - 1))
    imag = jnp.where(lane < half, pltpu.roll(first, half, first.ndim - 1), second)
    return real, imag


def swapped(spec):
    return pltpu.roll(spec, spec.shape[-1] // 2, spec.ndim - 1)


def multipliers(real, imag, packed):
    half = packed.shape[-1] // 2
    lane = lax.broadcasted_iota(jnp.int32, packed.shape, packed.ndim - 1)
    edge = (lane == 0) | (lane == half)
    turned = swapped(packed)
    packed_real = jnp.where(lane <= half, packed, turned)
    packed_imag = jnp.where(edge, 0.0, jnp.where(lane < half, turned, -packed))
    return real, jnp.where(edge, imag, real), jnp.where(edge, 0.0, imag), packed_real, packed_imag


def cross(own, partner):
    real, real_edge, imag, packed_real, packed_imag = own
    other_real, other_imag, other, other_swapped = partner
    return (
        real * other_real + imag * other_imag,
        real_edge * other_imag - imag * other_real,
        packed_real * other + packed_imag * other_swapped,
    )


def soft_lags(crossed, inverse, values):
    corr = lax.dot_general(inverse, crossed, BY_LAST, preferred_element_type=F32)
    top = jnp.max(corr, axis=0, keepdims=True)
    weights = jnp.exp2((corr - top) * EXPONENT_SCALE)
    total = jnp.sum(weights, axis=0, keepdims=True)
    moment = jnp.sum(weights * values, axis=0, keepdims=True)
    return moment / total


def two_parts(x):
    high = x.astype(BF16)
    return high, (x - high.astype(F32)).astype(BF16)


def transform(wave_ref, table_ref, scr):
    block = 384

    def step(k, carry):
        rows = pl.ds(pl.multiple_of(k * block, block), block)
        spec = jnp.dot(wave_ref[rows, :], table_ref[...], preferred_element_type=F32)
        scr[rows, :] = spec.astype(BF16).astype(F32)
        return carry

    lax.fori_loop(0, wave_ref.shape[0] // block, step, 0)


def payload_kernel(wave_ref, table_ref, ids_ref, out_ref, scr):
    stations = out_ref.shape[0] // 2
    events = ids_ref.shape[0]
    part = events // 2
    channels = stations * COMPONENTS
    transform(wave_ref, table_ref, scr)
    for s in range(stations):
        first, second, third = (
            scr[pl.ds(COMPONENTS * s + c, events, stride=channels), :] for c in range(COMPONENTS)
        )
        for k, rows in enumerate((*arrange(first, second), third)):
            rows = rows.astype(BF16)
            out_ref[s, k * events : (k + 1) * events, :] = rows
            out_ref[stations + s, k * events : (k + 1) * events, :] = rows
    ids = ids_ref[...].T[K_LOCAL : K_LOCAL + K_REGION]
    tail = out_ref.shape[1] - COMPONENTS * events
    for h in range(2):
        mine = ids[:, h * part : (h + 1) * part]
        row = jnp.concatenate([mine[n : n + 1] for n in range(K_REGION)], axis=1)
        row = jnp.concatenate([row, jnp.zeros((1, 2 * LANES - row.shape[1]), jnp.int32)], axis=1)
        source, event = row // events % (2 * stations), row % events
        rows = jnp.concatenate(
            [source[:, :LANES], source[:, LANES:], event[:, :LANES], event[:, LANES:]]
            + [jnp.zeros((tail - 4, LANES), jnp.int32)],
            axis=0,
        )
        rows = rows.astype(F32).astype(BF16)
        for s in range(stations):
            out_ref[h * stations + s, COMPONENTS * events :, :] = rows


def by_event_kernel(wave_ref, table_ref, out_ref, scr):
    events, _, stations, _ = out_ref.shape
    channels = stations * COMPONENTS
    transform(wave_ref, table_ref, scr)

    def one_event(event, carry):
        first, second, third = (
            scr[pl.ds(event * channels + c, stations, stride=COMPONENTS), :]
            for c in range(COMPONENTS)
        )
        for k, rows in enumerate((*arrange(first, second), third)):
            out_ref[event, k] = rows.astype(BF16)
        return carry

    lax.fori_loop(0, events, one_event, 0, unroll=4)


BATCH = 4


def home_kernel(
    pool_ids,
    id_row_ref,
    low_ref,
    own_ref,
    high_ref,
    partner_ref,
    pick_ref,
    inverse_ref,
    values_ref,
    arrival_ref,
    mask_ref,
    lag_ref,
    sums_ref,
    to_low_ref,
    to_high_ref,
    pool,
    crossed,
    partner_rows,
    residuals,
    spread,
    sems,
):
    events = own_ref.shape[0]
    stations = own_ref.shape[2]
    width = K_HOME * stations
    copies = [
        pltpu.make_async_copy(
            ref, pool.at[pl.ds(k * events, events), pl.ds(0, COMPONENTS)], sems.at[k]
        )
        for k, ref in enumerate((low_ref, own_ref, high_ref))
    ]
    for copy in copies:
        copy.start()
    for copy in copies:
        copy.wait()

    def swap(event, carry):
        pool[event, COMPONENTS] = swapped(pool[event, COMPONENTS - 1].astype(F32)).astype(BF16)
        return carry

    lax.fori_loop(0, 3 * events, swap, 0, unroll=8)
    values = jnp.tile(values_ref[...], (1, BATCH * width // LANES))

    def some_events(step, carry):
        for b in range(BATCH):
            event = step * BATCH + b
            own = multipliers(*(pool[events + event, k].astype(F32) for k in range(COMPONENTS)))
            for n in range(K_HOME):
                j = pool_ids[event * K_HOME + n]
                partner = [pool[j, k].astype(F32) for k in range(COMPONENTS + 1)]
                rows = slice(b * width + n * stations, b * width + (n + 1) * stations)
                for k, values_k in enumerate(cross(own, partner)):
                    crossed[rows, k * LANES : (k + 1) * LANES] = values_k.astype(BF16)
                partner_rows[rows, :] = partner_ref[j]
        lags = soft_lags(crossed[...], inverse_ref[...], values)
        picks = lax.dot_general(
            pick_ref[...], partner_rows[...], BY_LAST, preferred_element_type=F32
        )
        for b in range(BATCH):
            row = pl.ds(step * BATCH + b, 1)
            lag = lags[:, b * width : (b + 1) * width]
            picked = picks[:, b * width : (b + 1) * width]
            local = K_LOCAL * stations
            gap = jnp.zeros((1, K_REGION * stations), F32)
            lag_ref[row, :] = jnp.concatenate([lag[:, :local], gap, lag[:, local:]], axis=1)
            residuals[row, :] = (
                mask_ref[row, :]
                * picked[1:2]
                * (lag - (picked[0:1] - arrival_ref[row, :]))
                * (1.0 / lag_ref.shape[1])
            )
        return carry

    lax.fori_loop(0, events // BATCH, some_events, 0)

    residual = residuals[...]
    column = lax.broadcasted_iota(jnp.int32, (events, width), 1) // stations
    for n in range(K_HOME):
        high, low = two_parts(jnp.where(column == n, residual, 0.0))
        spread[n * events : (n + 1) * events, :width] = high
        spread[n * events : (n + 1) * events, width:] = low
    pool_rows = lax.broadcasted_iota(jnp.int32, (3 * events, K_HOME * events), 0)
    hits = jnp.where(id_row_ref[...] == pool_rows, 1.0, 0.0).astype(BF16)
    gathered = jnp.dot(hits, spread[...], preferred_element_type=F32)
    gathered = gathered[:, :width] + gathered[:, width:]
    station = lax.broadcasted_iota(jnp.int32, (stations, width), 0)
    lane = lax.broadcasted_iota(jnp.int32, (stations, width), 1) % stations
    fold = jnp.where(station == lane, 1.0, 0.0)
    fold_dot = functools.partial(
        lax.dot_general,
        dimension_numbers=BY_LAST,
        precision=lax.Precision.HIGHEST,
        preferred_element_type=F32,
    )
    own_sums = fold_dot(fold, residual)
    low_sums = fold_dot(fold, gathered[:events])
    in_sums = fold_dot(fold, gathered[events : 2 * events])
    high_sums = fold_dot(fold, gathered[2 * events :])
    sums_ref[...] = own_sums - in_sums
    to_low_ref[...] = low_sums
    to_high_ref[...] = high_sums


def task_kernel(
    half_ref,
    spec_ref,
    tables_ref,
    arrival_ref,
    mask_ref,
    inverse_ref,
    values_ref,
    home_ref,
    out_ref,
    table,
    fetched,
    crossed,
    id_rows,
    ids,
    sem,
):
    sources, payload, _ = spec_ref.shape
    events = tables_ref.shape[0] // 4
    part = events // 2
    span = K_REGION * part
    width = 2 * span
    half = half_ref[0]

    def read_ids(source, carry):
        tail = spec_ref[source, COMPONENTS * events :, :].astype(F32)
        rows = (tail[:2] * events + tail[2:4]).astype(jnp.int32)
        id_rows[pl.ds(2 * source, 1), :] = rows[:1]
        id_rows[pl.ds(2 * source + 1, 1), :] = rows[1:]
        return carry

    lax.fori_loop(0, sources, read_ids, 0)
    copy = pltpu.make_async_copy(id_rows, ids, sem)
    copy.start()

    def fill(source, carry):
        rows = [
            spec_ref[source, k * events : (k + 1) * events, :].astype(F32)
            for k in range(COMPONENTS)
        ]
        rows.append(swapped(rows[-1]))
        base = source * (events * 8)
        for k, values_k in enumerate(rows):
            table[pl.ds(base + k, events, stride=8), :] = values_k
            table[pl.ds(base + 4 + k, events, stride=8), :] = values_k
        return carry

    lax.fori_loop(0, sources, fill, 0)
    copy.wait()

    values = jnp.tile(values_ref[...], (1, width // LANES))
    upper = lax.broadcasted_iota(jnp.int32, (8, LANES), 0) < 4
    source_rows = lax.broadcasted_iota(jnp.int32, (sources, width), 0)
    event_rows = lax.broadcasted_iota(jnp.int32, (events, width), 0)
    lane = lax.broadcasted_iota(jnp.int32, (1, width), 1)
    out_lane = lax.broadcasted_iota(jnp.int32, (1, LANES), 1)
    own_event = lane % part + half * part

    def two_sources(step, sums):
        for q in range(0, width, 2):
            row, column = q // span * 2 + q % span // LANES, q % span % LANES
            first = ids[step * 4 + row, column]
            second = ids[step * 4 + row, column + 1]
            first = table[pl.ds(pl.multiple_of(first * 8, 8), 8), :]
            second = table[pl.ds(pl.multiple_of(second * 8, 8), 8), :]
            fetched[q * 4 : q * 4 + 8, :] = jnp.where(upper, first, second)
        for u in range(2):
            own = multipliers(
                *(
                    spec_ref[
                        2 * step + u,
                        pl.ds(pl.multiple_of(k * events + half * part, part), part),
                        :,
                    ].astype(F32)
                    for k in range(COMPONENTS)
                )
            )
            for n in range(K_REGION):
                start = u * span + n * part
                partner = [
                    fetched[pl.ds(start * 4 + k, part, stride=4), :]
                    for k in range(COMPONENTS + 1)
                ]
                for k, values_k in enumerate(cross(own, partner)):
                    crossed[start : start + part, k * LANES : (k + 1) * LANES] = values_k.astype(
                        BF16
                    )
        lag = soft_lags(crossed[...], inverse_ref[...], values)
        out_ref[2 * step, :, :LANES] = lag[:, :LANES]
        out_ref[2 * step + 1, :, :LANES] = lag[:, span : span + LANES]
        for u in range(2):
            rest = lag[:, u * span + LANES : (u + 1) * span]
            out_ref[2 * step + u, :, LANES : LANES + rest.shape[1]] = rest
        id_row = jnp.concatenate(
            [
                piece
                for u in range(2)
                for piece in (
                    id_rows[pl.ds(4 * step + 2 * u, 1), :],
                    id_rows[pl.ds(4 * step + 2 * u + 1, 1), :][:, : span - LANES],
                )
            ],
            axis=1,
        )
        from_source = source_rows == id_row // events
        from_event = event_rows == id_row % events
        looked_up = jnp.dot(
            tables_ref[...],
            jnp.where(from_source, 1.0, 0.0).astype(BF16),
            preferred_element_type=F32,
        )
        arrival = looked_up[:events] + looked_up[events : 2 * events]
        arrival = arrival + looked_up[2 * events : 3 * events]
        arrival = jnp.sum(jnp.where(from_event, arrival, 0.0), axis=0, keepdims=True)
        mask = jnp.where(from_event, looked_up[3 * events :], 0.0)
        mask = jnp.sum(mask, axis=0, keepdims=True)
        row = pl.ds(step, 1)
        residual = (
            mask_ref[row, :]
            * mask
            * (lag - (arrival - arrival_ref[row, :]))
            * (1.0 / ((K_HOME + K_REGION) * (sources // 2)))
        )
        own_source = lane // span + 2 * step
        for sign, by_source, by_event in (
            (-1.0, from_source, from_event),
            (1.0, source_rows == own_source, event_rows == own_event),
        ):
            high, low = two_parts(jnp.where(by_source, sign * residual, 0.0))
            where_event = jnp.where(by_event, 1.0, 0.0).astype(BF16)
            for term in (high, low):
                sums = sums + lax.dot_general(
                    term, where_event, BY_LAST, preferred_element_type=F32
                )
        return sums

    sums = lax.fori_loop(0, sources // 2, two_sources, jnp.zeros((sources, events), F32))
    out_ref[:, 0, span:] = sums


def final_kernel(
    remote_ref, lag_in_ref, sums_ref, low_ref, high_ref, place_ref, stations_ref, lag_ref, grad_ref
):
    events = lag_ref.shape[0]
    stations = sums_ref.shape[0]
    part = events // 2
    span = K_REGION * part
    lag_ref[...] = lag_in_ref[...]
    for h in range(2):
        turned = remote_ref[h * stations : (h + 1) * stations, 0, :span].T
        for n in range(K_REGION):
            start = (K_LOCAL + n) * stations
            lag_ref[h * part : (h + 1) * part, start : start + stations] = turned[
                n * part : (n + 1) * part
            ]
    sums = sums_ref[...] - low_ref[...] - high_ref[...]
    sums = sums + remote_ref[:stations, 0, span:] + remote_ref[stations:, 0, span:]
    offsets = [place_ref[c : c + 1, :] - stations_ref[:, c : c + 1] for c in range(3)]
    distance = jnp.sqrt(sum(offset * offset for offset in offsets))
    for c in range(3):
        direction = offsets[c] / (WAVE_SPEED * distance)
        grad_ref[c : c + 1, :] = jnp.sum(direction * sums, axis=0, keepdims=True)
    grad_ref[3:4, :] = jnp.sum(sums, axis=0, keepdims=True)


def arrivals(places, stations):
    offsets = places[:3, :, None] - stations[:, None, :]
    distance = jnp.sqrt(jnp.sum(offsets * offsets, axis=0))
    return places[3][:, None] + distance / WAVE_SPEED


def three_parts(x):
    high = lax.reduce_precision(x, 8, 7)
    middle = lax.reduce_precision(x - high, 8, 7)
    low = x - high - middle
    return high, middle, low


def vmem(count):
    return [pl.BlockSpec(memory_space=pltpu.VMEM)] * count


def shape(dims, dtype=F32):
    return jax.ShapeDtypeStruct(dims, dtype)


def shifted(block, axis, distance):
    devices = range(lax.axis_size(axis))
    route = [(i - distance, i) for i in devices if i - distance in devices]
    return lax.ppermute(block, axis, route)


def per_device(waveforms, neighbours, masks, locations, stations):
    events, channels, samples = waveforms.shape
    neighbour_count = neighbours.shape[1]
    station_count = stations.shape[1]
    slab_count = lax.axis_size("slab")
    region_events = slab_count * events
    region_index = lax.axis_index("region")
    slab_index = lax.axis_index("slab")
    block_start = region_index * region_events + slab_index * events
    half = slab_index // station_count
    my_station = slab_index % station_count
    part = events // 2
    span = K_REGION * part
    params = pltpu.CompilerParams(vmem_limit_bytes=VMEM_BYTES)
    inverse = jnp.asarray(inverse_rows(samples))
    values = jnp.asarray(lag_values(samples))

    wave_rows = waveforms.reshape(-1, samples)
    table = jnp.asarray(forward_table(samples))
    payload = pl.pallas_call(
        payload_kernel,
        out_shape=shape((2 * station_count, COMPONENTS * events + 8, samples), BF16),
        in_specs=vmem(3),
        out_specs=vmem(1)[0],
        scratch_shapes=[pltpu.VMEM((events * channels, samples), F32)],
        compiler_params=params,
        name="payload",
    )(wave_rows, table, neighbours)
    task_spec = lax.all_to_all(payload, "slab", 0, 0, tiled=True)
    by_event = pl.pallas_call(
        by_event_kernel,
        out_shape=shape((events, COMPONENTS, station_count, samples), BF16),
        in_specs=vmem(2),
        out_specs=vmem(1)[0],
        scratch_shapes=[pltpu.VMEM((events * channels, samples), F32)],
        compiler_params=params,
        name="by_event",
    )(wave_rows, table)
    low_spec = shifted(by_event, "region", 1)
    high_spec = shifted(by_event, "region", -1)

    starts = [
        jnp.clip(region_index + k, 0, lax.axis_size("region") - 1) * region_events
        + slab_index * events
        for k in (-1, 0, 1)
    ]
    near_places = jnp.concatenate(
        [lax.dynamic_slice_in_dim(locations, start, events, 1) for start in starts], axis=1
    )
    near_masks = jnp.concatenate(
        [lax.dynamic_slice_in_dim(masks, start, events, 1) for start in starts], axis=1
    ).astype(F32)
    near_arrival = arrivals(near_places, stations)
    partner_rows = jnp.stack([*three_parts(near_arrival), near_masks.T], axis=-1).astype(BF16)
    partner_rows = jnp.pad(partner_rows, ((0, 0), (0, 0), (0, LANES - 4)))
    pick = np.zeros((8, LANES), ml_dtypes.bfloat16)
    pick[0, :3] = 1
    pick[1, 3] = 1
    own_places = near_places[:, events : 2 * events]
    own_arrival = jnp.tile(near_arrival[events : 2 * events], (1, K_HOME))
    own_mask = jnp.tile(near_masks[:, events : 2 * events].T, (1, K_HOME))
    cross_ids = neighbours[:, K_LOCAL + K_REGION :]
    lower_side = cross_ids // region_events < region_index
    pool_ids = jnp.concatenate(
        [
            events + neighbours[:, :K_LOCAL] % events,
            jnp.where(lower_side, 0, 2 * events) + cross_ids % events,
        ],
        axis=1,
    )
    width = K_HOME * station_count
    lag_home, sums, to_low, to_high = pl.pallas_call(
        home_kernel,
        out_shape=(
            shape((events, neighbour_count * station_count)),
            shape((station_count, events)),
            shape((station_count, events)),
            shape((station_count, events)),
        ),
        in_specs=[pl.BlockSpec(memory_space=pltpu.SMEM)]
        + vmem(1)
        + [pl.BlockSpec(memory_space=pl.ANY)] * 3
        + vmem(6),
        out_specs=vmem(4),
        scratch_shapes=[
            pltpu.VMEM((3 * events, COMPONENTS + 1, station_count, samples), BF16),
            pltpu.VMEM((BATCH * width, COMPONENTS * samples), BF16),
            pltpu.VMEM((BATCH * width, LANES), BF16),
            pltpu.VMEM((events, width), F32),
            pltpu.VMEM((K_HOME * events, 2 * width), BF16),
            pltpu.SemaphoreType.DMA((3,)),
        ],
        compiler_params=params,
        cost_estimate=pl.CostEstimate(flops=10**10, bytes_accessed=10**7, transcendentals=10**7),
        name="home",
    )(
        pool_ids.reshape(-1),
        pool_ids.T.reshape(1, -1),
        low_spec,
        by_event,
        high_spec,
        partner_rows,
        jnp.asarray(pick),
        inverse,
        values,
        own_arrival,
        own_mask,
    )
    from_high = shifted(to_low, "region", -1)
    from_low = shifted(to_high, "region", 1)

    region_places = lax.dynamic_slice_in_dim(
        locations, region_index * region_events, region_events, 1
    )
    station_place = lax.dynamic_slice_in_dim(stations, my_station, 1, 1)
    task_arrival = arrivals(region_places, station_place)[:, 0].reshape(slab_count, events)
    task_mask = (
        lax.dynamic_slice(
            masks, (my_station, region_index * region_events), (1, region_events)
        )
        .reshape(slab_count, events)
        .astype(F32)
    )
    tables = jnp.concatenate([*three_parts(task_arrival), task_mask], axis=1).T.astype(BF16)

    def per_pair(rows):
        rows = lax.dynamic_slice_in_dim(rows, half * part, part, 1)
        return jnp.tile(rows, (1, K_REGION)).reshape(slab_count // 2, 2 * span)

    results = pl.pallas_call(
        task_kernel,
        out_shape=shape((slab_count, 1, span + events)),
        in_specs=[pl.BlockSpec(memory_space=pltpu.SMEM)] + vmem(6)
        + [pl.BlockSpec(memory_space=pl.ANY)],
        out_specs=vmem(1)[0],
        scratch_shapes=[
            pltpu.VMEM((region_events * 8, LANES), F32),
            pltpu.VMEM((2 * span * 4, LANES), F32),
            pltpu.VMEM((2 * span, COMPONENTS * samples), BF16),
            pltpu.VMEM((2 * slab_count, LANES), jnp.int32),
            pltpu.SMEM((2 * slab_count, LANES), jnp.int32),
            pltpu.SemaphoreType.DMA,
        ],
        compiler_params=params,
        cost_estimate=pl.CostEstimate(flops=10**10, bytes_accessed=10**7, transcendentals=10**7),
        name="task",
    )(
        half.reshape(1),
        task_spec,
        tables,
        per_pair(task_arrival),
        per_pair(task_mask),
        inverse,
        values,
        sums,
    )
    remote = lax.all_to_all(results, "slab", 0, 0, tiled=True)
    return pl.pallas_call(
        final_kernel,
        out_shape=(
            shape((events, neighbour_count * station_count)),
            shape((4, events)),
        ),
        in_specs=vmem(7),
        out_specs=vmem(2),
        compiler_params=params,
        name="final",
    )(remote, lag_home, sums, from_low, from_high, own_places, stations.T)


def solution(mesh):
    in_specs = (P(("region", "slab"), None, None), P(("region", "slab"), None), P(), P(), P())
    out_specs = (P(("region", "slab"), None), P(None, ("region", "slab")))
    return jax.shard_map(
        per_device, mesh=mesh, in_specs=in_specs, out_specs=out_specs, check_vma=False
    )
```

time: 673 us -> 110 us (0.16)
  waiting for transfers between devices: 342 us -> 5.1 us
  local copies, waits for them, and re-layouts: 192 us -> 14.1 us
  other arithmetic: 83.9 us -> 2.4 us
  Pallas kernels: 0 us -> 55.5 us
  matrix products: 19.5 us -> 0 us
  starting transfers between devices: 13.4 us -> 30.6 us
  between operations: 14.4 us -> 0.86 us
    unnamed x3 -> x0, waiting for transfers between devices: 198 us -> none
    all_gather x1 -> x0, waiting for transfers between devices: 145 us -> none  [per_device(): region_pool = lax.all_gather(spectra, 'slab', axis=0, tiled=True)]
    gather x19 -> x0, local copies, waits for them, and re-layouts: 93.4 us -> none  [the longest x16 61.8 us: lag_group(): jnp.take(pool_rows, row_index.reshape(-1), axis=0)]
    pallas_call x0 -> x5, Pallas kernels: none -> 55.5 us  [the longest x1 24.4 us: per_device(): pl.pallas_call(home_kernel, out_shape=(shape((events, neighbour_count * s...]
    concatenate x32 -> x2, local copies, waits for them, and re-layouts: 32.6 us -> 0.83 us  [the longest x1 0.74 us: per_device(): jnp.concatenate([*three_parts(task_arrival), task_mask], axis=1)]
    mul x17 -> x0, other arithmetic: 27 us -> none  [the longest x16 27 us: cross_packed(): imag_product = own_imag * other_imag]
    dot_general x21 -> x0, matrix products: 19.5 us -> none  [the longest x16 16.2 us: soft_lags(): jnp.dot(crossed.reshape(-1, layout[-1]), inverse, preferred_element_type=...]
    another operation x20 -> x6, other arithmetic: 19.1 us -> 0.13 us  [the longest x2 0.09 us: per_device(): jnp.stack([*three_parts(near_arrival), near_masks.T], axis=-1).astype(BF16)]
  transfers between devices with their start and end apart: 6 -> 6, of which waited for: 2 -> 2; matrix products, arithmetic and copies ran while one was open for 8% -> 13% of each run, Pallas kernels for 0% -> 26%
where the time goes in v1:
time: 110 us; the launch traced here: 109 us
  Pallas kernels  55.5 us (50%)
  starting transfers between devices  30.6 us (28%)
  local copies, waits for them, and re-layouts  14.1 us (13%)
  waiting for transfers between devices  5.1 us (5%)
  other arithmetic  2.4 us (2%)
    pallas_call x1, Pallas kernels, per_device(): pl.pallas_call(home_kernel, out_shape=(shape((events, neighbour_count * s...  24.4 us
    pallas_call x1, Pallas kernels, per_device(): pl.pallas_call(task_kernel, out_shape=shape((slab_count, 1, span + events...  20.4 us
    ppermute x4, starting transfers between devices, shifted(): return lax.ppermute(block, axis, route)  12.8 us
    all_to_all x1, starting transfers between devices, per_device(): task_spec = lax.all_to_all(payload, 'slab', 0, 0, tiled=True)  11.3 us
    all_to_all x1, starting transfers between devices, per_device(): remote = lax.all_to_all(results, 'slab', 0, 0, tiled=True)  6.5 us
    unnamed x22, local copies, waits for them, and re-layouts  4.83 us
    pallas_call x1, Pallas kernels, per_device(): pl.pallas_call(by_event_kernel, out_shape=shape((events, COMPONENTS, stat...  4.68 us
    pallas_call x1, Pallas kernels, per_device(): pl.pallas_call(payload_kernel, out_shape=shape((2 * station_count, COMPON...  4.26 us
  transfers between devices with their start and end apart: 6, of which 2 were waited for; matrix products, arithmetic and copies ran while one was open for 13% of the time, Pallas kernels for 26%

profile of v1, /device:TPU:1, one launch (start us, length us, event | category | flops | bytes accessed | tf_op | source)
XLA Modules:
  0.0 108.6 jit_solution(14522498636902980888)
XLA Ops:
  0.6 4.7 %by_event.1.own_ref = bf16[64,3,16,128]{3,2,1,0:T(8,128)(2,1)} custom-call(bf16[3072,128]{1,0:T(8,128)(2,1)} %bitcast.25, bf16[128,128]{1,0:T(8,128)(2,1)} %constant.102.clone.table_ref), custom_call_target="tpu_custom_call" | custom-call | tf_op jit(solution)/shard_map/by_event/pallas_call | solution.py:500
  5.3 4.5 %collective-permute-start = (bf16[64,3,16,128]{3,2,1,0:T(8,128)(2,1)}, bf16[64,3,16,128]{3,2,1,0:T(8,128)(2,1)S(1)}, u32[]{:S(2)}, u32[]{:S(2)}) collective-permute-start(bf16[64,3,16,128]{3,2,1,0:T(8,128)(2,1)} %by_event.1.own_ref), channel_id=1, source_target_pairs={{0,32},{32,64},{64,96},{96,128},{128,160},{160,192},{192,224},{1,3... | collective-permute-start | bytes 2359304 | tf_op jit(solution)/shard_map/ppermute | solution.py:468
  9.8 2.0 %collective-permute-start.1 = (bf16[64,3,16,128]{3,2,1,0:T(8,128)(2,1)}, bf16[64,3,16,128]{3,2,1,0:T(8,128)(2,1)}, u32[]{:S(2)}, u32[]{:S(2)}) collective-permute-start(bf16[64,3,16,128]{3,2,1,0:T(8,128)(2,1)} %by_event.1.own_ref), channel_id=1, source_target_pairs={{32,0},{64,32},{96,64},{128,96},{160,128},{192,160},{224,192},{33,... | collective-permute-start | bytes 2359304 | tf_op jit(solution)/shard_map/ppermute | solution.py:468
  11.8 1.4 %copy.36.ids_ref = s32[64,32]{1,0:T(8,128)} copy(s32[64,32]{0,1:T(8,128)} %param.10) | data formatting | bytes 16384 | tf_op args[1]
  13.2 4.3 %payload.1 = bf16[32,200,128]{2,1,0:T(8,128)(2,1)} custom-call(bf16[3072,128]{1,0:T(8,128)(2,1)} %bitcast.26, bf16[128,128]{1,0:T(8,128)(2,1)} %constant.102.clone.table_ref, s32[64,32]{1,0:T(8,128)} %copy.36.ids_ref), custom_call_target="tpu_custom_call" | custom-call | tf_op jit(solution)/shard_map/payload/pallas_call | solution.py:490
  17.5 0.0 copy-start.4
  17.5 11.3 %all-to-all-start = ((bf16[32,200,128]{2,1,0:T(8,128)(2,1)}), bf16[32,200,128]{2,1,0:T(8,128)(2,1)S(1)}, u32[]{:S(2)}, u32[]{:S(2)}) async-start(bf16[32,200,128]{2,1,0:T(8,128)(2,1)} %payload.1), calls=%async_computation | async-start | bytes 3276800 | tf_op jit(solution)/shard_map/all_to_all | solution.py:499
  28.8 0.0 copy-start.2
  28.8 0.8 constant_dynamic-slice_fusion.5
  29.6 0.0 copy-start.3
  29.6 0.1 pad_maximum_fusion.2
  29.7 0.1 pad_maximum_fusion.4
  29.7 0.0 copy-done.4
  29.7 0.1 multiply_reduce_fusion
  29.9 0.1 slice.32
  29.9 0.8 constant_dynamic-slice_fusion.2
  30.7 0.1 convert_bitcast_fusion
  30.8 0.7 copy.39
  31.6 0.1 slice_add_fusion
  31.7 0.8 copy.40.arrival_ref
  32.4 0.1 slice_bitcast_fusion
  32.5 0.8 copy.41.mask_ref
  33.3 0.0 copy-done.2
  33.4 0.1 copy.38
  33.4 0.7 reshape.165.pool_ids
  34.2 0.7 reshape.166.id_row_ref
  34.9 0.2 fusion.6
  35.0 1.0 dynamic-slice_reduce_fusion
  36.0 0.1 broadcast_in_dim_squeeze.4
  36.1 0.9 fusion.1
  37.0 0.1 div.41
  37.0 0.1 convert_element_type.16
  37.1 0.1 pad_maximum_fusion.1
  37.2 0.7 copy.37
  38.0 0.1 constant_dynamic-slice_fusion.7
  38.0 0.7 tile.17.arrival_ref
  38.7 0.0 copy-done.3
  38.7 0.1 constant_dynamic-slice_fusion.6
  38.8 0.7 tile.37.mask_ref
  39.5 1.0 pad.4.partner_ref
  40.6 0.0 collective-permute-done.low_ref
  40.6 0.0 copy-start.7
  40.6 0.0 collective-permute-done.1.high_ref
  40.6 0.9 copy-done.7
  41.5 24.4 %home.1 = (f32[64,512]{1,0:T(8,128)}, f32[16,64]{1,0:T(8,128)}, f32[16,64]{1,0:T(8,128)}, f32[16,64]{1,0:T(8,128)}) custom-call(s32[1664]{0:T(1024)} %reshape.165.pool_ids, s32[1,1664]{1,0:T(1,128)} %reshape.166.id_row_ref, bf16[64,3,16,128]{3,2,1,0:T(8,128)(2,1)} %copy-done.7, bf16[64,3,16,128]{3,2,1,0:T(8,128)(2,1)} %by_event.1.own_ref, ...), custom_call_target="tpu_custom_call" | custom-call | flops 10000000000 | bytes 10000000 | tf_op jit(solution)/shard_map/home/pallas_call | solution.py:542
  65.9 2.7 %all-to-all-done.spec_ref = bf16[32,200,128]{2,1,0:T(8,128)(2,1)S(1)} async-done(((bf16[32,200,128]{2,1,0:T(8,128)(2,1)}), bf16[32,200,128]{2,1,0:T(8,128)(2,1)S(1)}, u32[]{:S(2)}, u32[]{:S(2)}) %all-to-all-start) | async-done | bytes 1638432 | tf_op jit(solution)/shard_map/all_to_all | solution.py:499
  68.6 0.0 copy-start
  68.6 1.2 %copy-done = bf16[32,200,128]{2,1,0:T(8,128)(2,1)} copy-done((bf16[32,200,128]{2,1,0:T(8,128)(2,1)}, bf16[32,200,128]{2,1,0:T(8,128)(2,1)S(1)}, u32[]{:S(2)}) %copy-start) | copy-done | bytes 1638424
  69.8 0.0 copy-start.9
  69.8 0.0 copy-start.8
  69.8 20.4 %task.1 = f32[32,1,256]{2,1,0:T(1,128)} custom-call(s32[1]{0:T(128)} %bitcast.half_ref, bf16[32,200,128]{2,1,0:T(8,128)(2,1)} %copy-done, bf16[256,32]{1,0:T(8,128)(2,1)} %bitcast.29, f32[16,384]{1,0:T(8,128)} %tile.17.arrival_ref, f32[16,384]{1,0:T(8,128)} %tile.37.mask_ref, bf16[128,384]{1,0:T(8,128)(2,1)} %constant.100.clone.inverse_ref, ...), custom_call_target="tpu_custom_call" | custom-call | flops 10000000000 | bytes 10000000 | tf_op jit(solution)/shard_map/task/pallas_call | solution.py:600
  90.2 6.5 %all-to-all-start.1 = ((f32[32,1,256]{2,1,0:T(1,128)}), f32[32,1,256]{2,1,0:T(1,128)S(1)}, u32[]{:S(2)}, u32[]{:S(2)}) async-start(f32[32,1,256]{2,1,0:T(1,128)} %task.1), calls=%async_computation.1 | async-start | bytes 65536 | tf_op jit(solution)/shard_map/all_to_all | solution.py:627
  96.7 0.0 copy-done.9
  96.7 4.5 %collective-permute-start.2 = (f32[16,64]{1,0:T(8,128)S(1)}, f32[16,64]{1,0:T(8,128)S(1)}, u32[]{:S(2)}, u32[]{:S(2)}) collective-permute-start(f32[16,64]{1,0:T(8,128)S(1)} %copy-done.9), channel_id=1, source_target_pairs={{0,32},{32,64},{64,96},{96,128},{128,160},{160,192},{192,224},{1,3... | collective-permute-start | bytes 12296 | tf_op jit(solution)/shard_map/ppermute | solution.py:468
  101.2 0.0 copy-done.8
  101.2 1.9 %collective-permute-start.3 = (f32[16,64]{1,0:T(8,128)S(1)}, f32[16,64]{1,0:T(8,128)S(1)}, u32[]{:S(2)}, u32[]{:S(2)}) collective-permute-start(f32[16,64]{1,0:T(8,128)S(1)} %copy-done.8), channel_id=1, source_target_pairs={{32,0},{64,32},{96,64},{128,96},{160,128},{192,160},{224,192},{33,... | collective-permute-start | bytes 12296 | tf_op jit(solution)/shard_map/ppermute | solution.py:468
  103.1 0.7 copy.42
  103.8 0.0 collective-permute-done.2.low_ref
  103.8 2.4 %collective-permute-done.3.high_ref = f32[16,64]{1,0:T(8,128)S(1)} collective-permute-done((f32[16,64]{1,0:T(8,128)S(1)}, f32[16,64]{1,0:T(8,128)S(1)}, u32[]{:S(2)}, u32[]{:S(2)}) %collective-permute-start.3) | collective-permute-done | bytes 4128 | tf_op jit(solution)/shard_map/ppermute | solution.py:468
  106.1 0.0 all-to-all-done.1.remote_ref
  106.1 0.0 copy-done.5
  106.1 0.6 copy-done.6
  106.7 0.0 copy-done.1
  106.8 1.8 %final.1 = (f32[64,512]{1,0:T(8,128)}, f32[4,64]{1,0:T(4,128)}) custom-call(f32[32,1,256]{2,1,0:T(1,128)} %copy-done.1, f32[64,512]{1,0:T(8,128)} %get-tuple-element.7.lag_in_ref, f32[16,64]{1,0:T(8,128)} %get-tuple-element.6.home_ref.sums_ref, f32[16,64]{1,0:T(8,128)} %copy-done.5, f32[16,64]{1,0:T(8,128)} %copy-done.6, f32[4,64]{1,0:T(4,128)} %copy-done.3, ...), custom_call_target="tpu_custom_call" | custom-call | tf_op jit(solution)/shard_map/final/pallas_call | solution.py:628
  (17 shorter events, 0.2 us)
Async XLA Ops:
  5.3 35.3 %collective-permute-start = (bf16[64,3,16,128]{3,2,1,0:T(8,128)(2,1)}, bf16[64,3,16,128]{3,2,1,0:T(8,128)(2,1)S(1)}, u32[]{:S(2)}, u32[]{:S(2)}) collective-permute-start(bf16[64,3,16,128]{3,2,1,0:T(8,128)(2,1)} %by_event.1.own_ref), channel_id=1, source_target_pairs={{0,32},{32,64},{64,96},{96,128},{128,160},{160,192},{192,224},{1,3... | collective-permute-start | bytes 2359304 | tf_op jit(solution)/shard_map/ppermute | solution.py:468
  9.8 30.8 %collective-permute-start.1 = (bf16[64,3,16,128]{3,2,1,0:T(8,128)(2,1)}, bf16[64,3,16,128]{3,2,1,0:T(8,128)(2,1)}, u32[]{:S(2)}, u32[]{:S(2)}) collective-permute-start(bf16[64,3,16,128]{3,2,1,0:T(8,128)(2,1)} %by_event.1.own_ref), channel_id=1, source_target_pairs={{32,0},{64,32},{96,64},{128,96},{160,128},{192,160},{224,192},{33,... | collective-permute-start | bytes 2359304 | tf_op jit(solution)/shard_map/ppermute | solution.py:468
  17.5 12.3 %copy-start.4 = (f32[3,16]{1,0:T(4,128)S(1)}, f32[3,16]{1,0:T(4,128)}, u32[]{:S(2)}) copy-start(f32[3,16]{1,0:T(4,128)} %param.13) | copy-start | bytes 580
  17.5 51.1 %all-to-all-start = ((bf16[32,200,128]{2,1,0:T(8,128)(2,1)}), bf16[32,200,128]{2,1,0:T(8,128)(2,1)S(1)}, u32[]{:S(2)}, u32[]{:S(2)}) async-start(bf16[32,200,128]{2,1,0:T(8,128)(2,1)} %payload.1), calls=%async_computation | async-start | bytes 3276800 | tf_op jit(solution)/shard_map/all_to_all | solution.py:499
  28.8 4.5 %copy-start.2 = (s32[64,32]{0,1:T(8,128)S(1)}, s32[64,32]{0,1:T(8,128)}, u32[]{:S(2)}) copy-start(s32[64,32]{0,1:T(8,128)} %param.10) | copy-start | bytes 24580
  29.6 9.1 %copy-start.3 = (f32[4,64]{1,0:T(4,128)}, f32[4,64]{1,0:T(4,128)S(1)}, u32[]{:S(2)}) copy-start(f32[4,64]{1,0:T(4,128)S(1)} %get-tuple-element.19.place_ref) | copy-start | bytes 3076
  40.6 0.9 copy-start.7
  68.6 1.2 %copy-start = (bf16[32,200,128]{2,1,0:T(8,128)(2,1)}, bf16[32,200,128]{2,1,0:T(8,128)(2,1)S(1)}, u32[]{:S(2)}) copy-start(bf16[32,200,128]{2,1,0:T(8,128)(2,1)S(1)} %all-to-all-done.spec_ref) | copy-start | bytes 4915204
  69.8 26.9 %copy-start.9 = (f32[16,64]{1,0:T(8,128)S(1)}, f32[16,64]{1,0:T(8,128)}, u32[]{:S(2)}) copy-start(f32[16,64]{1,0:T(8,128)} %get-tuple-element.8) | copy-start | bytes 12292
  69.8 31.4 %copy-start.8 = (f32[16,64]{1,0:T(8,128)S(1)}, f32[16,64]{1,0:T(8,128)}, u32[]{:S(2)}) copy-start(f32[16,64]{1,0:T(8,128)} %get-tuple-element.9) | copy-start | bytes 12292
  90.2 16.0 %all-to-all-start.1 = ((f32[32,1,256]{2,1,0:T(1,128)}), f32[32,1,256]{2,1,0:T(1,128)S(1)}, u32[]{:S(2)}, u32[]{:S(2)}) async-start(f32[32,1,256]{2,1,0:T(1,128)} %task.1), calls=%async_computation.1 | async-start | bytes 65536 | tf_op jit(solution)/shard_map/all_to_all | solution.py:627
  96.7 7.1 %collective-permute-start.2 = (f32[16,64]{1,0:T(8,128)S(1)}, f32[16,64]{1,0:T(8,128)S(1)}, u32[]{:S(2)}, u32[]{:S(2)}) collective-permute-start(f32[16,64]{1,0:T(8,128)S(1)} %copy-done.9), channel_id=1, source_target_pairs={{0,32},{32,64},{64,96},{96,128},{128,160},{160,192},{192,224},{1,3... | collective-permute-start | bytes 12296 | tf_op jit(solution)/shard_map/ppermute | solution.py:468
  101.2 5.0 %collective-permute-start.3 = (f32[16,64]{1,0:T(8,128)S(1)}, f32[16,64]{1,0:T(8,128)S(1)}, u32[]{:S(2)}, u32[]{:S(2)}) collective-permute-start(f32[16,64]{1,0:T(8,128)S(1)} %copy-done.8), channel_id=1, source_target_pairs={{32,0},{64,32},{96,64},{128,96},{160,128},{192,160},{224,192},{33,... | collective-permute-start | bytes 12296 | tf_op jit(solution)/shard_map/ppermute | solution.py:468
  103.8 2.4 %copy-start.5 = (f32[16,64]{1,0:T(8,128)}, f32[16,64]{1,0:T(8,128)S(1)}, u32[]{:S(2)}) copy-start(f32[16,64]{1,0:T(8,128)S(1)} %collective-permute-done.2.low_ref) | copy-start | bytes 12292
  106.1 0.6 copy-start.6
  106.1 0.6 copy-start.1

commit v2 on v1

v2 whole, which is shorter than its diff:
```python
import functools

import jax
import jax.numpy as jnp
import ml_dtypes
import numpy as np
from jax import lax
from jax.experimental import pallas as pl
from jax.experimental.pallas import tpu as pltpu
from jax.sharding import PartitionSpec as P

K_LOCAL = 24
K_REGION = 6
K_CROSS = 2
K_HOME = K_LOCAL + K_CROSS
COMPONENTS = 3
BATCH = 4
LANES = 128

SHARPNESS = 0.1
WAVE_SPEED = 0.6
EXPONENT_SCALE = SHARPNESS * 1.4426950408889634

F32 = jnp.float32
BF16 = jnp.bfloat16
BY_LAST = (((1,), (1,)), ((), ()))


def forward_table(samples):
    half_length = samples // 2
    sample_ids = np.arange(samples)[:, None]
    cos_bins = np.arange(half_length + 1)[None, :]
    sin_bins = np.arange(1, half_length)[None, :]
    cos_angle = 2.0 * np.pi / samples * (sample_ids * cos_bins % samples)
    sin_angle = 2.0 * np.pi / samples * (sample_ids * sin_bins % samples)
    table = np.concatenate([np.cos(cos_angle), -np.sin(sin_angle)], axis=1)
    return table.astype(np.float32).astype(ml_dtypes.bfloat16)


def inverse_table(samples):
    half_length = samples // 2
    cos_bins = np.arange(half_length + 1)[:, None]
    sin_bins = np.arange(1, half_length)[:, None]
    lag_ids = np.arange(samples)[None, :]
    factors = np.where((cos_bins == 0) | (cos_bins == half_length), 1.0, 2.0) / samples
    cos_angle = 2.0 * np.pi / samples * (cos_bins * lag_ids % samples)
    sin_angle = 2.0 * np.pi / samples * (sin_bins * lag_ids % samples)
    table = np.concatenate(
        [factors * np.cos(cos_angle), -(2.0 / samples) * np.sin(sin_angle)], axis=0
    )
    return table.astype(np.float32).astype(ml_dtypes.bfloat16)


def inverse_rows(samples):
    table = inverse_table(samples)
    real, imag = table[: samples // 2], table[samples // 2 :]
    return np.concatenate([real, real, imag, imag, table], axis=0)


def lag_values(samples):
    lag_ids = np.arange(samples)
    values = np.where(lag_ids < samples // 2, lag_ids, lag_ids - samples)
    return np.broadcast_to(values[:, None], (samples, LANES)).astype(np.float32)


def arrange(first, second):
    half = first.shape[-1] // 2
    lane = lax.broadcasted_iota(jnp.int32, first.shape, first.ndim - 1)
    real = jnp.where(lane < half, first, pltpu.roll(second, half, second.ndim - 1))
    imag = jnp.where(lane < half, pltpu.roll(first, half, first.ndim - 1), second)
    return real, imag


def swapped(spec):
    return pltpu.roll(spec, spec.shape[-1] // 2, spec.ndim - 1)


def multipliers(real, imag, packed):
    half = packed.shape[-1] // 2
    lane = lax.broadcasted_iota(jnp.int32, packed.shape, packed.ndim - 1)
    edge = (lane == 0) | (lane == half)
    turned = swapped(packed)
    packed_real = jnp.where(lane <= half, packed, turned)
    packed_imag = jnp.where(edge, 0.0, jnp.where(lane < half, turned, -packed))
    return real, jnp.where(edge, imag, real), jnp.where(edge, 0.0, imag), packed_real, packed_imag


def cross(own, partner):
    real, real_edge, imag, packed_real, packed_imag = own
    other_real, other_imag, other, other_swapped = partner
    return (
        real * other_real + imag * other_imag,
        real_edge * other_imag - imag * other_real,
        packed_real * other + packed_imag * other_swapped,
    )


def soft_lags(corr, values):
    corr = corr.T
    top = jnp.max(corr, axis=0, keepdims=True)
    weights = jnp.exp2((corr - top) * EXPONENT_SCALE)
    total = jnp.sum(weights, axis=0, keepdims=True)
    moment = jnp.sum(weights * values, axis=0, keepdims=True)
    return moment / total


def all_soft_lags(crossed_ref, inverse_ref, values_ref, block):
    inverse, values = inverse_ref[...], values_ref[...]
    lags = []
    for start in range(0, crossed_ref.shape[0], block):
        corr = jnp.dot(
            crossed_ref[start : start + block, :], inverse, preferred_element_type=F32
        )
        for k in range(0, block, LANES):
            lags.append(soft_lags(corr[k : k + LANES], values))
    return jnp.concatenate(lags, axis=1)


def two_parts(x):
    high = x.astype(BF16)
    return high, (x - high.astype(F32)).astype(BF16)


def transform(wave_ref, table_ref, scr):
    block = 384

    def step(k, carry):
        rows = pl.ds(pl.multiple_of(k * block, block), block)
        spec = jnp.dot(wave_ref[rows, :], table_ref[...], preferred_element_type=F32)
        scr[rows, :] = spec.astype(BF16).astype(F32)
        return carry

    lax.fori_loop(0, wave_ref.shape[0] // block, step, 0, unroll=True)


def near_columns(ref, window, sem, region):
    slab = lax.axis_index("slab")
    start = region * (lax.axis_size("slab") * LANES // 2) + slab // 2 * LANES
    copy = pltpu.make_async_copy(
        ref.at[:, pl.ds(pl.multiple_of(start, LANES), LANES)], window, sem
    )
    copy.start()
    return copy


def own_columns(window):
    odd = lax.axis_index("slab") % 2 == 1
    values = window[...].astype(F32)
    half = values.shape[1] // 2
    return jnp.where(odd, pltpu.roll(values, half, 1), values)[:, :half]


def travel(places, station_columns):
    offsets = [places[c : c + 1, :] - station_columns[:, c : c + 1] for c in range(3)]
    return offsets, jnp.sqrt(sum(offset * offset for offset in offsets))


def three_parts(x):
    high = x.astype(BF16)
    rest = x - high.astype(F32)
    middle = rest.astype(BF16)
    return high, middle, (rest - middle.astype(F32)).astype(BF16)


def put_crossed(crossed, rows, own, partner):
    for k, values in enumerate(cross(own, partner)):
        crossed[rows, k * LANES : (k + 1) * LANES] = values.astype(BF16)


def look_up(arrival, mask, hits):
    stations = arrival.shape[0]
    rows = jnp.concatenate([p.astype(F32) for p in three_parts(arrival)] + [mask], axis=0)
    rows = jnp.dot(rows.astype(BF16), hits, preferred_element_type=F32)
    high, middle, low, found = (rows[k * stations : (k + 1) * stations] for k in range(4))
    return high + middle + low, found


def sum_by_name(residual, hits):
    stations = residual.shape[0]
    parts = jnp.concatenate(two_parts(residual), axis=0)
    sums = lax.dot_general(parts, hits, BY_LAST, preferred_element_type=F32)
    return sums[:stations] + sums[stations:]


def by_pair(lags, columns):
    turned = lags.T
    stations = turned.shape[0] // columns
    return jnp.concatenate(
        [turned[n * stations : (n + 1) * stations] for n in range(columns)], axis=1
    )


def payload_kernel(wave_ref, table_ref, ids_ref, kept_ref, sent_ref, by_event_ref, scr):
    stations = sent_ref.shape[0]
    events = ids_ref.shape[1]
    part = events // 2
    channels = stations * COMPONENTS
    core = lax.axis_index("region") % 2
    transform(wave_ref, table_ref, scr)
    ids = ids_ref[K_LOCAL : K_LOCAL + K_REGION, :]
    tail = sent_ref.shape[1] - COMPONENTS * part
    for out, base, half in ((kept_ref, core * stations, core), (sent_ref, 0, 1 - core)):
        mine = jnp.where(half == 1, ids[:, part:], ids[:, :part])
        row = jnp.concatenate([mine[n : n + 1] for n in range(K_REGION)], axis=1)
        row = jnp.concatenate([row, jnp.zeros((1, 2 * LANES - row.shape[1]), jnp.int32)], axis=1)
        source, event = row // events % (2 * stations), row % events
        rows = jnp.concatenate(
            [source[:, :LANES], source[:, LANES:], event[:, :LANES], event[:, LANES:]]
            + [jnp.zeros((tail - 4, LANES), jnp.int32)],
            axis=0,
        )
        rows = rows.astype(F32).astype(BF16)
        for s in range(stations):
            first, second, third = (
                scr[pl.ds(half * (part * channels) + COMPONENTS * s + c, part, stride=channels), :]
                for c in range(COMPONENTS)
            )
            for k, values in enumerate((*arrange(first, second), third)):
                out[base + s, k * part : (k + 1) * part, :] = values.astype(BF16)
            out[base + s, COMPONENTS * part :, :] = rows

    def one_event(event, carry):
        first, second, third = (
            scr[pl.ds(event * channels + c, stations, stride=COMPONENTS), :]
            for c in range(COMPONENTS)
        )
        for k, values in enumerate((*arrange(first, second), third, swapped(third))):
            by_event_ref[event, k] = values.astype(BF16)
        return carry

    lax.fori_loop(0, events, one_event, 0, unroll=8)


def home_kernel(
    ids,
    id_ref,
    stations_ref,
    inverse_ref,
    values_ref,
    core_ref,
    own_ref,
    x_ref,
    locations_ref,
    masks_ref,
    order_ref,
    lag_ref,
    sums_ref,
    to_core_ref,
    to_x_ref,
    done_ref,
    raw,
    pool,
    crossed,
    hits,
    place_windows,
    mask_windows,
    sems,
):
    events, _, stations, _ = own_ref.shape
    width = K_HOME * stations
    batches = events // BATCH
    region = lax.axis_index("region")
    last = lax.axis_size("region") - 1
    copies = [
        pltpu.make_async_copy(ref, raw.at[pl.ds(k * events, events)], sems.at[k])
        for k, ref in enumerate((core_ref, own_ref, x_ref))
    ]
    for copy in copies:
        copy.start()
    odd = region % 2
    near = (region + 1 - 2 * odd, region, jnp.clip(region - 1 + 2 * odd, 0, last))
    for k, where in enumerate(near):
        copies.append(near_columns(locations_ref, place_windows.at[k], sems.at[3 + k], where))
        copies.append(near_columns(masks_ref, mask_windows.at[k], sems.at[6 + k], where))
    blocks = [events] * K_LOCAL + [
        jnp.where((odd == 1) | (region == 0), 0, 2 * events),
        jnp.where((odd == 0) | (region == last), 0, 2 * events),
    ]
    columns = [*range(K_LOCAL), *range(K_LOCAL + K_REGION, K_LOCAL + K_REGION + K_CROSS)]
    named = lax.broadcasted_iota(jnp.int32, (3 * events, events), 0)
    for n in range(0, K_HOME, 2):
        pair = [
            jnp.where(
                id_ref[columns[m] : columns[m] + 1, :] % events + blocks[m] == named, 1.0, 0.0
            )
            for m in (n, n + 1)
        ]
        hits[:, n * events : (n + 2) * events] = jnp.concatenate(pair, axis=1).astype(BF16)
    done_ref[...] = jnp.zeros(done_ref.shape, done_ref.dtype)
    for copy in copies:
        copy.wait()

    def widen(event, carry):
        pool[event] = raw[event].astype(F32)
        return carry

    lax.fori_loop(0, 3 * events, widen, 0, unroll=8)

    def cross_batch(batch, rows_ref):
        for b in range(BATCH):
            event = batch * BATCH + b
            own = multipliers(*(pool[events + event, k] for k in range(COMPONENTS)))
            for n in range(K_HOME):
                j = lax.bitwise_and(ids[columns[n], event], events - 1) + blocks[n]
                partner = [pool[j, k] for k in range(COMPONENTS + 1)]
                start = b * width + n * stations
                put_crossed(rows_ref, slice(start, start + stations), own, partner)

    def finish_batch(batch, rows_ref):
        lags = all_soft_lags(rows_ref, inverse_ref, values_ref, BATCH * width)
        for b in range(BATCH):
            lag_ref[pl.ds(batch * BATCH + b, 1), :] = lags[:, b * width : (b + 1) * width]

    def two_batches(step, carry):
        cross_batch(2 * step + 1, crossed.at[1])
        finish_batch(2 * step, crossed.at[0])
        cross_batch(jnp.minimum(2 * step + 2, batches - 1), crossed.at[0])
        finish_batch(2 * step + 1, crossed.at[1])
        return carry

    cross_batch(0, crossed.at[0])
    lax.fori_loop(0, batches // 2, two_batches, 0)

    station_columns = stations_ref[...].T
    arrivals, masks = [], []
    for k in range(3):
        places = own_columns(place_windows.at[k])
        masks.append(own_columns(mask_windows.at[k]))
        _, distance = travel(places, station_columns)
        arrivals.append(places[3:4, :] + distance / WAVE_SPEED)
    near_arrivals, found = look_up(
        jnp.concatenate(arrivals, axis=1), jnp.concatenate(masks, axis=1), hits[...]
    )
    residual = (
        jnp.tile(masks[1], (1, K_HOME))
        * found
        * (by_pair(lag_ref[...], K_HOME) - (near_arrivals - jnp.tile(arrivals[1], (1, K_HOME))))
        * (1.0 / ((K_HOME + K_REGION) * stations))
    )
    own_sums = sum(residual[:, n * events : (n + 1) * events] for n in range(K_HOME))
    sums = sum_by_name(residual, hits[...])
    to_core_ref[...] = sums[:, :events]
    sums_ref[...] = own_sums - sums[:, events : 2 * events]
    to_x_ref[...] = sums[:, 2 * events :]


def task_kernel(
    stations_ref,
    mine_ref,
    other_ref,
    inverse_ref,
    values_ref,
    locations_ref,
    masks_ref,
    out_ref,
    table,
    fetched_even,
    fetched_odd,
    crossed_even,
    crossed_odd,
    id_rows,
    residuals,
    own_terms,
    place_window,
    mask_window,
    ids,
    sems,
):
    sources, payload, _ = mine_ref.shape
    stations = sources // 2
    part = payload // COMPONENTS // 8 * 8
    events = 2 * part
    span = K_REGION * part
    width = 2 * span
    region_events = sources * events
    region, slab = lax.axis_index("region"), lax.axis_index("slab")
    core = region % 2
    task_region = region - core + slab // stations
    station = slab % stations
    columns = pl.ds(pl.multiple_of(task_region * region_events, region_events), region_events)
    copies = [
        pltpu.make_async_copy(locations_ref.at[:, columns], place_window, sems.at[0]),
        pltpu.make_async_copy(masks_ref.at[:, columns], mask_window, sems.at[1]),
    ]
    for copy in copies:
        copy.start()

    def read_ids(source, carry):
        tail = mine_ref[source, COMPONENTS * part :, :].astype(F32)
        rows = ((tail[:2] * events + tail[2:4]) * 8).astype(jnp.int32)
        id_rows[pl.ds(2 * source, 1), :] = rows[:1]
        id_rows[pl.ds(2 * source + 1, 1), :] = rows[1:]
        return carry

    lax.fori_loop(0, sources, read_ids, 0, unroll=8)
    id_copy = pltpu.make_async_copy(id_rows, ids, sems.at[2])
    id_copy.start()

    def fill(source, carry):
        for ref, half in ((mine_ref, core), (other_ref, 1 - core)):
            rows = [
                ref[source, k * part : (k + 1) * part, :].astype(F32) for k in range(COMPONENTS)
            ]
            rows.append(swapped(rows[-1]))
            base = (source * events + half * part) * 8
            for k, values_k in enumerate(rows):
                table[pl.ds(base + k, part, stride=8), :] = values_k
                table[pl.ds(base + 4 + k, part, stride=8), :] = values_k
        return carry

    lax.fori_loop(0, sources, fill, 0, unroll=4)
    for copy in copies:
        copy.wait()
    offsets = [place_window[c : c + 1, :] - stations_ref[c, station] for c in range(3)]
    arrival = place_window[3:4, :] + (
        jnp.sqrt(sum(offset * offset for offset in offsets)) / WAVE_SPEED
    )
    mask = mask_window[pl.ds(station, 1), :].astype(F32)

    def as_rows(row):
        return jnp.concatenate(
            [row[:, t * LANES : (t + 1) * LANES] for t in range(region_events // LANES)], axis=0
        )

    tables = jnp.concatenate(
        [part_of.astype(F32) for part_of in three_parts(as_rows(arrival))] + [as_rows(mask)], axis=0
    ).astype(BF16)
    half_rows = tables.shape[0] // 4
    lane = lax.broadcasted_iota(jnp.int32, (LANES, width), 1)
    event_rows = lax.broadcasted_iota(jnp.int32, (LANES, width), 0)
    own_hits = event_rows == lane // span * events + core * part + lane % part
    own_hits = jnp.where(own_hits, 1.0, 0.0).astype(BF16)
    own = jnp.dot(tables, own_hits, preferred_element_type=F32)
    own_terms[:half_rows] = own[:half_rows] + own[half_rows : 2 * half_rows] + own[
        2 * half_rows : 3 * half_rows
    ]
    own_terms[half_rows:] = own[3 * half_rows :]
    id_copy.wait()

    upper = lax.broadcasted_iota(jnp.int32, (8, LANES), 0) < 4
    source_rows = lax.broadcasted_iota(jnp.int32, (half_rows, width), 0)
    out_lane = lax.broadcasted_iota(jnp.int32, (1, LANES), 1)

    def fetch(step, into):
        for q in range(0, width, 2):
            row, column = q // span * 2 + q % span // LANES, q % span % LANES
            first = ids[step * 4 + row, column]
            second = ids[step * 4 + row, column + 1]
            first = table[pl.ds(pl.multiple_of(first, 8), 8), :]
            second = table[pl.ds(pl.multiple_of(second, 8), 8), :]
            into[q * 4 : q * 4 + 8, :] = jnp.where(upper, first, second)

    def cross_two(step, source, into):
        for u in range(2):
            own = multipliers(
                *(
                    mine_ref[2 * step + u, k * part : (k + 1) * part, :].astype(F32)
                    for k in range(COMPONENTS)
                )
            )
            for n in range(K_REGION):
                start = u * span + n * part
                partner = [
                    source[pl.ds(start * 4 + k, part, stride=4), :]
                    for k in range(COMPONENTS + 1)
                ]
                put_crossed(into, slice(start, start + part), own, partner)

    def finish(step, rows_ref, sums):
        lag = all_soft_lags(rows_ref, inverse_ref, values_ref, LANES)
        for u in range(2):
            rest = lag[:, u * span + LANES : (u + 1) * span]
            rest = jnp.concatenate([rest, jnp.zeros((1, LANES - rest.shape[1]), F32)], axis=1)
            out_ref[2 * step + u] = jnp.concatenate(
                [lag[:, u * span : u * span + LANES], rest], axis=0
            )
        id_row = jnp.concatenate(
            [
                piece
                for u in range(2)
                for piece in (
                    id_rows[pl.ds(4 * step + 2 * u, 1), :],
                    id_rows[pl.ds(4 * step + 2 * u + 1, 1), :][:, : span - LANES],
                )
            ],
            axis=1,
        )
        id_row = id_row // 8
        from_source = source_rows == id_row // LANES
        from_event = jnp.where(event_rows == id_row % LANES, 1.0, 0.0).astype(BF16)
        looked_up = jnp.dot(tables, from_event, preferred_element_type=F32)
        arrival = looked_up[:half_rows] + looked_up[half_rows : 2 * half_rows]
        arrival = arrival + looked_up[2 * half_rows : 3 * half_rows]
        arrival = jnp.sum(jnp.where(from_source, arrival, 0.0), axis=0, keepdims=True)
        mask = jnp.where(from_source, looked_up[3 * half_rows :], 0.0)
        mask = jnp.sum(mask, axis=0, keepdims=True)
        residual = (
            own_terms[pl.ds(half_rows + step, 1), :]
            * mask
            * (lag - (arrival - own_terms[pl.ds(step, 1), :]))
            * (1.0 / ((K_LOCAL + K_REGION + K_CROSS) * stations))
        )
        residuals[pl.ds(step, 1), :] = residual
        terms = jnp.concatenate(two_parts(jnp.where(from_source, residual, 0.0)), axis=0)
        return sums + lax.dot_general(terms, from_event, BY_LAST, preferred_element_type=F32)

    steps = sources // 2

    def two_steps(pair, sums):
        first = 2 * pair
        fetch(jnp.minimum(first + 2, steps - 1), fetched_even)
        cross_two(first + 1, fetched_odd, crossed_odd)
        sums = finish(first, crossed_even, sums)
        fetch(jnp.minimum(first + 3, steps - 1), fetched_odd)
        cross_two(jnp.minimum(first + 2, steps - 1), fetched_even, crossed_even)
        return finish(first + 1, crossed_odd, sums)

    fetch(0, fetched_even)
    cross_two(0, fetched_even, crossed_even)
    fetch(1, fetched_odd)
    sums = lax.fori_loop(0, steps // 2, two_steps, jnp.zeros((2 * half_rows, LANES), F32))
    terms = jnp.concatenate(two_parts(residuals[...]), axis=0)
    sums = lax.dot_general(terms, own_hits, BY_LAST, preferred_element_type=F32) - sums
    sums = sums[:half_rows] + sums[half_rows:]
    for t in range(half_rows):
        for u in range(2):
            row = sums[t : t + 1, :]
            row = pltpu.roll(row, LANES // 2, 1) if u == 0 else row
            lags = out_ref[2 * t + u]
            out_ref[2 * t + u] = jnp.concatenate(
                [lags[:1], jnp.where(out_lane < span - LANES, lags[1:], row)], axis=0
            )


def gather_kernel(home_lag_ref, sums_ref, core_ref, x_ref, order_ref, lag_ref, out_ref):
    stations = sums_ref.shape[0]
    local = K_LOCAL * stations
    remote = K_REGION * stations
    home = home_lag_ref[...]
    gap = jnp.zeros((home.shape[0], remote), F32)
    lag_ref[...] = jnp.concatenate([home[:, :local], gap, home[:, local:]], axis=1)
    out_ref[...] = sums_ref[...] - core_ref[...] - x_ref[...]


def final_kernel(
    kept_ref,
    got_ref,
    home_lag_ref,
    sums_ref,
    stations_ref,
    locations_ref,
    lag_ref,
    grad_ref,
    place_window,
    lag_window,
    sems,
):
    events = grad_ref.shape[1]
    stations = sums_ref.shape[0]
    part = events // 2
    span = K_REGION * part
    core = lax.axis_index("region") % 2
    copy = near_columns(locations_ref, place_window, sems.at[0], lax.axis_index("region"))
    columns = pl.ds(K_LOCAL * stations, LANES)
    lags = pltpu.make_async_copy(home_lag_ref.at[:, columns], lag_window, sems.at[1])
    lags.start()
    sums = sums_ref[...]
    block = pl.ds(pl.multiple_of(core * stations, stations), stations)
    kept, got = kept_ref[block], got_ref[block]
    rows = []
    for h in range(2):
        values = jnp.where(core == h, kept, got)
        sums = sums + values[:, 1, span - LANES :]
        turned = jnp.concatenate([values[:, 0, :], values[:, 1, : span - LANES]], axis=1).T
        rows.append(
            jnp.concatenate([turned[n * part : (n + 1) * part] for n in range(K_REGION)], axis=1)
        )
    rows = jnp.concatenate(rows, axis=0)
    copy.wait()
    lags.wait()
    lag_window[:, : rows.shape[1]] = rows
    lags = pltpu.make_async_copy(lag_window, lag_ref.at[:, columns], sems.at[1])
    lags.start()
    offsets, distance = travel(own_columns(place_window), stations_ref[...].T)
    for c in range(3):
        direction = offsets[c] / (WAVE_SPEED * distance)
        grad_ref[c : c + 1, :] = jnp.sum(direction * sums, axis=0, keepdims=True)
    grad_ref[3:4, :] = jnp.sum(sums, axis=0, keepdims=True)
    lags.wait()


def params(mebibytes):
    return pltpu.CompilerParams(vmem_limit_bytes=mebibytes * 1024 * 1024)


def vmem(count):
    return [pl.BlockSpec(memory_space=pltpu.VMEM)] * count


def smem(count):
    return [pl.BlockSpec(memory_space=pltpu.SMEM)] * count


def anywhere(count):
    return [pl.BlockSpec(memory_space=pl.ANY)] * count


def shape(dims, dtype=F32):
    return jax.ShapeDtypeStruct(dims, dtype)


def other_core(block):
    count = lax.axis_size("region")
    return lax.ppermute(block, "region", [(i, i + 1 - 2 * (i % 2)) for i in range(count)])


def other_chip(block):
    odd = range(1, lax.axis_size("region") - 1, 2)
    return lax.ppermute(block, "region", [p for i in odd for p in ((i, i + 1), (i + 1, i))])


def per_device(waveforms, neighbours, masks, locations, stations):
    events, channels, samples = waveforms.shape
    neighbour_count = neighbours.shape[1]
    station_count = stations.shape[1]
    slab_count = lax.axis_size("slab")
    region_events = slab_count * events
    core = lax.axis_index("region") % 2
    part = events // 2
    span = K_REGION * part
    inverse = jnp.asarray(inverse_rows(samples))
    values = jnp.asarray(lag_values(samples))
    wave_rows = waveforms.reshape(-1, samples)
    table = jnp.asarray(forward_table(samples))
    id_columns = neighbours.T
    by_event_shape = (events, COMPONENTS + 1, station_count, samples)
    payload_rows = COMPONENTS * part + 8

    kept, sent, by_event = pl.pallas_call(
        payload_kernel,
        out_shape=(
            shape((slab_count, payload_rows, samples), BF16),
            shape((station_count, payload_rows, samples), BF16),
            shape(by_event_shape, BF16),
        ),
        in_specs=vmem(3),
        out_specs=vmem(3),
        scratch_shapes=[pltpu.VMEM((events * channels, samples), F32)],
        compiler_params=params(16),
        name="payload",
    )(wave_rows, table, id_columns)
    payload = lax.dynamic_update_slice_in_dim(
        kept, other_core(sent), (1 - core) * station_count, 0
    )
    mine = lax.all_to_all(payload, "slab", 0, 0, tiled=True)

    core_spec = other_core(by_event)
    x_spec = other_chip(by_event)

    width = K_HOME * station_count
    lag_home, sums, to_core, to_x, done = pl.pallas_call(
        home_kernel,
        out_shape=(
            shape((events, width)),
            shape((station_count, events)),
            shape((station_count, events)),
            shape((station_count, events)),
            shape((1, 1, LANES), BF16),
        ),
        in_specs=smem(1) + vmem(4) + anywhere(6),
        out_specs=vmem(5),
        scratch_shapes=[
            pltpu.VMEM((3 * events, *by_event_shape[1:]), BF16),
            pltpu.VMEM((3 * events, *by_event_shape[1:]), F32),
            pltpu.VMEM((2, BATCH * width, COMPONENTS * samples), BF16),
            pltpu.VMEM((3 * events, K_HOME * events), BF16),
            pltpu.VMEM((3, 4, LANES), F32),
            pltpu.VMEM((3, station_count, LANES), jnp.int32),
            pltpu.SemaphoreType.DMA((9,)),
        ],
        compiler_params=params(26),
        cost_estimate=pl.CostEstimate(flops=10**10, bytes_accessed=10**7, transcendentals=10**7),
        name="home",
    )(
        id_columns,
        id_columns,
        stations,
        inverse,
        values,
        core_spec,
        by_event,
        x_spec,
        locations,
        masks,
        payload,
    )
    from_core = other_core(to_core)
    from_x = other_chip(to_x)
    mine = lax.dynamic_update_slice(mine, done, (0, payload_rows - 1, 0))
    other = other_core(mine)

    results = pl.pallas_call(
        task_kernel,
        out_shape=shape((slab_count, 2, LANES)),
        in_specs=smem(1) + vmem(4) + anywhere(2),
        out_specs=vmem(1)[0],
        scratch_shapes=[
            pltpu.VMEM((region_events * 8, LANES), F32),
            pltpu.VMEM((2 * span * 4, LANES), F32),
            pltpu.VMEM((2 * span * 4, LANES), F32),
            pltpu.VMEM((2 * span, COMPONENTS * samples), BF16),
            pltpu.VMEM((2 * span, COMPONENTS * samples), BF16),
            pltpu.VMEM((2 * slab_count, LANES), jnp.int32),
            pltpu.VMEM((slab_count // 2, 2 * span), F32),
            pltpu.VMEM((slab_count, 2 * span), F32),
            pltpu.VMEM((4, region_events), F32),
            pltpu.VMEM((station_count, region_events), jnp.int32),
            pltpu.SMEM((2 * slab_count, LANES), jnp.int32),
            pltpu.SemaphoreType.DMA((3,)),
        ],
        compiler_params=params(26),
        cost_estimate=pl.CostEstimate(flops=10**10, bytes_accessed=10**7, transcendentals=10**7),
        name="task",
    )(stations, mine, other, inverse, values, locations, masks)
    back = lax.all_to_all(results, "slab", 0, 0, tiled=True)
    lag_home, sums = pl.pallas_call(
        gather_kernel,
        out_shape=(
            shape((events, neighbour_count * station_count)),
            shape((station_count, events)),
        ),
        in_specs=vmem(4) + anywhere(1),
        out_specs=vmem(2),
        compiler_params=params(8),
        cost_estimate=pl.CostEstimate(flops=10**9, bytes_accessed=10**7, transcendentals=0),
        name="gather",
    )(lag_home, sums, from_core, from_x, results)
    return pl.pallas_call(
        final_kernel,
        out_shape=(
            shape((events, neighbour_count * station_count)),
            shape((4, events)),
        ),
        in_specs=vmem(2) + anywhere(1) + vmem(2) + anywhere(1),
        out_specs=(anywhere(1)[0], vmem(1)[0]),
        scratch_shapes=[
            pltpu.VMEM((4, LANES), F32),
            pltpu.VMEM((events, LANES), F32),
            pltpu.SemaphoreType.DMA((2,)),
        ],
        input_output_aliases={2: 0},
        compiler_params=params(8),
        name="final",
    )(back, other_core(back), lag_home, sums, stations, locations)


def solution(mesh):
    in_specs = (P(("region", "slab"), None, None), P(("region", "slab"), None), P(), P(), P())
    out_specs = (P(("region", "slab"), None), P(None, ("region", "slab")))
    return jax.shard_map(
        per_device, mesh=mesh, in_specs=in_specs, out_specs=out_specs, check_vma=False
    )
```

time: 110 us -> 81.6 us (0.74)
  Pallas kernels: 55.5 us -> 35.7 us
  local copies, waits for them, and re-layouts: 14.1 us -> 3.47 us
  waiting for transfers between devices: 5.1 us -> 13.4 us
  starting transfers between devices: 30.6 us -> 27.8 us
  other arithmetic: 2.4 us -> 0 us
    pallas_call x4, Pallas kernels: 53.7 us -> 33.7 us  [the longest x1 17.5 us: per_device(): pl.pallas_call(home_kernel, out_shape=(shape((events, width)), shape((sta...]
    all_to_all x2, waiting for transfers between devices: 2.74 us -> 8.46 us  [the longest x1 4.96 us: per_device(): back = lax.all_to_all(results, 'slab', 0, 0, tiled=True)]
    another operation x10 -> x0, local copies, waits for them, and re-layouts: 3.78 us -> none  [the longest x4 1.41 us: per_pair(): return jnp.tile(rows, (1, K_REGION)).reshape(slab_count // 2, 2 * span)]
    ppermute x4 -> x7, waiting for transfers between devices: 2.37 us -> 4.91 us  [the longest x5 2.53 us: other_core(): lax.ppermute(block, 'region', [(i, i + 1 - 2 * (i % 2)) for i in range(co...]
    ppermute x4 -> x7, starting transfers between devices: 12.8 us -> 10.6 us  [the longest x5 5.39 us: other_core(): lax.ppermute(block, 'region', [(i, i + 1 - 2 * (i % 2)) for i in range(co...]
    unnamed x22 -> x18, local copies, waits for them, and re-layouts: 4.83 us -> 2.63 us
    dynamic_slice x5 -> x0, local copies, waits for them, and re-layouts: 1.93 us -> none  [the longest x1 0.8 us: per_device(): lax.dynamic_slice_in_dim(masks, start, events, 1)]
    reshape x2 -> x0, local copies, waits for them, and re-layouts: 1.4 us -> none  [the longest x1 0.73 us: per_device(): pool_ids.reshape(-1)]
  transfers between devices with their start and end apart: 6 -> 9, of which waited for: 2 -> 5; matrix products, arithmetic and copies ran while one was open for 13% -> 1% of each run, Pallas kernels for 26% -> 23%
where the time goes in v2:
time: 81.6 us; the launch traced here: 81.1 us
  Pallas kernels  35.7 us (44%)
  starting transfers between devices  27.8 us (34%)
  waiting for transfers between devices  13.4 us (16%)
  local copies, waits for them, and re-layouts  3.47 us (4%)
    pallas_call x1, Pallas kernels, per_device(): pl.pallas_call(home_kernel, out_shape=(shape((events, width)), shape((sta...  17.5 us
    pallas_call x1, Pallas kernels, per_device(): pl.pallas_call(task_kernel, out_shape=shape((slab_count, 2, LANES)), in_s...  12.9 us
    all_to_all x1, starting transfers between devices, per_device(): mine = lax.all_to_all(payload, 'slab', 0, 0, tiled=True)  11.2 us
    all_to_all x1, starting transfers between devices, per_device(): back = lax.all_to_all(results, 'slab', 0, 0, tiled=True)  6.01 us
    ppermute x5, starting transfers between devices, other_core(): lax.ppermute(block, 'region', [(i, i + 1 - 2 * (i % 2)) for i in range(co...  5.39 us
    ppermute x2, starting transfers between devices, other_chip(): lax.ppermute(block, 'region', [p for i in odd for p in ((i, i + 1), (i +...  5.19 us
    all_to_all x1, waiting for transfers between devices, per_device(): back = lax.all_to_all(results, 'slab', 0, 0, tiled=True)  4.96 us
    all_to_all x1, waiting for transfers between devices, per_device(): mine = lax.all_to_all(payload, 'slab', 0, 0, tiled=True)  3.5 us
  transfers between devices with their start and end apart: 9, of which 5 were waited for; matrix products, arithmetic and copies ran while one was open for 1% of the time, Pallas kernels for 23%

profile of v2, /device:TPU:1, one launch (start us, length us, event | category | flops | bytes accessed | tf_op | source)
XLA Modules:
  0.0 81.1 jit_solution(3746619895143202951)
XLA Ops:
  0.6 0.0 copy-start
  0.6 1.1 %copy-done = bf16[64,48,128]{2,1,0:T(8,128)(2,1)S(1)} copy-done((bf16[64,48,128]{2,1,0:T(8,128)(2,1)S(1)}, bf16[64,48,128]{2,1,0:T(8,128)(2,1)}, u32[]{:S(2)}) %copy-start) | copy-done | bytes 786456
  1.8 0.0 copy-start.2
  1.8 0.8 copy-done.2
  2.5 0.0 copy-start.3
  2.5 0.7 copy-done.3
  3.2 2.6 %payload.1 = (bf16[32,104,128]{2,1,0:T(8,128)(2,1)}, bf16[16,104,128]{2,1,0:T(8,128)(2,1)S(1)}, bf16[64,4,16,128]{3,2,1,0:T(8,128)(2,1)S(1)}) custom-call(bf16[3072,128]{1,0:T(8,128)(2,1)S(1)} %bitcast.2, bf16[128,128]{1,0:T(8,128)(2,1)S(1)} %copy-done.2, s32[32,64]{1,0:T(8,128)S(1)} %bitcast.3), custom_call_target="tpu_custom_call" | custom-call | tf_op jit(solution)/shard_map/payload/pallas_call | solution.py:639
  5.8 3.2 %collective-permute-start = (bf16[16,104,128]{2,1,0:T(8,128)(2,1)S(1)}, bf16[16,104,128]{2,1,0:T(8,128)(2,1)S(1)}, u32[]{:S(2)}, u32[]{:S(2)}) collective-permute-start(bf16[16,104,128]{2,1,0:T(8,128)(2,1)S(1)} %get-tuple-element.13), channel_id=1, source_target_pairs={{0,32},{32,0},{64,96},{96,64},{128,160},{160,128},{192,224},{224,1... | collective-permute-start | bytes 1277960 | tf_op jit(solution)/shard_map/ppermute | solution.py:614
  9.0 0.0 collective-permute-start.1
  9.1 1.9 %collective-permute-start.2 = (bf16[64,4,16,128]{3,2,1,0:T(8,128)(2,1)S(1)}, bf16[64,4,16,128]{3,2,1,0:T(8,128)(2,1)}, u32[]{:S(2)}, u32[]{:S(2)}) collective-permute-start(bf16[64,4,16,128]{3,2,1,0:T(8,128)(2,1)S(1)} %get-tuple-element.14.own_ref), channel_id=1, source_target_pairs={{32,64},{64,32},{96,128},{128,96},{160,192},{192,160},{33,65},{65,... | collective-permute-start | bytes 3145736 | tf_op jit(solution)/shard_map/ppermute | solution.py:619
  11.0 0.0 collective-permute-done
  11.0 0.8 %constant_dynamic-update-slice_fusion.order_ref = bf16[32,104,128]{2,1,0:T(8,128)(2,1)} fusion(bf16[32,104,128]{2,1,0:T(8,128)(2,1)} %get-tuple-element.12, bf16[16,104,128]{2,1,0:T(8,128)(2,1)S(1)} %collective-permute-done, s32[]{:T(128)S(6)} %select_n.11), kind=kLoop, calls=%fused_computation | loop fusion | bytes 851972 | tf_op jit(solution)/shard_map/dynamic_update_slice | solution.py:652
  11.8 0.0 copy-start.1
  11.8 0.0 copy-start.4
  11.8 0.0 copy-start.5
  11.8 0.0 copy-start.6
  11.8 0.0 copy-start.7
  11.9 0.0 copy-start.8
  11.9 11.2 %all-to-all-start = ((bf16[32,104,128]{2,1,0:T(8,128)(2,1)}), bf16[32,104,128]{2,1,0:T(8,128)(2,1)S(1)}, u32[]{:S(2)}, u32[]{:S(2)}) async-start(bf16[32,104,128]{2,1,0:T(8,128)(2,1)} %constant_dynamic-update-slice_fusion.order_ref), calls=%async_computation | async-start | bytes 1703936 | tf_op jit(solution)/shard_map/all_to_all | solution.py:655
  23.1 0.0 collective-permute-done.1.core_ref
  23.1 2.4 %collective-permute-done.2.x_ref = bf16[64,4,16,128]{3,2,1,0:T(8,128)(2,1)} collective-permute-done((bf16[64,4,16,128]{3,2,1,0:T(8,128)(2,1)S(1)}, bf16[64,4,16,128]{3,2,1,0:T(8,128)(2,1)}, u32[]{:S(2)}, u32[]{:S(2)}) %collective-permute-start.2) | collective-permute-done | bytes 1048608 | tf_op jit(solution)/shard_map/ppermute | solution.py:619
  25.4 0.0 copy-done.1
  25.5 0.0 copy-done.4
  25.5 0.0 copy-done.5
  25.5 0.0 copy-done.6
  25.5 0.0 copy-done.7
  25.5 0.0 copy-done.8
  25.5 17.5 %home.1 = (f32[64,416]{1,0:T(8,128)S(1)}, f32[16,64]{1,0:T(8,128)S(1)}, f32[16,64]{1,0:T(8,128)S(1)}, f32[16,64]{1,0:T(8,128)S(1)}, bf16[1,1,128]{2,1,0:T(2,128)(2,1)S(1)}) custom-call(s32[32,64]{1,0:T(8,128)S(1)} %bitcast.4, s32[32,64]{1,0:T(8,128)S(1)} %bitcast.5, f32[3,16]{1,0:T(4,128)S(1)} %copy-done.5, bf16[384,128]{1,0:T(8,128)(2,1)S(1)} %copy-done.7, ...), custom_call_target="tpu_custom_call" | custom-call | flops 10000000000 | bytes 10000000 | tf_op jit(solution)/shard_map/home/pallas_call | solution.py:661
  43.0 3.5 %all-to-all-done = bf16[32,104,128]{2,1,0:T(8,128)(2,1)S(1)} async-done(((bf16[32,104,128]{2,1,0:T(8,128)(2,1)}), bf16[32,104,128]{2,1,0:T(8,128)(2,1)S(1)}, u32[]{:S(2)}, u32[]{:S(2)}) %all-to-all-start) | async-done | bytes 852000 | tf_op jit(solution)/shard_map/all_to_all | solution.py:655
  46.6 0.1 collective-permute-start.3
  46.7 2.4 %collective-permute-done.3.other_ref = bf16[32,104,128]{2,1,0:T(8,128)(2,1)S(1)} collective-permute-done((bf16[32,104,128]{2,1,0:T(8,128)(2,1)S(1)}, bf16[32,104,128]{2,1,0:T(8,128)(2,1)S(1)}, u32[]{:S(2)}, u32[]{:S(2)}) %collective-permute-start.3) | collective-permute-done | bytes 852000 | tf_op jit(solution)/shard_map/ppermute | solution.py:614
  49.0 12.9 %task.1.order_ref = f32[32,2,128]{2,1,0:T(2,128)} custom-call(f32[3,16]{1,0:T(4,128)S(1)} %copy-done.5, bf16[32,104,128]{2,1,0:T(8,128)(2,1)S(1)} %dynamic_update_slice.7.mine_ref, bf16[32,104,128]{2,1,0:T(8,128)(2,1)S(1)} %collective-permute-done.3.other_ref, bf16[384,128]{1,0:T(8,128)(2,1)S(1)} %copy-done.7, f32[128,128]{1,0:T(8,128)S(1)} %copy-done.8, ...), custom_call_target="tpu_custom_call" | custom-call | flops 10000000000 | bytes 10000000 | tf_op jit(solution)/shard_map/task/pallas_call | solution.py:702
  61.9 6.0 %all-to-all-start.1 = ((f32[32,2,128]{2,1,0:T(2,128)}), f32[32,2,128]{2,1,0:T(2,128)S(1)}, u32[]{:S(2)}, u32[]{:S(2)}) async-start(f32[32,2,128]{2,1,0:T(2,128)} %task.1.order_ref), calls=%async_computation.1 | async-start | bytes 65536 | tf_op jit(solution)/shard_map/all_to_all | solution.py:725
  67.9 0.5 collective-permute-start.5
  68.5 3.3 %collective-permute-start.6 = (f32[16,64]{1,0:T(8,128)S(1)}, f32[16,64]{1,0:T(8,128)S(1)}, u32[]{:S(2)}, u32[]{:S(2)}) collective-permute-start(f32[16,64]{1,0:T(8,128)S(1)} %get-tuple-element.19), channel_id=1, source_target_pairs={{32,64},{64,32},{96,128},{128,96},{160,192},{192,160},{33,65},{65,... | collective-permute-start | bytes 12296 | tf_op jit(solution)/shard_map/ppermute | solution.py:619
  71.7 5.0 %all-to-all-done.1.kept_ref = f32[32,2,128]{2,1,0:T(2,128)S(1)} async-done(((f32[32,2,128]{2,1,0:T(2,128)}), f32[32,2,128]{2,1,0:T(2,128)S(1)}, u32[]{:S(2)}, u32[]{:S(2)}) %all-to-all-start.1) | async-done | bytes 32800 | tf_op jit(solution)/shard_map/all_to_all | solution.py:725
  76.7 1.5 %collective-permute-start.4 = (f32[32,2,128]{2,1,0:T(2,128)S(1)}, f32[32,2,128]{2,1,0:T(2,128)S(1)}, u32[]{:S(2)}, u32[]{:S(2)}) collective-permute-start(f32[32,2,128]{2,1,0:T(2,128)S(1)} %all-to-all-done.1.kept_ref), channel_id=1, source_target_pairs={{0,32},{32,0},{64,96},{96,64},{128,160},{160,128},{192,224},{224,1... | collective-permute-start | bytes 98312 | tf_op jit(solution)/shard_map/ppermute | solution.py:614
  78.2 0.0 collective-permute-done.5.core_ref
  78.2 0.0 collective-permute-done.6.x_ref
  78.2 0.7 gather.1
  79.0 0.1 collective-permute-done.4.got_ref
  79.1 2.0 %final.1 = (f32[64,512]{1,0:T(8,128)}, f32[4,64]{1,0:T(4,128)}) custom-call(f32[32,2,128]{2,1,0:T(2,128)S(1)} %all-to-all-done.1.kept_ref, f32[32,2,128]{2,1,0:T(2,128)S(1)} %collective-permute-done.4.got_ref, f32[64,512]{1,0:T(8,128)} %get-tuple-element.20.home_lag_ref, f32[16,64]{1,0:T(8,128)S(1)} %get-tuple-element.21.sums_ref, ...), custom_call_target="tpu_custom_call", output_to_operand_aliasing={{0}: (2, {})} | custom-call | tf_op jit(solution)/shard_map/final/pallas_call | solution.py:738
  (1 shorter events, 0.0 us)
Async XLA Ops:
  0.6 1.1 %copy-start = (bf16[64,48,128]{2,1,0:T(8,128)(2,1)S(1)}, bf16[64,48,128]{2,1,0:T(8,128)(2,1)}, u32[]{:S(2)}) copy-start(bf16[64,48,128]{2,1,0:T(8,128)(2,1)} %param.8) | copy-start | bytes 2359300
  1.8 0.8 copy-start.2
  2.5 0.7 copy-start.3
  5.8 5.2 %collective-permute-start = (bf16[16,104,128]{2,1,0:T(8,128)(2,1)S(1)}, bf16[16,104,128]{2,1,0:T(8,128)(2,1)S(1)}, u32[]{:S(2)}, u32[]{:S(2)}) collective-permute-start(bf16[16,104,128]{2,1,0:T(8,128)(2,1)S(1)} %get-tuple-element.13), channel_id=1, source_target_pairs={{0,32},{32,0},{64,96},{96,64},{128,160},{160,128},{192,224},{224,1... | collective-permute-start | bytes 1277960 | tf_op jit(solution)/shard_map/ppermute | solution.py:614
  9.0 14.0 %collective-permute-start.1 = (bf16[64,4,16,128]{3,2,1,0:T(8,128)(2,1)S(1)}, bf16[64,4,16,128]{3,2,1,0:T(8,128)(2,1)}, u32[]{:S(2)}, u32[]{:S(2)}) collective-permute-start(bf16[64,4,16,128]{3,2,1,0:T(8,128)(2,1)S(1)} %get-tuple-element.14.own_ref), channel_id=1, source_target_pairs={{0,32},{32,0},{64,96},{96,64},{128,160},{160,128},{192,224},{224,1... | collective-permute-start | bytes 3145736 | tf_op jit(solution)/shard_map/ppermute | solution.py:614
  9.1 16.4 %collective-permute-start.2 = (bf16[64,4,16,128]{3,2,1,0:T(8,128)(2,1)S(1)}, bf16[64,4,16,128]{3,2,1,0:T(8,128)(2,1)}, u32[]{:S(2)}, u32[]{:S(2)}) collective-permute-start(bf16[64,4,16,128]{3,2,1,0:T(8,128)(2,1)S(1)} %get-tuple-element.14.own_ref), channel_id=1, source_target_pairs={{32,64},{64,32},{96,128},{128,96},{160,192},{192,160},{33,65},{65,... | collective-permute-start | bytes 3145736 | tf_op jit(solution)/shard_map/ppermute | solution.py:619
  11.8 13.6 %copy-start.1 = (f32[4,16384]{1,0:T(4,128)S(1)}, f32[4,16384]{1,0:T(4,128)}, u32[]{:S(2)}) copy-start(f32[4,16384]{1,0:T(4,128)} %locations_ref.5) | copy-start | bytes 786436
  11.8 13.6 %copy-start.4 = (s32[64,32]{0,1:T(8,128)S(1)}, s32[64,32]{0,1:T(8,128)}, u32[]{:S(2)}) copy-start(s32[64,32]{0,1:T(8,128)} %param.9) | copy-start | bytes 24580
  11.8 13.6 %copy-start.5 = (f32[3,16]{1,0:T(4,128)S(1)}, f32[3,16]{1,0:T(4,128)}, u32[]{:S(2)}) copy-start(f32[3,16]{1,0:T(4,128)} %stations_ref.5) | copy-start | bytes 580
  11.8 13.6 %copy-start.6 = (s32[16,16384]{1,0:T(8,128)S(1)}, s32[16,16384]{1,0:T(8,128)}, u32[]{:S(2)}) copy-start(s32[16,16384]{1,0:T(8,128)} %masks_ref.3) | copy-start | bytes 3145732
  11.8 13.6 %copy-start.7 = (bf16[384,128]{1,0:T(8,128)(2,1)S(1)}, bf16[384,128]{1,0:T(8,128)(2,1)}, u32[]{:S(2)}) copy-start(bf16[384,128]{1,0:T(8,128)(2,1)} %constant.33.clone.inverse_ref) | copy-start | bytes 294916
  11.9 13.6 %copy-start.8 = (f32[128,128]{1,0:T(8,128)S(1)}, f32[128,128]{1,0:T(8,128)}, u32[]{:S(2)}) copy-start(f32[128,128]{1,0:T(8,128)} %constant.34.clone.values_ref) | copy-start | bytes 196612
  11.9 34.7 %all-to-all-start = ((bf16[32,104,128]{2,1,0:T(8,128)(2,1)}), bf16[32,104,128]{2,1,0:T(8,128)(2,1)S(1)}, u32[]{:S(2)}, u32[]{:S(2)}) async-start(bf16[32,104,128]{2,1,0:T(8,128)(2,1)} %constant_dynamic-update-slice_fusion.order_ref), calls=%async_computation | async-start | bytes 1703936 | tf_op jit(solution)/shard_map/all_to_all | solution.py:655
  46.6 2.5 %collective-permute-start.3 = (bf16[32,104,128]{2,1,0:T(8,128)(2,1)S(1)}, bf16[32,104,128]{2,1,0:T(8,128)(2,1)S(1)}, u32[]{:S(2)}, u32[]{:S(2)}) collective-permute-start(bf16[32,104,128]{2,1,0:T(8,128)(2,1)S(1)} %dynamic_update_slice.7.mine_ref), channel_id=1, source_target_pairs={{0,32},{32,0},{64,96},{96,64},{128,160},{160,128},{192,224},{224,1... | collective-permute-start | bytes 2555912 | tf_op jit(solution)/shard_map/ppermute | solution.py:614
  61.9 14.8 %all-to-all-start.1 = ((f32[32,2,128]{2,1,0:T(2,128)}), f32[32,2,128]{2,1,0:T(2,128)S(1)}, u32[]{:S(2)}, u32[]{:S(2)}) async-start(f32[32,2,128]{2,1,0:T(2,128)} %task.1.order_ref), calls=%async_computation.1 | async-start | bytes 65536 | tf_op jit(solution)/shard_map/all_to_all | solution.py:725
  67.9 10.3 %collective-permute-start.5 = (f32[16,64]{1,0:T(8,128)S(1)}, f32[16,64]{1,0:T(8,128)S(1)}, u32[]{:S(2)}, u32[]{:S(2)}) collective-permute-start(f32[16,64]{1,0:T(8,128)S(1)} %get-tuple-element.18), channel_id=1, source_target_pairs={{0,32},{32,0},{64,96},{96,64},{128,160},{160,128},{192,224},{224,1... | collective-permute-start | bytes 12296 | tf_op jit(solution)/shard_map/ppermute | solution.py:614
  68.5 9.8 %collective-permute-start.6 = (f32[16,64]{1,0:T(8,128)S(1)}, f32[16,64]{1,0:T(8,128)S(1)}, u32[]{:S(2)}, u32[]{:S(2)}) collective-permute-start(f32[16,64]{1,0:T(8,128)S(1)} %get-tuple-element.19), channel_id=1, source_target_pairs={{32,64},{64,32},{96,128},{128,96},{160,192},{192,160},{33,65},{65,... | collective-permute-start | bytes 12296 | tf_op jit(solution)/shard_map/ppermute | solution.py:619
  76.7 2.4 %collective-permute-start.4 = (f32[32,2,128]{2,1,0:T(2,128)S(1)}, f32[32,2,128]{2,1,0:T(2,128)S(1)}, u32[]{:S(2)}, u32[]{:S(2)}) collective-permute-start(f32[32,2,128]{2,1,0:T(2,128)S(1)} %all-to-all-done.1.kept_ref), channel_id=1, source_target_pairs={{0,32},{32,0},{64,96},{96,64},{128,160},{160,128},{192,224},{224,1... | collective-permute-start | bytes 98312 | tf_op jit(solution)/shard_map/ppermute | solution.py:614

commit v3 on v2

--- a/solution.py
+++ b/solution.py
@@ -242,7 +242,6 @@
     x_ref,
     locations_ref,
     masks_ref,
-    order_ref,
     lag_ref,
     sums_ref,
     to_core_ref,
@@ -532,38 +531,54 @@
             )
 
 
-def gather_kernel(home_lag_ref, sums_ref, core_ref, x_ref, order_ref, lag_ref, out_ref):
-    stations = sums_ref.shape[0]
+def gather_kernel(
+    home_lag_ref,
+    sums_ref,
+    core_ref,
+    x_ref,
+    stations_ref,
+    locations_ref,
+    order_ref,
+    lag_ref,
+    last_ref,
+    out_ref,
+    direction_ref,
+    place_window,
+    sem,
+):
+    stations, events = sums_ref.shape
+    copy = near_columns(locations_ref, place_window, sem, lax.axis_index("region"))
     local = K_LOCAL * stations
     remote = K_REGION * stations
     home = home_lag_ref[...]
-    gap = jnp.zeros((home.shape[0], remote), F32)
-    lag_ref[...] = jnp.concatenate([home[:, :local], gap, home[:, local:]], axis=1)
+    gap = jnp.zeros((events, remote), F32)
+    last = jnp.concatenate([gap, home[:, local:]], axis=1)
+    last_ref[...] = last
+    lag_ref[...] = jnp.concatenate([home[:, :local], last], axis=1)
     out_ref[...] = sums_ref[...] - core_ref[...] - x_ref[...]
+    copy.wait()
+    offsets, distance = travel(own_columns(place_window), stations_ref[...].T)
+    for c in range(3):
+        direction_ref[c] = offsets[c] / (WAVE_SPEED * distance)
 
 
 def final_kernel(
     kept_ref,
     got_ref,
+    last_ref,
+    sums_ref,
+    direction_ref,
     home_lag_ref,
-    sums_ref,
-    stations_ref,
-    locations_ref,
     lag_ref,
     grad_ref,
-    place_window,
     lag_window,
-    sems,
+    sem,
 ):
     events = grad_ref.shape[1]
     stations = sums_ref.shape[0]
     part = events // 2
     span = K_REGION * part
     core = lax.axis_index("region") % 2
-    copy = near_columns(locations_ref, place_window, sems.at[0], lax.axis_index("region"))
-    columns = pl.ds(K_LOCAL * stations, LANES)
-    lags = pltpu.make_async_copy(home_lag_ref.at[:, columns], lag_window, sems.at[1])
-    lags.start()
     sums = sums_ref[...]
     block = pl.ds(pl.multiple_of(core * stations, stations), stations)
     kept, got = kept_ref[block], got_ref[block]
@@ -576,15 +591,12 @@
             jnp.concatenate([turned[n * part : (n + 1) * part] for n in range(K_REGION)], axis=1)
         )
     rows = jnp.concatenate(rows, axis=0)
-    copy.wait()
-    lags.wait()
-    lag_window[:, : rows.shape[1]] = rows
-    lags = pltpu.make_async_copy(lag_window, lag_ref.at[:, columns], sems.at[1])
+    lag_window[...] = jnp.concatenate([rows, last_ref[:, rows.shape[1] :]], axis=1)
+    columns = pl.ds(K_LOCAL * stations, LANES)
+    lags = pltpu.make_async_copy(lag_window, lag_ref.at[:, columns], sem)
     lags.start()
-    offsets, distance = travel(own_columns(place_window), stations_ref[...].T)
     for c in range(3):
-        direction = offsets[c] / (WAVE_SPEED * distance)
-        grad_ref[c : c + 1, :] = jnp.sum(direction * sums, axis=0, keepdims=True)
+        grad_ref[c : c + 1, :] = jnp.sum(direction_ref[c] * sums, axis=0, keepdims=True)
     grad_ref[3:4, :] = jnp.sum(sums, axis=0, keepdims=True)
     lags.wait()
 
@@ -646,7 +658,7 @@
         in_specs=vmem(3),
         out_specs=vmem(3),
         scratch_shapes=[pltpu.VMEM((events * channels, samples), F32)],
-        compiler_params=params(16),
+        compiler_params=params(60),
         name="payload",
     )(wave_rows, table, id_columns)
     payload = lax.dynamic_update_slice_in_dim(
@@ -667,7 +679,7 @@
             shape((station_count, events)),
             shape((1, 1, LANES), BF16),
         ),
-        in_specs=smem(1) + vmem(4) + anywhere(6),
+        in_specs=smem(1) + vmem(4) + anywhere(5),
         out_specs=vmem(5),
         scratch_shapes=[
             pltpu.VMEM((3 * events, *by_event_shape[1:]), BF16),
@@ -692,7 +704,6 @@
         x_spec,
         locations,
         masks,
-        payload,
     )
     from_core = other_core(to_core)
     from_x = other_chip(to_x)
@@ -723,35 +734,34 @@
         name="task",
     )(stations, mine, other, inverse, values, locations, masks)
     back = lax.all_to_all(results, "slab", 0, 0, tiled=True)
-    lag_home, sums = pl.pallas_call(
+    lag_home, last, sums, direction = pl.pallas_call(
         gather_kernel,
         out_shape=(
             shape((events, neighbour_count * station_count)),
+            shape((events, LANES)),
             shape((station_count, events)),
+            shape((3, station_count, events)),
         ),
-        in_specs=vmem(4) + anywhere(1),
-        out_specs=vmem(2),
+        in_specs=vmem(5) + anywhere(2),
+        out_specs=vmem(4),
+        scratch_shapes=[pltpu.VMEM((4, LANES), F32), pltpu.SemaphoreType.DMA],
         compiler_params=params(8),
         cost_estimate=pl.CostEstimate(flops=10**9, bytes_accessed=10**7, transcendentals=0),
         name="gather",
-    )(lag_home, sums, from_core, from_x, results)
+    )(lag_home, sums, from_core, from_x, stations, locations, results)
     return pl.pallas_call(
         final_kernel,
         out_shape=(
             shape((events, neighbour_count * station_count)),
             shape((4, events)),
         ),
-        in_specs=vmem(2) + anywhere(1) + vmem(2) + anywhere(1),
+        in_specs=vmem(5) + anywhere(1),
         out_specs=(anywhere(1)[0], vmem(1)[0]),
-        scratch_shapes=[
-            pltpu.VMEM((4, LANES), F32),
-            pltpu.VMEM((events, LANES), F32),
-            pltpu.SemaphoreType.DMA((2,)),
-        ],
-        input_output_aliases={2: 0},
+        scratch_shapes=[pltpu.VMEM((events, LANES), F32), pltpu.SemaphoreType.DMA],
+        input_output_aliases={5: 0},
         compiler_params=params(8),
         name="final",
-    )(back, other_core(back), lag_home, sums, stations, locations)
+    )(back, other_core(back), last, sums, direction, lag_home)
 
 
 def solution(mesh):

time: 81.6 us -> 80.1 us (0.982)
  starting transfers between devices: 27.8 us -> 30.6 us
  waiting for transfers between devices: 13.4 us -> 10.7 us
  local copies, waits for them, and re-layouts: 3.47 us -> 0.87 us
  Pallas kernels: 35.7 us -> 36.8 us
    ppermute x5, starting transfers between devices: 5.39 us -> 9.32 us  [other_core(): lax.ppermute(block, 'region', [(i, i + 1 - 2 * (i % 2)) for i in range(co...]
    all_to_all x1, waiting for transfers between devices: 3.5 us -> 0.62 us  [per_device(): mine = lax.all_to_all(payload, 'slab', 0, 0, tiled=True)]
    unnamed x18 -> x14, local copies, waits for them, and re-layouts: 2.63 us -> 0.03 us
    pallas_call x1, Pallas kernels: 2.56 us -> 4.2 us  [per_device(): pl.pallas_call(payload_kernel, out_shape=(shape((slab_count, payload_rows...]
where the time goes in v3:
time: 80.1 us; the launch traced here: 79.8 us
  Pallas kernels  36.8 us (46%)
  starting transfers between devices  30.6 us (38%)
  waiting for transfers between devices  10.7 us (13%)
  local copies, waits for them, and re-layouts  0.87 us (1%)
    pallas_call x1, Pallas kernels, per_device(): pl.pallas_call(home_kernel, out_shape=(shape((events, width)), shape((sta...  17.5 us
    pallas_call x1, Pallas kernels, per_device(): pl.pallas_call(task_kernel, out_shape=shape((slab_count, 2, LANES)), in_s...  12.9 us
    all_to_all x1, starting transfers between devices, per_device(): mine = lax.all_to_all(payload, 'slab', 0, 0, tiled=True)  10.7 us
    ppermute x5, starting transfers between devices, other_core(): lax.ppermute(block, 'region', [(i, i + 1 - 2 * (i % 2)) for i in range(co...  9.32 us
    all_to_all x1, starting transfers between devices, per_device(): back = lax.all_to_all(results, 'slab', 0, 0, tiled=True)  5.59 us
    all_to_all x1, waiting for transfers between devices, per_device(): back = lax.all_to_all(results, 'slab', 0, 0, tiled=True)  5.15 us
    ppermute x2, starting transfers between devices, other_chip(): lax.ppermute(block, 'region', [p for i in odd for p in ((i, i + 1), (i +...  4.99 us
    pallas_call x1, Pallas kernels, per_device(): pl.pallas_call(payload_kernel, out_shape=(shape((slab_count, payload_rows...  4.2 us
  transfers between devices with their start and end apart: 9, of which 5 were waited for; matrix products, arithmetic and copies ran while one was open for 1% of the time, Pallas kernels for 23%

profile of v3, /device:TPU:1, one launch (start us, length us, event | category | flops | bytes accessed | tf_op | source)
XLA Modules:
  0.0 79.8 jit_solution(5831972136952545428)
XLA Ops:
  0.6 4.2 %payload.1 = (bf16[32,104,128]{2,1,0:T(8,128)(2,1)}, bf16[16,104,128]{2,1,0:T(8,128)(2,1)}, bf16[64,4,16,128]{3,2,1,0:T(8,128)(2,1)}) custom-call(bf16[3072,128]{1,0:T(8,128)(2,1)} %bitcast.5, bf16[128,128]{1,0:T(8,128)(2,1)} %constant.35.clone.table_ref, s32[32,64]{1,0:T(8,128)} %bitcast.2), custom_call_target="tpu_custom_call" | custom-call | tf_op jit(solution)/shard_map/payload/pallas_call | solution.py:651
  4.8 3.2 %collective-permute-start = (bf16[16,104,128]{2,1,0:T(8,128)(2,1)}, bf16[16,104,128]{2,1,0:T(8,128)(2,1)S(1)}, u32[]{:S(2)}, u32[]{:S(2)}) collective-permute-start(bf16[16,104,128]{2,1,0:T(8,128)(2,1)} %get-tuple-element.15), channel_id=1, source_target_pairs={{0,32},{32,0},{64,96},{96,64},{128,160},{160,128},{192,224},{224,1... | collective-permute-start | bytes 1277960 | tf_op jit(solution)/shard_map/ppermute | solution.py:626
  8.1 1.9 %collective-permute-start.2 = (bf16[64,4,16,128]{3,2,1,0:T(8,128)(2,1)}, bf16[64,4,16,128]{3,2,1,0:T(8,128)(2,1)}, u32[]{:S(2)}, u32[]{:S(2)}) collective-permute-start(bf16[64,4,16,128]{3,2,1,0:T(8,128)(2,1)} %get-tuple-element.16.own_ref), channel_id=1, source_target_pairs={{32,64},{64,32},{96,128},{128,96},{160,192},{192,160},{33,65},{65,... | collective-permute-start | bytes 3145736 | tf_op jit(solution)/shard_map/ppermute | solution.py:631
  10.0 0.1 collective-permute-start.1
  10.1 0.0 collective-permute-done
  10.1 0.0 copy-start.2
  10.1 0.8 %constant_dynamic-update-slice_fusion = bf16[32,104,128]{2,1,0:T(8,128)(2,1)} fusion(bf16[32,104,128]{2,1,0:T(8,128)(2,1)} %get-tuple-element.14, bf16[16,104,128]{2,1,0:T(8,128)(2,1)S(1)} %collective-permute-done, s32[]{:T(128)S(6)} %select_n.11), kind=kLoop, calls=%fused_computation | loop fusion | bytes 851972 | tf_op jit(solution)/shard_map/dynamic_update_slice | solution.py:664
  10.9 0.0 copy-start
  10.9 0.0 copy-start.1
  10.9 0.0 copy-start.3
  10.9 0.0 copy-start.4
  10.9 0.0 copy-start.5
  11.0 0.0 copy-start.6
  11.0 10.7 %all-to-all-start = ((bf16[32,104,128]{2,1,0:T(8,128)(2,1)}), bf16[32,104,128]{2,1,0:T(8,128)(2,1)S(1)}, u32[]{:S(2)}, u32[]{:S(2)}) async-start(bf16[32,104,128]{2,1,0:T(8,128)(2,1)} %constant_dynamic-update-slice_fusion), calls=%async_computation | async-start | bytes 1703936 | tf_op jit(solution)/shard_map/all_to_all | solution.py:667
  21.7 2.8 %collective-permute-done.2.x_ref = bf16[64,4,16,128]{3,2,1,0:T(8,128)(2,1)} collective-permute-done((bf16[64,4,16,128]{3,2,1,0:T(8,128)(2,1)}, bf16[64,4,16,128]{3,2,1,0:T(8,128)(2,1)}, u32[]{:S(2)}, u32[]{:S(2)}) %collective-permute-start.2) | collective-permute-done | bytes 1048608 | tf_op jit(solution)/shard_map/ppermute | solution.py:631
  24.5 0.0 collective-permute-done.1.core_ref
  24.5 0.0 copy-done.2
  24.5 0.0 copy-done
  24.5 0.0 copy-done.1
  24.5 0.0 copy-done.3
  24.5 0.0 copy-done.4
  24.5 0.0 copy-done.5
  24.5 0.0 copy-done.6
  24.6 17.5 %home.1 = (f32[64,416]{1,0:T(8,128)S(1)}, f32[16,64]{1,0:T(8,128)S(1)}, f32[16,64]{1,0:T(8,128)S(1)}, f32[16,64]{1,0:T(8,128)S(1)}, bf16[1,1,128]{2,1,0:T(2,128)(2,1)S(1)}) custom-call(s32[32,64]{1,0:T(8,128)S(1)} %bitcast.3, s32[32,64]{1,0:T(8,128)S(1)} %bitcast.4, f32[3,16]{1,0:T(4,128)S(1)} %copy-done.4, bf16[384,128]{1,0:T(8,128)(2,1)S(1)} %copy-done.5, ...), custom_call_target="tpu_custom_call" | custom-call | flops 10000000000 | bytes 10000000 | tf_op jit(solution)/shard_map/home/pallas_call | solution.py:673
  42.1 0.6 all-to-all-done
  42.8 3.9 %collective-permute-start.3 = (bf16[32,104,128]{2,1,0:T(8,128)(2,1)S(1)}, bf16[32,104,128]{2,1,0:T(8,128)(2,1)S(1)}, u32[]{:S(2)}, u32[]{:S(2)}) collective-permute-start(bf16[32,104,128]{2,1,0:T(8,128)(2,1)S(1)} %dynamic_update_slice.7.mine_ref), channel_id=1, source_target_pairs={{0,32},{32,0},{64,96},{96,64},{128,160},{160,128},{192,224},{224,1... | collective-permute-start | bytes 2555912 | tf_op jit(solution)/shard_map/ppermute | solution.py:626
  46.7 2.0 %collective-permute-done.3.other_ref = bf16[32,104,128]{2,1,0:T(8,128)(2,1)S(1)} collective-permute-done((bf16[32,104,128]{2,1,0:T(8,128)(2,1)S(1)}, bf16[32,104,128]{2,1,0:T(8,128)(2,1)S(1)}, u32[]{:S(2)}, u32[]{:S(2)}) %collective-permute-start.3) | collective-permute-done | bytes 852000 | tf_op jit(solution)/shard_map/ppermute | solution.py:626
  48.7 12.9 %task.1.order_ref = f32[32,2,128]{2,1,0:T(2,128)} custom-call(f32[3,16]{1,0:T(4,128)S(1)} %copy-done.4, bf16[32,104,128]{2,1,0:T(8,128)(2,1)S(1)} %dynamic_update_slice.7.mine_ref, bf16[32,104,128]{2,1,0:T(8,128)(2,1)S(1)} %collective-permute-done.3.other_ref, bf16[384,128]{1,0:T(8,128)(2,1)S(1)} %copy-done.5, f32[128,128]{1,0:T(8,128)S(1)} %copy-done.6, ...), custom_call_target="tpu_custom_call" | custom-call | flops 10000000000 | bytes 10000000 | tf_op jit(solution)/shard_map/task/pallas_call | solution.py:713
  61.6 5.6 %all-to-all-start.1 = ((f32[32,2,128]{2,1,0:T(2,128)}), f32[32,2,128]{2,1,0:T(2,128)S(1)}, u32[]{:S(2)}, u32[]{:S(2)}) async-start(f32[32,2,128]{2,1,0:T(2,128)} %task.1.order_ref), calls=%async_computation.1 | async-start | bytes 65536 | tf_op jit(solution)/shard_map/all_to_all | solution.py:736
  67.2 0.5 collective-permute-start.5
  67.7 3.1 %collective-permute-start.6 = (f32[16,64]{1,0:T(8,128)S(1)}, f32[16,64]{1,0:T(8,128)S(1)}, u32[]{:S(2)}, u32[]{:S(2)}) collective-permute-start(f32[16,64]{1,0:T(8,128)S(1)} %get-tuple-element.21), channel_id=1, source_target_pairs={{32,64},{64,32},{96,128},{128,96},{160,192},{192,160},{33,65},{65,... | collective-permute-start | bytes 12296 | tf_op jit(solution)/shard_map/ppermute | solution.py:631
  70.8 5.1 %all-to-all-done.1.kept_ref = f32[32,2,128]{2,1,0:T(2,128)S(1)} async-done(((f32[32,2,128]{2,1,0:T(2,128)}), f32[32,2,128]{2,1,0:T(2,128)S(1)}, u32[]{:S(2)}, u32[]{:S(2)}) %all-to-all-start.1) | async-done | bytes 32800 | tf_op jit(solution)/shard_map/all_to_all | solution.py:736
  75.9 1.5 %collective-permute-start.4 = (f32[32,2,128]{2,1,0:T(2,128)S(1)}, f32[32,2,128]{2,1,0:T(2,128)S(1)}, u32[]{:S(2)}, u32[]{:S(2)}) collective-permute-start(f32[32,2,128]{2,1,0:T(2,128)S(1)} %all-to-all-done.1.kept_ref), channel_id=1, source_target_pairs={{0,32},{32,0},{64,96},{96,64},{128,160},{160,128},{192,224},{224,1... | collective-permute-start | bytes 98312 | tf_op jit(solution)/shard_map/ppermute | solution.py:626
  77.5 0.0 collective-permute-done.5.core_ref
  77.5 0.0 collective-permute-done.6.x_ref
  77.5 0.8 gather.1
  78.3 0.1 collective-permute-done.4.got_ref
  78.3 1.4 %final.1 = (f32[64,512]{1,0:T(8,128)}, f32[4,64]{1,0:T(4,128)}) custom-call(f32[32,2,128]{2,1,0:T(2,128)S(1)} %all-to-all-done.1.kept_ref, f32[32,2,128]{2,1,0:T(2,128)S(1)} %collective-permute-done.4.got_ref, f32[64,128]{1,0:T(8,128)S(1)} %get-tuple-element.22.last_ref, f32[16,64]{1,0:T(8,128)S(1)} %get-tuple-element.23.sums_ref, ...), custom_call_target="tpu_custom_call", output_to_operand_aliasing={{0}: (5, {})} | custom-call | tf_op jit(solution)/shard_map/final/pallas_call | solution.py:752
  (1 shorter events, 0.0 us)
Async XLA Ops:
  4.8 5.3 %collective-permute-start = (bf16[16,104,128]{2,1,0:T(8,128)(2,1)}, bf16[16,104,128]{2,1,0:T(8,128)(2,1)S(1)}, u32[]{:S(2)}, u32[]{:S(2)}) collective-permute-start(bf16[16,104,128]{2,1,0:T(8,128)(2,1)} %get-tuple-element.15), channel_id=1, source_target_pairs={{0,32},{32,0},{64,96},{96,64},{128,160},{160,128},{192,224},{224,1... | collective-permute-start | bytes 1277960 | tf_op jit(solution)/shard_map/ppermute | solution.py:626
  8.1 16.4 %collective-permute-start.2 = (bf16[64,4,16,128]{3,2,1,0:T(8,128)(2,1)}, bf16[64,4,16,128]{3,2,1,0:T(8,128)(2,1)}, u32[]{:S(2)}, u32[]{:S(2)}) collective-permute-start(bf16[64,4,16,128]{3,2,1,0:T(8,128)(2,1)} %get-tuple-element.16.own_ref), channel_id=1, source_target_pairs={{32,64},{64,32},{96,128},{128,96},{160,192},{192,160},{33,65},{65,... | collective-permute-start | bytes 3145736 | tf_op jit(solution)/shard_map/ppermute | solution.py:631
  10.0 14.5 %collective-permute-start.1 = (bf16[64,4,16,128]{3,2,1,0:T(8,128)(2,1)}, bf16[64,4,16,128]{3,2,1,0:T(8,128)(2,1)}, u32[]{:S(2)}, u32[]{:S(2)}) collective-permute-start(bf16[64,4,16,128]{3,2,1,0:T(8,128)(2,1)} %get-tuple-element.16.own_ref), channel_id=1, source_target_pairs={{0,32},{32,0},{64,96},{96,64},{128,160},{160,128},{192,224},{224,1... | collective-permute-start | bytes 3145736 | tf_op jit(solution)/shard_map/ppermute | solution.py:626
  10.1 14.4 %copy-start.2 = (bf16[64,4,16,128]{3,2,1,0:T(8,128)(2,1)S(1)}, bf16[64,4,16,128]{3,2,1,0:T(8,128)(2,1)}, u32[]{:S(2)}) copy-start(bf16[64,4,16,128]{3,2,1,0:T(8,128)(2,1)} %get-tuple-element.16.own_ref) | copy-start | bytes 3145732
  10.9 13.6 %copy-start = (s32[64,32]{0,1:T(8,128)S(1)}, s32[64,32]{0,1:T(8,128)}, u32[]{:S(2)}) copy-start(s32[64,32]{0,1:T(8,128)} %param.9) | copy-start | bytes 24580
  10.9 13.6 %copy-start.1 = (s32[16,16384]{1,0:T(8,128)S(1)}, s32[16,16384]{1,0:T(8,128)}, u32[]{:S(2)}) copy-start(s32[16,16384]{1,0:T(8,128)} %masks_ref.3) | copy-start | bytes 3145732
  10.9 13.6 %copy-start.3 = (f32[4,16384]{1,0:T(4,128)S(1)}, f32[4,16384]{1,0:T(4,128)}, u32[]{:S(2)}) copy-start(f32[4,16384]{1,0:T(4,128)} %locations_ref.5) | copy-start | bytes 786436
  10.9 13.6 %copy-start.4 = (f32[3,16]{1,0:T(4,128)S(1)}, f32[3,16]{1,0:T(4,128)}, u32[]{:S(2)}) copy-start(f32[3,16]{1,0:T(4,128)} %stations_ref.5) | copy-start | bytes 580
  10.9 13.6 %copy-start.5 = (bf16[384,128]{1,0:T(8,128)(2,1)S(1)}, bf16[384,128]{1,0:T(8,128)(2,1)}, u32[]{:S(2)}) copy-start(bf16[384,128]{1,0:T(8,128)(2,1)} %constant.33.clone.inverse_ref) | copy-start | bytes 294916
  11.0 13.6 %copy-start.6 = (f32[128,128]{1,0:T(8,128)S(1)}, f32[128,128]{1,0:T(8,128)}, u32[]{:S(2)}) copy-start(f32[128,128]{1,0:T(8,128)} %constant.34.clone.values_ref) | copy-start | bytes 196612
  11.0 31.8 %all-to-all-start = ((bf16[32,104,128]{2,1,0:T(8,128)(2,1)}), bf16[32,104,128]{2,1,0:T(8,128)(2,1)S(1)}, u32[]{:S(2)}, u32[]{:S(2)}) async-start(bf16[32,104,128]{2,1,0:T(8,128)(2,1)} %constant_dynamic-update-slice_fusion), calls=%async_computation | async-start | bytes 1703936 | tf_op jit(solution)/shard_map/all_to_all | solution.py:667
  42.8 5.9 %collective-permute-start.3 = (bf16[32,104,128]{2,1,0:T(8,128)(2,1)S(1)}, bf16[32,104,128]{2,1,0:T(8,128)(2,1)S(1)}, u32[]{:S(2)}, u32[]{:S(2)}) collective-permute-start(bf16[32,104,128]{2,1,0:T(8,128)(2,1)S(1)} %dynamic_update_slice.7.mine_ref), channel_id=1, source_target_pairs={{0,32},{32,0},{64,96},{96,64},{128,160},{160,128},{192,224},{224,1... | collective-permute-start | bytes 2555912 | tf_op jit(solution)/shard_map/ppermute | solution.py:626
  61.6 14.4 %all-to-all-start.1 = ((f32[32,2,128]{2,1,0:T(2,128)}), f32[32,2,128]{2,1,0:T(2,128)S(1)}, u32[]{:S(2)}, u32[]{:S(2)}) async-start(f32[32,2,128]{2,1,0:T(2,128)} %task.1.order_ref), calls=%async_computation.1 | async-start | bytes 65536 | tf_op jit(solution)/shard_map/all_to_all | solution.py:736
  67.2 10.3 %collective-permute-start.5 = (f32[16,64]{1,0:T(8,128)S(1)}, f32[16,64]{1,0:T(8,128)S(1)}, u32[]{:S(2)}, u32[]{:S(2)}) collective-permute-start(f32[16,64]{1,0:T(8,128)S(1)} %get-tuple-element.20), channel_id=1, source_target_pairs={{0,32},{32,0},{64,96},{96,64},{128,160},{160,128},{192,224},{224,1... | collective-permute-start | bytes 12296 | tf_op jit(solution)/shard_map/ppermute | solution.py:626
  67.7 9.8 %collective-permute-start.6 = (f32[16,64]{1,0:T(8,128)S(1)}, f32[16,64]{1,0:T(8,128)S(1)}, u32[]{:S(2)}, u32[]{:S(2)}) collective-permute-start(f32[16,64]{1,0:T(8,128)S(1)} %get-tuple-element.21), channel_id=1, source_target_pairs={{32,64},{64,32},{96,128},{128,96},{160,192},{192,160},{33,65},{65,... | collective-permute-start | bytes 12296 | tf_op jit(solution)/shard_map/ppermute | solution.py:631
  75.9 2.4 %collective-permute-start.4 = (f32[32,2,128]{2,1,0:T(2,128)S(1)}, f32[32,2,128]{2,1,0:T(2,128)S(1)}, u32[]{:S(2)}, u32[]{:S(2)}) collective-permute-start(f32[32,2,128]{2,1,0:T(2,128)S(1)} %all-to-all-done.1.kept_ref), channel_id=1, source_target_pairs={{0,32},{32,0},{64,96},{96,64},{128,160},{160,128},{192,224},{224,1... | collective-permute-start | bytes 98312 | tf_op jit(solution)/shard_map/ppermute | solution.py:626

commit v4 on v3

--- a/solution.py
+++ b/solution.py
@@ -343,26 +343,25 @@
     to_x_ref[...] = sums[:, 2 * events :]
 
 
-def task_kernel(
+def pair_ids(id_rows, step, span):
+    pieces = []
+    for u in range(2):
+        row = 4 * step + 2 * u
+        pieces.append(id_rows[pl.ds(row, 1), :])
+        pieces.append(id_rows[pl.ds(row + 1, 1), :][:, : span - LANES])
+    return jnp.concatenate(pieces, axis=1)
+
+
+def lookup_kernel(
     stations_ref,
     mine_ref,
-    other_ref,
-    inverse_ref,
-    values_ref,
     locations_ref,
     masks_ref,
-    out_ref,
-    table,
-    fetched_even,
-    fetched_odd,
-    crossed_even,
-    crossed_odd,
     id_rows,
-    residuals,
+    found_ref,
     own_terms,
     place_window,
     mask_window,
-    ids,
     sems,
 ):
     sources, payload, _ = mine_ref.shape
@@ -392,22 +391,6 @@
         return carry
 
     lax.fori_loop(0, sources, read_ids, 0, unroll=8)
-    id_copy = pltpu.make_async_copy(id_rows, ids, sems.at[2])
-    id_copy.start()
-
-    def fill(source, carry):
-        for ref, half in ((mine_ref, core), (other_ref, 1 - core)):
-            rows = [
-                ref[source, k * part : (k + 1) * part, :].astype(F32) for k in range(COMPONENTS)
-            ]
-            rows.append(swapped(rows[-1]))
-            base = (source * events + half * part) * 8
-            for k, values_k in enumerate(rows):
-                table[pl.ds(base + k, part, stride=8), :] = values_k
-                table[pl.ds(base + 4 + k, part, stride=8), :] = values_k
-        return carry
-
-    lax.fori_loop(0, sources, fill, 0, unroll=4)
     for copy in copies:
         copy.wait()
     offsets = [place_window[c : c + 1, :] - stations_ref[c, station] for c in range(3)]
@@ -434,7 +417,72 @@
         2 * half_rows : 3 * half_rows
     ]
     own_terms[half_rows:] = own[3 * half_rows :]
+    source_rows = lax.broadcasted_iota(jnp.int32, (half_rows, width), 0)
+
+    def two_sources(step, carry):
+        id_row = pair_ids(id_rows, step, span) // 8
+        from_source = source_rows == id_row // LANES
+        from_event = jnp.where(event_rows == id_row % LANES, 1.0, 0.0).astype(BF16)
+        looked_up = jnp.dot(tables, from_event, preferred_element_type=F32)
+        arrival = looked_up[:half_rows] + looked_up[half_rows : 2 * half_rows]
+        arrival = arrival + looked_up[2 * half_rows : 3 * half_rows]
+        mask = jnp.where(from_source, looked_up[3 * half_rows :], 0.0)
+        found_ref[pl.ds(step, 1), :] = jnp.sum(
+            jnp.where(from_source, arrival, 0.0), axis=0, keepdims=True
+        )
+        found_ref[pl.ds(half_rows + step, 1), :] = jnp.sum(mask, axis=0, keepdims=True)
+        return carry
+
+    lax.fori_loop(0, half_rows, two_sources, 0, unroll=4)
+
+
+def task_kernel(
+    id_rows,
+    found_ref,
+    own_terms,
+    mine_ref,
+    other_ref,
+    inverse_ref,
+    values_ref,
+    out_ref,
+    table,
+    fetched_even,
+    fetched_odd,
+    crossed_even,
+    crossed_odd,
+    residuals,
+    ids,
+    sem,
+):
+    sources, payload, _ = mine_ref.shape
+    stations = sources // 2
+    part = payload // COMPONENTS // 8 * 8
+    events = 2 * part
+    span = K_REGION * part
+    width = 2 * span
+    core = lax.axis_index("region") % 2
+    half_rows = sources // 2
+    id_copy = pltpu.make_async_copy(id_rows, ids, sem)
+    id_copy.start()
+
+    def fill(source, carry):
+        for ref, half in ((mine_ref, core), (other_ref, 1 - core)):
+            rows = [
+                ref[source, k * part : (k + 1) * part, :].astype(F32) for k in range(COMPONENTS)
+            ]
+            rows.append(swapped(rows[-1]))
+            base = (source * events + half * part) * 8
+            for k, values_k in enumerate(rows):
+                table[pl.ds(base + k, part, stride=8), :] = values_k
+                table[pl.ds(base + 4 + k, part, stride=8), :] = values_k
+        return carry
+
+    lax.fori_loop(0, sources, fill, 0, unroll=4)
     id_copy.wait()
+    lane = lax.broadcasted_iota(jnp.int32, (LANES, width), 1)
+    event_rows = lax.broadcasted_iota(jnp.int32, (LANES, width), 0)
+    own_hits = event_rows == lane // span * events + core * part + lane % part
+    own_hits = jnp.where(own_hits, 1.0, 0.0).astype(BF16)
 
     upper = lax.broadcasted_iota(jnp.int32, (8, LANES), 0) < 4
     source_rows = lax.broadcasted_iota(jnp.int32, (half_rows, width), 0)
@@ -473,26 +521,11 @@
             out_ref[2 * step + u] = jnp.concatenate(
                 [lag[:, u * span : u * span + LANES], rest], axis=0
             )
-        id_row = jnp.concatenate(
-            [
-                piece
-                for u in range(2)
-                for piece in (
-                    id_rows[pl.ds(4 * step + 2 * u, 1), :],
-                    id_rows[pl.ds(4 * step + 2 * u + 1, 1), :][:, : span - LANES],
-                )
-            ],
-            axis=1,
-        )
-        id_row = id_row // 8
+        id_row = pair_ids(id_rows, step, span) // 8
         from_source = source_rows == id_row // LANES
         from_event = jnp.where(event_rows == id_row % LANES, 1.0, 0.0).astype(BF16)
-        looked_up = jnp.dot(tables, from_event, preferred_element_type=F32)
-        arrival = looked_up[:half_rows] + looked_up[half_rows : 2 * half_rows]
-        arrival = arrival + looked_up[2 * half_rows : 3 * half_rows]
-        arrival = jnp.sum(jnp.where(from_source, arrival, 0.0), axis=0, keepdims=True)
-        mask = jnp.where(from_source, looked_up[3 * half_rows :], 0.0)
-        mask = jnp.sum(mask, axis=0, keepdims=True)
+        arrival = found_ref[pl.ds(step, 1), :]
+        mask = found_ref[pl.ds(half_rows + step, 1), :]
         residual = (
             own_terms[pl.ds(half_rows + step, 1), :]
             * mask
@@ -710,10 +743,28 @@
     mine = lax.dynamic_update_slice(mine, done, (0, payload_rows - 1, 0))
     other = other_core(mine)
 
+    id_rows, found, own_terms = pl.pallas_call(
+        lookup_kernel,
+        out_shape=(
+            shape((2 * slab_count, LANES), jnp.int32),
+            shape((slab_count, 2 * span)),
+            shape((slab_count, 2 * span)),
+        ),
+        in_specs=smem(1) + vmem(1) + anywhere(2),
+        out_specs=vmem(3),
+        scratch_shapes=[
+            pltpu.VMEM((4, region_events), F32),
+            pltpu.VMEM((station_count, region_events), jnp.int32),
+            pltpu.SemaphoreType.DMA((2,)),
+        ],
+        compiler_params=params(16),
+        cost_estimate=pl.CostEstimate(flops=10**9, bytes_accessed=10**7, transcendentals=0),
+        name="lookup",
+    )(stations, mine, locations, masks)
     results = pl.pallas_call(
         task_kernel,
         out_shape=shape((slab_count, 2, LANES)),
-        in_specs=smem(1) + vmem(4) + anywhere(2),
+        in_specs=vmem(7),
         out_specs=vmem(1)[0],
         scratch_shapes=[
             pltpu.VMEM((region_events * 8, LANES), F32),
@@ -721,18 +772,14 @@
             pltpu.VMEM((2 * span * 4, LANES), F32),
             pltpu.VMEM((2 * span, COMPONENTS * samples), BF16),
             pltpu.VMEM((2 * span, COMPONENTS * samples), BF16),
-            pltpu.VMEM((2 * slab_count, LANES), jnp.int32),
             pltpu.VMEM((slab_count // 2, 2 * span), F32),
-            pltpu.VMEM((slab_count, 2 * span), F32),
-            pltpu.VMEM((4, region_events), F32),
-            pltpu.VMEM((station_count, region_events), jnp.int32),
             pltpu.SMEM((2 * slab_count, LANES), jnp.int32),
-            pltpu.SemaphoreType.DMA((3,)),
+            pltpu.SemaphoreType.DMA,
         ],
         compiler_params=params(26),
         cost_estimate=pl.CostEstimate(flops=10**10, bytes_accessed=10**7, transcendentals=10**7),
         name="task",
-    )(stations, mine, other, inverse, values, locations, masks)
+    )(id_rows, found, own_terms, mine, other, inverse, values)
     back = lax.all_to_all(results, "slab", 0, 0, tiled=True)
     lag_home, last, sums, direction = pl.pallas_call(
         gather_kernel,

time: 80.1 us -> 79.7 us (level)
  waiting for transfers between devices: 10.7 us -> 8.58 us
  Pallas kernels: 36.8 us -> 38.4 us
    pallas_call x0 -> x1, Pallas kernels: none -> 2.29 us  [per_device(): pl.pallas_call(lookup_kernel, out_shape=(shape((2 * slab_count, LANES), j...]
    ppermute x5, waiting for transfers between devices: 2.11 us -> 0.1 us  [other_core(): lax.ppermute(block, 'region', [(i, i + 1 - 2 * (i % 2)) for i in range(co...]
  transfers between devices with their start and end apart: 9 -> 9, of which waited for: 5 -> 4; matrix products, arithmetic and copies ran while one was open for 1% -> 1% of each run, Pallas kernels for 23% -> 26%
where the time goes in v4:
time: 79.7 us; the launch traced here: 79.3 us
  Pallas kernels  38.4 us (48%)
  starting transfers between devices  30.7 us (39%)
  waiting for transfers between devices  8.58 us (11%)
  local copies, waits for them, and re-layouts  0.85 us (1%)
  between operations  0.81 us (1%)
    pallas_call x1, Pallas kernels, per_device(): pl.pallas_call(home_kernel, out_shape=(shape((events, width)), shape((sta...  17.5 us
    pallas_call x1, Pallas kernels, per_device(): pl.pallas_call(task_kernel, out_shape=shape((slab_count, 2, LANES)), in_s...  12.2 us
    all_to_all x1, starting transfers between devices, per_device(): mine = lax.all_to_all(payload, 'slab', 0, 0, tiled=True)  10.7 us
    ppermute x5, starting transfers between devices, other_core(): lax.ppermute(block, 'region', [(i, i + 1 - 2 * (i % 2)) for i in range(co...  9.94 us
    all_to_all x1, starting transfers between devices, per_device(): back = lax.all_to_all(results, 'slab', 0, 0, tiled=True)  5.1 us
    all_to_all x1, waiting for transfers between devices, per_device(): back = lax.all_to_all(results, 'slab', 0, 0, tiled=True)  5 us
    ppermute x2, starting transfers between devices, other_chip(): lax.ppermute(block, 'region', [p for i in odd for p in ((i, i + 1), (i +...  4.97 us
    pallas_call x1, Pallas kernels, per_device(): pl.pallas_call(payload_kernel, out_shape=(shape((slab_count, payload_rows...  4.18 us
  transfers between devices with their start and end apart: 9, of which 4 were waited for; matrix products, arithmetic and copies ran while one was open for 1% of the time, Pallas kernels for 26%

profile of v4, /device:TPU:1, one launch (start us, length us, event | category | flops | bytes accessed | tf_op | source)
XLA Modules:
  0.0 79.3 jit_solution(1604621861965319442)
XLA Ops:
  0.6 4.2 %payload.1 = (bf16[32,104,128]{2,1,0:T(8,128)(2,1)}, bf16[16,104,128]{2,1,0:T(8,128)(2,1)}, bf16[64,4,16,128]{3,2,1,0:T(8,128)(2,1)}) custom-call(bf16[3072,128]{1,0:T(8,128)(2,1)} %bitcast.5, bf16[128,128]{1,0:T(8,128)(2,1)} %constant.35.clone.table_ref, s32[32,64]{1,0:T(8,128)} %bitcast.2), custom_call_target="tpu_custom_call" | custom-call | tf_op jit(solution)/shard_map/payload/pallas_call | solution.py:684
  4.8 3.2 %collective-permute-start = (bf16[16,104,128]{2,1,0:T(8,128)(2,1)}, bf16[16,104,128]{2,1,0:T(8,128)(2,1)S(1)}, u32[]{:S(2)}, u32[]{:S(2)}) collective-permute-start(bf16[16,104,128]{2,1,0:T(8,128)(2,1)} %get-tuple-element.18), channel_id=1, source_target_pairs={{0,32},{32,0},{64,96},{96,64},{128,160},{160,128},{192,224},{224,1... | collective-permute-start | bytes 1277960 | tf_op jit(solution)/shard_map/ppermute | solution.py:659
  8.0 1.9 %collective-permute-start.2 = (bf16[64,4,16,128]{3,2,1,0:T(8,128)(2,1)}, bf16[64,4,16,128]{3,2,1,0:T(8,128)(2,1)}, u32[]{:S(2)}, u32[]{:S(2)}) collective-permute-start(bf16[64,4,16,128]{3,2,1,0:T(8,128)(2,1)} %get-tuple-element.19.own_ref), channel_id=1, source_target_pairs={{32,64},{64,32},{96,128},{128,96},{160,192},{192,160},{33,65},{65,... | collective-permute-start | bytes 3145736 | tf_op jit(solution)/shard_map/ppermute | solution.py:664
  10.0 0.1 collective-permute-start.1
  10.1 0.0 collective-permute-done
  10.1 0.0 copy-start.2
  10.1 0.8 %constant_dynamic-update-slice_fusion = bf16[32,104,128]{2,1,0:T(8,128)(2,1)} fusion(bf16[32,104,128]{2,1,0:T(8,128)(2,1)} %get-tuple-element.17, bf16[16,104,128]{2,1,0:T(8,128)(2,1)S(1)} %collective-permute-done, s32[]{:T(128)S(6)} %select_n.11), kind=kLoop, calls=%fused_computation | loop fusion | bytes 851972 | tf_op jit(solution)/shard_map/dynamic_update_slice | solution.py:697
  10.9 0.0 copy-start
  10.9 0.0 copy-start.1
  10.9 0.0 copy-start.3
  10.9 0.0 copy-start.4
  10.9 0.0 copy-start.5
  10.9 0.0 copy-start.6
  10.9 10.7 %all-to-all-start = ((bf16[32,104,128]{2,1,0:T(8,128)(2,1)}), bf16[32,104,128]{2,1,0:T(8,128)(2,1)S(1)}, u32[]{:S(2)}, u32[]{:S(2)}) async-start(bf16[32,104,128]{2,1,0:T(8,128)(2,1)} %constant_dynamic-update-slice_fusion), calls=%async_computation | async-start | bytes 1703936 | tf_op jit(solution)/shard_map/all_to_all | solution.py:700
  21.6 2.8 %collective-permute-done.2.x_ref = bf16[64,4,16,128]{3,2,1,0:T(8,128)(2,1)} collective-permute-done((bf16[64,4,16,128]{3,2,1,0:T(8,128)(2,1)}, bf16[64,4,16,128]{3,2,1,0:T(8,128)(2,1)}, u32[]{:S(2)}, u32[]{:S(2)}) %collective-permute-start.2) | collective-permute-done | bytes 1048608 | tf_op jit(solution)/shard_map/ppermute | solution.py:664
  24.5 0.0 collective-permute-done.1.core_ref
  24.5 0.0 copy-done.2
  24.5 0.0 copy-done
  24.5 0.0 copy-done.1
  24.5 0.0 copy-done.3
  24.5 0.0 copy-done.4
  24.5 0.0 copy-done.5
  24.5 0.0 copy-done.6
  24.5 17.5 %home.1 = (f32[64,416]{1,0:T(8,128)S(1)}, f32[16,64]{1,0:T(8,128)S(1)}, f32[16,64]{1,0:T(8,128)S(1)}, f32[16,64]{1,0:T(8,128)S(1)}, bf16[1,1,128]{2,1,0:T(2,128)(2,1)S(1)}) custom-call(s32[32,64]{1,0:T(8,128)S(1)} %bitcast.3, s32[32,64]{1,0:T(8,128)S(1)} %bitcast.4, f32[3,16]{1,0:T(4,128)S(1)} %copy-done.4, bf16[384,128]{1,0:T(8,128)(2,1)S(1)} %copy-done.5, ...), custom_call_target="tpu_custom_call" | custom-call | flops 10000000000 | bytes 10000000 | tf_op jit(solution)/shard_map/home/pallas_call | solution.py:706
  42.0 0.7 all-to-all-done
  42.7 4.2 %collective-permute-start.3 = (bf16[32,104,128]{2,1,0:T(8,128)(2,1)S(1)}, bf16[32,104,128]{2,1,0:T(8,128)(2,1)S(1)}, u32[]{:S(2)}, u32[]{:S(2)}) collective-permute-start(bf16[32,104,128]{2,1,0:T(8,128)(2,1)S(1)} %dynamic_update_slice.7.mine_ref), channel_id=1, source_target_pairs={{0,32},{32,0},{64,96},{96,64},{128,160},{160,128},{192,224},{224,1... | collective-permute-start | bytes 2555912 | tf_op jit(solution)/shard_map/ppermute | solution.py:659
  46.9 2.3 %lookup.1 = (s32[64,128]{1,0:T(8,128)S(1)}, f32[32,384]{1,0:T(8,128)S(1)}, f32[32,384]{1,0:T(8,128)S(1)}) custom-call(f32[3,16]{1,0:T(4,128)S(1)} %copy-done.4, bf16[32,104,128]{2,1,0:T(8,128)(2,1)S(1)} %dynamic_update_slice.7.mine_ref, f32[4,16384]{1,0:T(4,128)S(1)} %copy-done.3, s32[16,16384]{1,0:T(8,128)S(1)} %copy-done.1), custom_call_target="tpu_custom_call" | custom-call | flops 1000000000 | bytes 10000000 | tf_op jit(solution)/shard_map/lookup/pallas_call | solution.py:746
  49.2 0.0 collective-permute-done.3.other_ref
  49.2 12.2 %task.1.order_ref = f32[32,2,128]{2,1,0:T(2,128)} custom-call(s32[64,128]{1,0:T(8,128)S(1)} %get-tuple-element.21.id_rows, f32[32,384]{1,0:T(8,128)S(1)} %get-tuple-element.22.found_ref, f32[32,384]{1,0:T(8,128)S(1)} %get-tuple-element.23.own_terms, bf16[32,104,128]{2,1,0:T(8,128)(2,1)S(1)} %dynamic_update_slice.7.mine_ref, ...), custom_call_target="tpu_custom_call" | custom-call | flops 10000000000 | bytes 10000000 | tf_op jit(solution)/shard_map/task/pallas_call | solution.py:764
  61.4 5.1 %all-to-all-start.1 = ((f32[32,2,128]{2,1,0:T(2,128)}), f32[32,2,128]{2,1,0:T(2,128)S(1)}, u32[]{:S(2)}, u32[]{:S(2)}) async-start(f32[32,2,128]{2,1,0:T(2,128)} %task.1.order_ref), calls=%async_computation.1 | async-start | bytes 65536 | tf_op jit(solution)/shard_map/all_to_all | solution.py:783
  66.6 0.7 collective-permute-start.5
  67.2 3.1 %collective-permute-start.6 = (f32[16,64]{1,0:T(8,128)S(1)}, f32[16,64]{1,0:T(8,128)S(1)}, u32[]{:S(2)}, u32[]{:S(2)}) collective-permute-start(f32[16,64]{1,0:T(8,128)S(1)} %get-tuple-element.27), channel_id=1, source_target_pairs={{32,64},{64,32},{96,128},{128,96},{160,192},{192,160},{33,65},{65,... | collective-permute-start | bytes 12296 | tf_op jit(solution)/shard_map/ppermute | solution.py:664
  70.3 5.0 %all-to-all-done.1.kept_ref = f32[32,2,128]{2,1,0:T(2,128)S(1)} async-done(((f32[32,2,128]{2,1,0:T(2,128)}), f32[32,2,128]{2,1,0:T(2,128)S(1)}, u32[]{:S(2)}, u32[]{:S(2)}) %all-to-all-start.1) | async-done | bytes 32800 | tf_op jit(solution)/shard_map/all_to_all | solution.py:783
  75.3 1.7 %collective-permute-start.4 = (f32[32,2,128]{2,1,0:T(2,128)S(1)}, f32[32,2,128]{2,1,0:T(2,128)S(1)}, u32[]{:S(2)}, u32[]{:S(2)}) collective-permute-start(f32[32,2,128]{2,1,0:T(2,128)S(1)} %all-to-all-done.1.kept_ref), channel_id=1, source_target_pairs={{0,32},{32,0},{64,96},{96,64},{128,160},{160,128},{192,224},{224,1... | collective-permute-start | bytes 98312 | tf_op jit(solution)/shard_map/ppermute | solution.py:659
  77.0 0.0 collective-permute-done.5.core_ref
  77.0 0.0 collective-permute-done.6.x_ref
  77.0 0.8 gather.1
  77.8 0.1 collective-permute-done.4.got_ref
  77.9 1.4 %final.1 = (f32[64,512]{1,0:T(8,128)}, f32[4,64]{1,0:T(4,128)}) custom-call(f32[32,2,128]{2,1,0:T(2,128)S(1)} %all-to-all-done.1.kept_ref, f32[32,2,128]{2,1,0:T(2,128)S(1)} %collective-permute-done.4.got_ref, f32[64,128]{1,0:T(8,128)S(1)} %get-tuple-element.28.last_ref, f32[16,64]{1,0:T(8,128)S(1)} %get-tuple-element.29.sums_ref, ...), custom_call_target="tpu_custom_call", output_to_operand_aliasing={{0}: (5, {})} | custom-call | tf_op jit(solution)/shard_map/final/pallas_call | solution.py:799
  (1 shorter events, 0.0 us)
Async XLA Ops:
  4.8 5.3 %collective-permute-start = (bf16[16,104,128]{2,1,0:T(8,128)(2,1)}, bf16[16,104,128]{2,1,0:T(8,128)(2,1)S(1)}, u32[]{:S(2)}, u32[]{:S(2)}) collective-permute-start(bf16[16,104,128]{2,1,0:T(8,128)(2,1)} %get-tuple-element.18), channel_id=1, source_target_pairs={{0,32},{32,0},{64,96},{96,64},{128,160},{160,128},{192,224},{224,1... | collective-permute-start | bytes 1277960 | tf_op jit(solution)/shard_map/ppermute | solution.py:659
  8.0 16.4 %collective-permute-start.2 = (bf16[64,4,16,128]{3,2,1,0:T(8,128)(2,1)}, bf16[64,4,16,128]{3,2,1,0:T(8,128)(2,1)}, u32[]{:S(2)}, u32[]{:S(2)}) collective-permute-start(bf16[64,4,16,128]{3,2,1,0:T(8,128)(2,1)} %get-tuple-element.19.own_ref), channel_id=1, source_target_pairs={{32,64},{64,32},{96,128},{128,96},{160,192},{192,160},{33,65},{65,... | collective-permute-start | bytes 3145736 | tf_op jit(solution)/shard_map/ppermute | solution.py:664
  10.0 14.5 %collective-permute-start.1 = (bf16[64,4,16,128]{3,2,1,0:T(8,128)(2,1)}, bf16[64,4,16,128]{3,2,1,0:T(8,128)(2,1)}, u32[]{:S(2)}, u32[]{:S(2)}) collective-permute-start(bf16[64,4,16,128]{3,2,1,0:T(8,128)(2,1)} %get-tuple-element.19.own_ref), channel_id=1, source_target_pairs={{0,32},{32,0},{64,96},{96,64},{128,160},{160,128},{192,224},{224,1... | collective-permute-start | bytes 3145736 | tf_op jit(solution)/shard_map/ppermute | solution.py:659
  10.1 14.4 %copy-start.2 = (bf16[64,4,16,128]{3,2,1,0:T(8,128)(2,1)S(1)}, bf16[64,4,16,128]{3,2,1,0:T(8,128)(2,1)}, u32[]{:S(2)}) copy-start(bf16[64,4,16,128]{3,2,1,0:T(8,128)(2,1)} %get-tuple-element.19.own_ref) | copy-start | bytes 3145732
  10.9 13.6 %copy-start = (s32[64,32]{0,1:T(8,128)S(1)}, s32[64,32]{0,1:T(8,128)}, u32[]{:S(2)}) copy-start(s32[64,32]{0,1:T(8,128)} %param.9) | copy-start | bytes 24580
  10.9 13.6 %copy-start.1 = (s32[16,16384]{1,0:T(8,128)S(1)}, s32[16,16384]{1,0:T(8,128)}, u32[]{:S(2)}) copy-start(s32[16,16384]{1,0:T(8,128)} %masks_ref.3) | copy-start | bytes 3145732
  10.9 13.6 %copy-start.3 = (f32[4,16384]{1,0:T(4,128)S(1)}, f32[4,16384]{1,0:T(4,128)}, u32[]{:S(2)}) copy-start(f32[4,16384]{1,0:T(4,128)} %locations_ref.5) | copy-start | bytes 786436
  10.9 13.6 %copy-start.4 = (f32[3,16]{1,0:T(4,128)S(1)}, f32[3,16]{1,0:T(4,128)}, u32[]{:S(2)}) copy-start(f32[3,16]{1,0:T(4,128)} %stations_ref.5) | copy-start | bytes 580
  10.9 13.6 %copy-start.5 = (bf16[384,128]{1,0:T(8,128)(2,1)S(1)}, bf16[384,128]{1,0:T(8,128)(2,1)}, u32[]{:S(2)}) copy-start(bf16[384,128]{1,0:T(8,128)(2,1)} %constant.33.clone.inverse_ref) | copy-start | bytes 294916
  10.9 13.6 %copy-start.6 = (f32[128,128]{1,0:T(8,128)S(1)}, f32[128,128]{1,0:T(8,128)}, u32[]{:S(2)}) copy-start(f32[128,128]{1,0:T(8,128)} %constant.34.clone.values_ref) | copy-start | bytes 196612
  10.9 31.7 %all-to-all-start = ((bf16[32,104,128]{2,1,0:T(8,128)(2,1)}), bf16[32,104,128]{2,1,0:T(8,128)(2,1)S(1)}, u32[]{:S(2)}, u32[]{:S(2)}) async-start(bf16[32,104,128]{2,1,0:T(8,128)(2,1)} %constant_dynamic-update-slice_fusion), calls=%async_computation | async-start | bytes 1703936 | tf_op jit(solution)/shard_map/all_to_all | solution.py:700
  42.7 6.5 %collective-permute-start.3 = (bf16[32,104,128]{2,1,0:T(8,128)(2,1)S(1)}, bf16[32,104,128]{2,1,0:T(8,128)(2,1)S(1)}, u32[]{:S(2)}, u32[]{:S(2)}) collective-permute-start(bf16[32,104,128]{2,1,0:T(8,128)(2,1)S(1)} %dynamic_update_slice.7.mine_ref), channel_id=1, source_target_pairs={{0,32},{32,0},{64,96},{96,64},{128,160},{160,128},{192,224},{224,1... | collective-permute-start | bytes 2555912 | tf_op jit(solution)/shard_map/ppermute | solution.py:659
  61.4 13.9 %all-to-all-start.1 = ((f32[32,2,128]{2,1,0:T(2,128)}), f32[32,2,128]{2,1,0:T(2,128)S(1)}, u32[]{:S(2)}, u32[]{:S(2)}) async-start(f32[32,2,128]{2,1,0:T(2,128)} %task.1.order_ref), calls=%async_computation.1 | async-start | bytes 65536 | tf_op jit(solution)/shard_map/all_to_all | solution.py:783
  66.6 10.5 %collective-permute-start.5 = (f32[16,64]{1,0:T(8,128)S(1)}, f32[16,64]{1,0:T(8,128)S(1)}, u32[]{:S(2)}, u32[]{:S(2)}) collective-permute-start(f32[16,64]{1,0:T(8,128)S(1)} %get-tuple-element.26), channel_id=1, source_target_pairs={{0,32},{32,0},{64,96},{96,64},{128,160},{160,128},{192,224},{224,1... | collective-permute-start | bytes 12296 | tf_op jit(solution)/shard_map/ppermute | solution.py:659
  67.2 9.8 %collective-permute-start.6 = (f32[16,64]{1,0:T(8,128)S(1)}, f32[16,64]{1,0:T(8,128)S(1)}, u32[]{:S(2)}, u32[]{:S(2)}) collective-permute-start(f32[16,64]{1,0:T(8,128)S(1)} %get-tuple-element.27), channel_id=1, source_target_pairs={{32,64},{64,32},{96,128},{128,96},{160,192},{192,160},{33,65},{65,... | collective-permute-start | bytes 12296 | tf_op jit(solution)/shard_map/ppermute | solution.py:664
  75.3 2.6 %collective-permute-start.4 = (f32[32,2,128]{2,1,0:T(2,128)S(1)}, f32[32,2,128]{2,1,0:T(2,128)S(1)}, u32[]{:S(2)}, u32[]{:S(2)}) collective-permute-start(f32[32,2,128]{2,1,0:T(2,128)S(1)} %all-to-all-done.1.kept_ref), channel_id=1, source_target_pairs={{0,32},{32,0},{64,96},{96,64},{128,160},{160,128},{192,224},{224,1... | collective-permute-start | bytes 98312 | tf_op jit(solution)/shard_map/ppermute | solution.py:659

commit v5 on v4

--- a/solution.py
+++ b/solution.py
@@ -57,12 +57,6 @@
     return np.concatenate([real, real, imag, imag, table], axis=0)
 
 
-def lag_values(samples):
-    lag_ids = np.arange(samples)
-    values = np.where(lag_ids < samples // 2, lag_ids, lag_ids - samples)
-    return np.broadcast_to(values[:, None], (samples, LANES)).astype(np.float32)
-
-
 def arrange(first, second):
     half = first.shape[-1] // 2
     lane = lax.broadcasted_iota(jnp.int32, first.shape, first.ndim - 1)
@@ -95,24 +89,40 @@
     )
 
 
-def soft_lags(corr, values):
-    corr = corr.T
+def soft_lags(corr):
     top = jnp.max(corr, axis=0, keepdims=True)
     weights = jnp.exp2((corr - top) * EXPONENT_SCALE)
-    total = jnp.sum(weights, axis=0, keepdims=True)
-    moment = jnp.sum(weights * values, axis=0, keepdims=True)
-    return moment / total
-
-
-def all_soft_lags(crossed_ref, inverse_ref, values_ref, block):
-    inverse, values = inverse_ref[...], values_ref[...]
+    groups = [weights[k : k + 8] for k in range(0, weights.shape[0], 8)]
+    half = len(groups) // 2
+    after = groups[half - 1]
+    ahead = after
+    for k in range(half - 2, 0, -1):
+        after = after + groups[k]
+        ahead = ahead + after
+    after = after + groups[0]
+    before = groups[half]
+    behind = before
+    for k in range(half + 1, len(groups)):
+        before = before + groups[k]
+        behind = behind + before
+    total = after + before
+    row = lax.broadcasted_iota(jnp.int32, total.shape, 0).astype(F32)
+    moment = jnp.sum((ahead - behind) * 8.0 + row * total, axis=0, keepdims=True)
+    return moment / jnp.sum(total, axis=0, keepdims=True)
+
+
+def all_soft_lags(crossed_ref, inverse_ref):
+    corr = jnp.dot(crossed_ref[...], inverse_ref[...], preferred_element_type=F32)
+    lags = [soft_lags(corr[k : k + LANES].T) for k in range(0, corr.shape[0], LANES)]
+    return jnp.concatenate(lags, axis=1)
+
+
+def soft_lags_by_block(crossed_ref, turned_ref):
     lags = []
-    for start in range(0, crossed_ref.shape[0], block):
-        corr = jnp.dot(
-            crossed_ref[start : start + block, :], inverse, preferred_element_type=F32
-        )
-        for k in range(0, block, LANES):
-            lags.append(soft_lags(corr[k : k + LANES], values))
+    for k in range(0, crossed_ref.shape[0], LANES):
+        rows = crossed_ref[k : k + LANES, :]
+        corr = lax.dot_general(turned_ref[...], rows, BY_LAST, preferred_element_type=F32)
+        lags.append(soft_lags(corr))
     return jnp.concatenate(lags, axis=1)
 
 
@@ -236,7 +246,6 @@
     id_ref,
     stations_ref,
     inverse_ref,
-    values_ref,
     core_ref,
     own_ref,
     x_ref,
@@ -306,7 +315,7 @@
                 put_crossed(rows_ref, slice(start, start + stations), own, partner)
 
     def finish_batch(batch, rows_ref):
-        lags = all_soft_lags(rows_ref, inverse_ref, values_ref, BATCH * width)
+        lags = all_soft_lags(rows_ref, inverse_ref)
         for b in range(BATCH):
             lag_ref[pl.ds(batch * BATCH + b, 1), :] = lags[:, b * width : (b + 1) * width]
 
@@ -442,8 +451,7 @@
     own_terms,
     mine_ref,
     other_ref,
-    inverse_ref,
-    values_ref,
+    turned_ref,
     out_ref,
     table,
     fetched_even,
@@ -477,7 +485,7 @@
                 table[pl.ds(base + 4 + k, part, stride=8), :] = values_k
         return carry
 
-    lax.fori_loop(0, sources, fill, 0, unroll=4)
+    lax.fori_loop(0, sources, fill, 0, unroll=8)
     id_copy.wait()
     lane = lax.broadcasted_iota(jnp.int32, (LANES, width), 1)
     event_rows = lax.broadcasted_iota(jnp.int32, (LANES, width), 0)
@@ -514,7 +522,7 @@
                 put_crossed(into, slice(start, start + part), own, partner)
 
     def finish(step, rows_ref, sums):
-        lag = all_soft_lags(rows_ref, inverse_ref, values_ref, LANES)
+        lag = soft_lags_by_block(rows_ref, turned_ref)
         for u in range(2):
             rest = lag[:, u * span + LANES : (u + 1) * span]
             rest = jnp.concatenate([rest, jnp.zeros((1, LANES - rest.shape[1]), F32)], axis=1)
@@ -674,7 +682,7 @@
     part = events // 2
     span = K_REGION * part
     inverse = jnp.asarray(inverse_rows(samples))
-    values = jnp.asarray(lag_values(samples))
+    turned = jnp.asarray(np.ascontiguousarray(inverse_rows(samples).T))
     wave_rows = waveforms.reshape(-1, samples)
     table = jnp.asarray(forward_table(samples))
     id_columns = neighbours.T
@@ -712,7 +720,7 @@
             shape((station_count, events)),
             shape((1, 1, LANES), BF16),
         ),
-        in_specs=smem(1) + vmem(4) + anywhere(5),
+        in_specs=smem(1) + vmem(3) + anywhere(5),
         out_specs=vmem(5),
         scratch_shapes=[
             pltpu.VMEM((3 * events, *by_event_shape[1:]), BF16),
@@ -731,7 +739,6 @@
         id_columns,
         stations,
         inverse,
-        values,
         core_spec,
         by_event,
         x_spec,
@@ -764,7 +771,7 @@
     results = pl.pallas_call(
         task_kernel,
         out_shape=shape((slab_count, 2, LANES)),
-        in_specs=vmem(7),
+        in_specs=vmem(6),
         out_specs=vmem(1)[0],
         scratch_shapes=[
             pltpu.VMEM((region_events * 8, LANES), F32),
@@ -779,7 +786,7 @@
         compiler_params=params(26),
         cost_estimate=pl.CostEstimate(flops=10**10, bytes_accessed=10**7, transcendentals=10**7),
         name="task",
-    )(id_rows, found, own_terms, mine, other, inverse, values)
+    )(id_rows, found, own_terms, mine, other, turned)
     back = lax.all_to_all(results, "slab", 0, 0, tiled=True)
     lag_home, last, sums, direction = pl.pallas_call(
         gather_kernel,

time: 79.7 us -> 78.9 us (0.990)
  Pallas kernels: 38.4 us -> 37.5 us
where the time goes in v5:
time: 78.9 us; the launch traced here: 78.5 us
  Pallas kernels  37.5 us (48%)
  starting transfers between devices  30.3 us (38%)
  waiting for transfers between devices  9.16 us (12%)
  local copies, waits for them, and re-layouts  0.85 us (1%)
  between operations  0.8 us (1%)
    pallas_call x1, Pallas kernels, per_device(): pl.pallas_call(home_kernel, out_shape=(shape((events, width)), shape((sta...  17.1 us
    pallas_call x1, Pallas kernels, per_device(): pl.pallas_call(task_kernel, out_shape=shape((slab_count, 2, LANES)), in_s...  11.8 us
    all_to_all x1, starting transfers between devices, per_device(): mine = lax.all_to_all(payload, 'slab', 0, 0, tiled=True)  10.7 us
    ppermute x5, starting transfers between devices, other_core(): lax.ppermute(block, 'region', [(i, i + 1 - 2 * (i % 2)) for i in range(co...  9.41 us
    all_to_all x1, waiting for transfers between devices, per_device(): back = lax.all_to_all(results, 'slab', 0, 0, tiled=True)  5.15 us
    ppermute x2, starting transfers between devices, other_chip(): lax.ppermute(block, 'region', [p for i in odd for p in ((i, i + 1), (i +...  5.09 us
    all_to_all x1, starting transfers between devices, per_device(): back = lax.all_to_all(results, 'slab', 0, 0, tiled=True)  5.06 us
    pallas_call x1, Pallas kernels, per_device(): pl.pallas_call(payload_kernel, out_shape=(shape((slab_count, payload_rows...  4.18 us
  transfers between devices with their start and end apart: 9, of which 4 were waited for; matrix products, arithmetic and copies ran while one was open for 1% of the time, Pallas kernels for 26%

profile of v5, /device:TPU:1, one launch (start us, length us, event | category | flops | bytes accessed | tf_op | source)
XLA Modules:
  0.0 78.5 jit_solution(8061301038116966413)
XLA Ops:
  0.6 4.2 %payload.1 = (bf16[32,104,128]{2,1,0:T(8,128)(2,1)}, bf16[16,104,128]{2,1,0:T(8,128)(2,1)}, bf16[64,4,16,128]{3,2,1,0:T(8,128)(2,1)}) custom-call(bf16[3072,128]{1,0:T(8,128)(2,1)} %bitcast.5, bf16[128,128]{1,0:T(8,128)(2,1)} %constant.35.clone.table_ref, s32[32,64]{1,0:T(8,128)} %bitcast.2), custom_call_target="tpu_custom_call" | custom-call | tf_op jit(solution)/shard_map/payload/pallas_call | solution.py:692
  4.8 3.2 %collective-permute-start = (bf16[16,104,128]{2,1,0:T(8,128)(2,1)}, bf16[16,104,128]{2,1,0:T(8,128)(2,1)S(1)}, u32[]{:S(2)}, u32[]{:S(2)}) collective-permute-start(bf16[16,104,128]{2,1,0:T(8,128)(2,1)} %get-tuple-element.18), channel_id=1, source_target_pairs={{0,32},{32,0},{64,96},{96,64},{128,160},{160,128},{192,224},{224,1... | collective-permute-start | bytes 1277960 | tf_op jit(solution)/shard_map/ppermute | solution.py:667
  8.0 1.9 %collective-permute-start.2 = (bf16[64,4,16,128]{3,2,1,0:T(8,128)(2,1)}, bf16[64,4,16,128]{3,2,1,0:T(8,128)(2,1)}, u32[]{:S(2)}, u32[]{:S(2)}) collective-permute-start(bf16[64,4,16,128]{3,2,1,0:T(8,128)(2,1)} %get-tuple-element.19.own_ref), channel_id=1, source_target_pairs={{32,64},{64,32},{96,128},{128,96},{160,192},{192,160},{33,65},{65,... | collective-permute-start | bytes 3145736 | tf_op jit(solution)/shard_map/ppermute | solution.py:672
  10.0 0.1 collective-permute-start.1
  10.1 0.0 collective-permute-done
  10.1 0.0 copy-start.2
  10.1 0.8 %constant_dynamic-update-slice_fusion = bf16[32,104,128]{2,1,0:T(8,128)(2,1)} fusion(bf16[32,104,128]{2,1,0:T(8,128)(2,1)} %get-tuple-element.17, bf16[16,104,128]{2,1,0:T(8,128)(2,1)S(1)} %collective-permute-done, s32[]{:T(128)S(6)} %select_n.11), kind=kLoop, calls=%fused_computation | loop fusion | bytes 851972 | tf_op jit(solution)/shard_map/dynamic_update_slice | solution.py:705
  10.9 0.0 copy-start
  10.9 0.0 copy-start.1
  10.9 0.0 copy-start.3
  10.9 0.0 copy-start.4
  10.9 0.0 copy-start.6
  10.9 10.7 %all-to-all-start = ((bf16[32,104,128]{2,1,0:T(8,128)(2,1)}), bf16[32,104,128]{2,1,0:T(8,128)(2,1)S(1)}, u32[]{:S(2)}, u32[]{:S(2)}) async-start(bf16[32,104,128]{2,1,0:T(8,128)(2,1)} %constant_dynamic-update-slice_fusion), calls=%async_computation | async-start | bytes 1703936 | tf_op jit(solution)/shard_map/all_to_all | solution.py:708
  21.6 2.8 %collective-permute-done.2.x_ref = bf16[64,4,16,128]{3,2,1,0:T(8,128)(2,1)} collective-permute-done((bf16[64,4,16,128]{3,2,1,0:T(8,128)(2,1)}, bf16[64,4,16,128]{3,2,1,0:T(8,128)(2,1)}, u32[]{:S(2)}, u32[]{:S(2)}) %collective-permute-start.2) | collective-permute-done | bytes 1048608 | tf_op jit(solution)/shard_map/ppermute | solution.py:672
  24.5 0.0 collective-permute-done.1.core_ref
  24.5 0.0 copy-done.2
  24.5 0.0 copy-done
  24.5 0.0 copy-done.1
  24.5 0.0 copy-done.3
  24.5 0.0 copy-done.4
  24.5 0.0 copy-done.6
  24.5 17.1 %home.1 = (f32[64,416]{1,0:T(8,128)S(1)}, f32[16,64]{1,0:T(8,128)S(1)}, f32[16,64]{1,0:T(8,128)S(1)}, f32[16,64]{1,0:T(8,128)S(1)}, bf16[1,1,128]{2,1,0:T(2,128)(2,1)S(1)}) custom-call(s32[32,64]{1,0:T(8,128)S(1)} %bitcast.3, s32[32,64]{1,0:T(8,128)S(1)} %bitcast.4, f32[3,16]{1,0:T(4,128)S(1)} %copy-done.4, bf16[384,128]{1,0:T(8,128)(2,1)S(1)} %copy-done.6, ...), custom_call_target="tpu_custom_call" | custom-call | flops 10000000000 | bytes 10000000 | tf_op jit(solution)/shard_map/home/pallas_call | solution.py:714
  41.6 1.1 %all-to-all-done = bf16[32,104,128]{2,1,0:T(8,128)(2,1)S(1)} async-done(((bf16[32,104,128]{2,1,0:T(8,128)(2,1)}), bf16[32,104,128]{2,1,0:T(8,128)(2,1)S(1)}, u32[]{:S(2)}, u32[]{:S(2)}) %all-to-all-start) | async-done | bytes 852000 | tf_op jit(solution)/shard_map/all_to_all | solution.py:708
  42.7 0.0 copy-start.5
  42.7 4.2 %collective-permute-start.3 = (bf16[32,104,128]{2,1,0:T(8,128)(2,1)S(1)}, bf16[32,104,128]{2,1,0:T(8,128)(2,1)S(1)}, u32[]{:S(2)}, u32[]{:S(2)}) collective-permute-start(bf16[32,104,128]{2,1,0:T(8,128)(2,1)S(1)} %dynamic_update_slice.7.mine_ref), channel_id=1, source_target_pairs={{0,32},{32,0},{64,96},{96,64},{128,160},{160,128},{192,224},{224,1... | collective-permute-start | bytes 2555912 | tf_op jit(solution)/shard_map/ppermute | solution.py:667
  46.9 2.3 %lookup.1 = (s32[64,128]{1,0:T(8,128)S(1)}, f32[32,384]{1,0:T(8,128)S(1)}, f32[32,384]{1,0:T(8,128)S(1)}) custom-call(f32[3,16]{1,0:T(4,128)S(1)} %copy-done.4, bf16[32,104,128]{2,1,0:T(8,128)(2,1)S(1)} %dynamic_update_slice.7.mine_ref, f32[4,16384]{1,0:T(4,128)S(1)} %copy-done.3, s32[16,16384]{1,0:T(8,128)S(1)} %copy-done.1), custom_call_target="tpu_custom_call" | custom-call | flops 1000000000 | bytes 10000000 | tf_op jit(solution)/shard_map/lookup/pallas_call | solution.py:753
  49.2 0.0 collective-permute-done.3.other_ref
  49.2 0.0 copy-done.5
  49.2 11.8 %task.1.order_ref = f32[32,2,128]{2,1,0:T(2,128)} custom-call(s32[64,128]{1,0:T(8,128)S(1)} %get-tuple-element.21.id_rows, f32[32,384]{1,0:T(8,128)S(1)} %get-tuple-element.22.found_ref, f32[32,384]{1,0:T(8,128)S(1)} %get-tuple-element.23.own_terms, bf16[32,104,128]{2,1,0:T(8,128)(2,1)S(1)} %dynamic_update_slice.7.mine_ref, ...), custom_call_target="tpu_custom_call" | custom-call | flops 10000000000 | bytes 10000000 | tf_op jit(solution)/shard_map/task/pallas_call | solution.py:771
  61.0 5.1 %all-to-all-start.1 = ((f32[32,2,128]{2,1,0:T(2,128)}), f32[32,2,128]{2,1,0:T(2,128)S(1)}, u32[]{:S(2)}, u32[]{:S(2)}) async-start(f32[32,2,128]{2,1,0:T(2,128)} %task.1.order_ref), calls=%async_computation.1 | async-start | bytes 65536 | tf_op jit(solution)/shard_map/all_to_all | solution.py:790
  66.1 0.4 collective-permute-start.5
  66.5 3.2 %collective-permute-start.6 = (f32[16,64]{1,0:T(8,128)S(1)}, f32[16,64]{1,0:T(8,128)S(1)}, u32[]{:S(2)}, u32[]{:S(2)}) collective-permute-start(f32[16,64]{1,0:T(8,128)S(1)} %get-tuple-element.27), channel_id=1, source_target_pairs={{32,64},{64,32},{96,128},{128,96},{160,192},{192,160},{33,65},{65,... | collective-permute-start | bytes 12296 | tf_op jit(solution)/shard_map/ppermute | solution.py:672
  69.7 5.1 %all-to-all-done.1.kept_ref = f32[32,2,128]{2,1,0:T(2,128)S(1)} async-done(((f32[32,2,128]{2,1,0:T(2,128)}), f32[32,2,128]{2,1,0:T(2,128)S(1)}, u32[]{:S(2)}, u32[]{:S(2)}) %all-to-all-start.1) | async-done | bytes 32800 | tf_op jit(solution)/shard_map/all_to_all | solution.py:790
  74.8 1.5 %collective-permute-start.4 = (f32[32,2,128]{2,1,0:T(2,128)S(1)}, f32[32,2,128]{2,1,0:T(2,128)S(1)}, u32[]{:S(2)}, u32[]{:S(2)}) collective-permute-start(f32[32,2,128]{2,1,0:T(2,128)S(1)} %all-to-all-done.1.kept_ref), channel_id=1, source_target_pairs={{0,32},{32,0},{64,96},{96,64},{128,160},{160,128},{192,224},{224,1... | collective-permute-start | bytes 98312 | tf_op jit(solution)/shard_map/ppermute | solution.py:667
  76.3 0.0 collective-permute-done.5.core_ref
  76.3 0.0 collective-permute-done.6.x_ref
  76.3 0.8 gather.1
  77.0 0.1 collective-permute-done.4.got_ref
  77.1 1.4 %final.1 = (f32[64,512]{1,0:T(8,128)}, f32[4,64]{1,0:T(4,128)}) custom-call(f32[32,2,128]{2,1,0:T(2,128)S(1)} %all-to-all-done.1.kept_ref, f32[32,2,128]{2,1,0:T(2,128)S(1)} %collective-permute-done.4.got_ref, f32[64,128]{1,0:T(8,128)S(1)} %get-tuple-element.28.last_ref, f32[16,64]{1,0:T(8,128)S(1)} %get-tuple-element.29.sums_ref, ...), custom_call_target="tpu_custom_call", output_to_operand_aliasing={{0}: (5, {})} | custom-call | tf_op jit(solution)/shard_map/final/pallas_call | solution.py:806
  (1 shorter events, 0.0 us)
Async XLA Ops:
  4.8 5.3 %collective-permute-start = (bf16[16,104,128]{2,1,0:T(8,128)(2,1)}, bf16[16,104,128]{2,1,0:T(8,128)(2,1)S(1)}, u32[]{:S(2)}, u32[]{:S(2)}) collective-permute-start(bf16[16,104,128]{2,1,0:T(8,128)(2,1)} %get-tuple-element.18), channel_id=1, source_target_pairs={{0,32},{32,0},{64,96},{96,64},{128,160},{160,128},{192,224},{224,1... | collective-permute-start | bytes 1277960 | tf_op jit(solution)/shard_map/ppermute | solution.py:667
  8.0 16.4 %collective-permute-start.2 = (bf16[64,4,16,128]{3,2,1,0:T(8,128)(2,1)}, bf16[64,4,16,128]{3,2,1,0:T(8,128)(2,1)}, u32[]{:S(2)}, u32[]{:S(2)}) collective-permute-start(bf16[64,4,16,128]{3,2,1,0:T(8,128)(2,1)} %get-tuple-element.19.own_ref), channel_id=1, source_target_pairs={{32,64},{64,32},{96,128},{128,96},{160,192},{192,160},{33,65},{65,... | collective-permute-start | bytes 3145736 | tf_op jit(solution)/shard_map/ppermute | solution.py:672
  10.0 14.5 %collective-permute-start.1 = (bf16[64,4,16,128]{3,2,1,0:T(8,128)(2,1)}, bf16[64,4,16,128]{3,2,1,0:T(8,128)(2,1)}, u32[]{:S(2)}, u32[]{:S(2)}) collective-permute-start(bf16[64,4,16,128]{3,2,1,0:T(8,128)(2,1)} %get-tuple-element.19.own_ref), channel_id=1, source_target_pairs={{0,32},{32,0},{64,96},{96,64},{128,160},{160,128},{192,224},{224,1... | collective-permute-start | bytes 3145736 | tf_op jit(solution)/shard_map/ppermute | solution.py:667
  10.1 14.4 %copy-start.2 = (bf16[64,4,16,128]{3,2,1,0:T(8,128)(2,1)S(1)}, bf16[64,4,16,128]{3,2,1,0:T(8,128)(2,1)}, u32[]{:S(2)}) copy-start(bf16[64,4,16,128]{3,2,1,0:T(8,128)(2,1)} %get-tuple-element.19.own_ref) | copy-start | bytes 3145732
  10.9 13.6 %copy-start = (s32[64,32]{0,1:T(8,128)S(1)}, s32[64,32]{0,1:T(8,128)}, u32[]{:S(2)}) copy-start(s32[64,32]{0,1:T(8,128)} %param.9) | copy-start | bytes 24580
  10.9 13.6 %copy-start.1 = (s32[16,16384]{1,0:T(8,128)S(1)}, s32[16,16384]{1,0:T(8,128)}, u32[]{:S(2)}) copy-start(s32[16,16384]{1,0:T(8,128)} %masks_ref.3) | copy-start | bytes 3145732
  10.9 13.6 %copy-start.3 = (f32[4,16384]{1,0:T(4,128)S(1)}, f32[4,16384]{1,0:T(4,128)}, u32[]{:S(2)}) copy-start(f32[4,16384]{1,0:T(4,128)} %locations_ref.5) | copy-start | bytes 786436
  10.9 13.6 %copy-start.4 = (f32[3,16]{1,0:T(4,128)S(1)}, f32[3,16]{1,0:T(4,128)}, u32[]{:S(2)}) copy-start(f32[3,16]{1,0:T(4,128)} %stations_ref.5) | copy-start | bytes 580
  10.9 13.6 %copy-start.6 = (bf16[384,128]{1,0:T(8,128)(2,1)S(1)}, bf16[384,128]{1,0:T(8,128)(2,1)}, u32[]{:S(2)}) copy-start(bf16[384,128]{1,0:T(8,128)(2,1)} %constant.33.clone.inverse_ref) | copy-start | bytes 294916
  10.9 31.7 %all-to-all-start = ((bf16[32,104,128]{2,1,0:T(8,128)(2,1)}), bf16[32,104,128]{2,1,0:T(8,128)(2,1)S(1)}, u32[]{:S(2)}, u32[]{:S(2)}) async-start(bf16[32,104,128]{2,1,0:T(8,128)(2,1)} %constant_dynamic-update-slice_fusion), calls=%async_computation | async-start | bytes 1703936 | tf_op jit(solution)/shard_map/all_to_all | solution.py:708
  42.7 6.5 %copy-start.5 = (bf16[128,384]{1,0:T(8,128)(2,1)S(1)}, bf16[128,384]{1,0:T(8,128)(2,1)}, u32[]{:S(2)}) copy-start(bf16[128,384]{1,0:T(8,128)(2,1)} %constant.34.clone.turned_ref) | copy-start | bytes 294916
  42.7 6.5 %collective-permute-start.3 = (bf16[32,104,128]{2,1,0:T(8,128)(2,1)S(1)}, bf16[32,104,128]{2,1,0:T(8,128)(2,1)S(1)}, u32[]{:S(2)}, u32[]{:S(2)}) collective-permute-start(bf16[32,104,128]{2,1,0:T(8,128)(2,1)S(1)} %dynamic_update_slice.7.mine_ref), channel_id=1, source_target_pairs={{0,32},{32,0},{64,96},{96,64},{128,160},{160,128},{192,224},{224,1... | collective-permute-start | bytes 2555912 | tf_op jit(solution)/shard_map/ppermute | solution.py:667
  61.0 13.8 %all-to-all-start.1 = ((f32[32,2,128]{2,1,0:T(2,128)}), f32[32,2,128]{2,1,0:T(2,128)S(1)}, u32[]{:S(2)}, u32[]{:S(2)}) async-start(f32[32,2,128]{2,1,0:T(2,128)} %task.1.order_ref), calls=%async_computation.1 | async-start | bytes 65536 | tf_op jit(solution)/shard_map/all_to_all | solution.py:790
  66.1 10.2 %collective-permute-start.5 = (f32[16,64]{1,0:T(8,128)S(1)}, f32[16,64]{1,0:T(8,128)S(1)}, u32[]{:S(2)}, u32[]{:S(2)}) collective-permute-start(f32[16,64]{1,0:T(8,128)S(1)} %get-tuple-element.26), channel_id=1, source_target_pairs={{0,32},{32,0},{64,96},{96,64},{128,160},{160,128},{192,224},{224,1... | collective-permute-start | bytes 12296 | tf_op jit(solution)/shard_map/ppermute | solution.py:667
  66.5 9.8 %collective-permute-start.6 = (f32[16,64]{1,0:T(8,128)S(1)}, f32[16,64]{1,0:T(8,128)S(1)}, u32[]{:S(2)}, u32[]{:S(2)}) collective-permute-start(f32[16,64]{1,0:T(8,128)S(1)} %get-tuple-element.27), channel_id=1, source_target_pairs={{32,64},{64,32},{96,128},{128,96},{160,192},{192,160},{33,65},{65,... | collective-permute-start | bytes 12296 | tf_op jit(solution)/shard_map/ppermute | solution.py:672
  74.8 2.3 %collective-permute-start.4 = (f32[32,2,128]{2,1,0:T(2,128)S(1)}, f32[32,2,128]{2,1,0:T(2,128)S(1)}, u32[]{:S(2)}, u32[]{:S(2)}) collective-permute-start(f32[32,2,128]{2,1,0:T(2,128)S(1)} %all-to-all-done.1.kept_ref), channel_id=1, source_target_pairs={{0,32},{32,0},{64,96},{96,64},{128,160},{160,128},{192,224},{224,1... | collective-permute-start | bytes 98312 | tf_op jit(solution)/shard_map/ppermute | solution.py:667

commit v6 on v5

--- a/solution.py
+++ b/solution.py
@@ -119,10 +119,9 @@
 
 def soft_lags_by_block(crossed_ref, turned_ref):
     lags = []
+    corr = lax.dot_general(turned_ref[...], crossed_ref[...], BY_LAST, preferred_element_type=F32)
     for k in range(0, crossed_ref.shape[0], LANES):
-        rows = crossed_ref[k : k + LANES, :]
-        corr = lax.dot_general(turned_ref[...], rows, BY_LAST, preferred_element_type=F32)
-        lags.append(soft_lags(corr))
+        lags.append(soft_lags(corr[:, k : k + LANES]))
     return jnp.concatenate(lags, axis=1)
 
 

time: 78.9 us -> 78.6 us (level)
  no operation moved by 1% of the time
where the time goes in v6:
time: 78.6 us; the launch traced here: 78.3 us
  Pallas kernels  37.2 us (47%)
  starting transfers between devices  30.3 us (39%)
  waiting for transfers between devices  9.17 us (12%)
  local copies, waits for them, and re-layouts  0.85 us (1%)
  between operations  0.8 us (1%)
    pallas_call x1, Pallas kernels, per_device(): pl.pallas_call(home_kernel, out_shape=(shape((events, width)), shape((sta...  17.1 us
    pallas_call x1, Pallas kernels, per_device(): pl.pallas_call(task_kernel, out_shape=shape((slab_count, 2, LANES)), in_s...  11.5 us
    all_to_all x1, starting transfers between devices, per_device(): mine = lax.all_to_all(payload, 'slab', 0, 0, tiled=True)  10.7 us
    ppermute x5, starting transfers between devices, other_core(): lax.ppermute(block, 'region', [(i, i + 1 - 2 * (i % 2)) for i in range(co...  9.39 us
    all_to_all x1, waiting for transfers between devices, per_device(): back = lax.all_to_all(results, 'slab', 0, 0, tiled=True)  5.15 us
    ppermute x2, starting transfers between devices, other_chip(): lax.ppermute(block, 'region', [p for i in odd for p in ((i, i + 1), (i +...  5.09 us
    all_to_all x1, starting transfers between devices, per_device(): back = lax.all_to_all(results, 'slab', 0, 0, tiled=True)  5.08 us
    pallas_call x1, Pallas kernels, per_device(): pl.pallas_call(payload_kernel, out_shape=(shape((slab_count, payload_rows...  4.18 us
  transfers between devices with their start and end apart: 9, of which 4 were waited for; matrix products, arithmetic and copies ran while one was open for 1% of the time, Pallas kernels for 26%

profile of v6, /device:TPU:1, one launch (start us, length us, event | category | flops | bytes accessed | tf_op | source)
XLA Modules:
  0.0 78.3 jit_solution(17383299310427516404)
XLA Ops:
  0.6 4.2 %payload.1 = (bf16[32,104,128]{2,1,0:T(8,128)(2,1)}, bf16[16,104,128]{2,1,0:T(8,128)(2,1)}, bf16[64,4,16,128]{3,2,1,0:T(8,128)(2,1)}) custom-call(bf16[3072,128]{1,0:T(8,128)(2,1)} %bitcast.5, bf16[128,128]{1,0:T(8,128)(2,1)} %constant.35.clone.table_ref, s32[32,64]{1,0:T(8,128)} %bitcast.2), custom_call_target="tpu_custom_call" | custom-call | tf_op jit(solution)/shard_map/payload/pallas_call | solution.py:691
  4.8 3.2 %collective-permute-start = (bf16[16,104,128]{2,1,0:T(8,128)(2,1)}, bf16[16,104,128]{2,1,0:T(8,128)(2,1)S(1)}, u32[]{:S(2)}, u32[]{:S(2)}) collective-permute-start(bf16[16,104,128]{2,1,0:T(8,128)(2,1)} %get-tuple-element.18), channel_id=1, source_target_pairs={{0,32},{32,0},{64,96},{96,64},{128,160},{160,128},{192,224},{224,1... | collective-permute-start | bytes 1277960 | tf_op jit(solution)/shard_map/ppermute | solution.py:666
  8.0 1.9 %collective-permute-start.2 = (bf16[64,4,16,128]{3,2,1,0:T(8,128)(2,1)}, bf16[64,4,16,128]{3,2,1,0:T(8,128)(2,1)}, u32[]{:S(2)}, u32[]{:S(2)}) collective-permute-start(bf16[64,4,16,128]{3,2,1,0:T(8,128)(2,1)} %get-tuple-element.19.own_ref), channel_id=1, source_target_pairs={{32,64},{64,32},{96,128},{128,96},{160,192},{192,160},{33,65},{65,... | collective-permute-start | bytes 3145736 | tf_op jit(solution)/shard_map/ppermute | solution.py:671
  10.0 0.1 collective-permute-start.1
  10.1 0.0 collective-permute-done
  10.1 0.0 copy-start.2
  10.1 0.8 %constant_dynamic-update-slice_fusion = bf16[32,104,128]{2,1,0:T(8,128)(2,1)} fusion(bf16[32,104,128]{2,1,0:T(8,128)(2,1)} %get-tuple-element.17, bf16[16,104,128]{2,1,0:T(8,128)(2,1)S(1)} %collective-permute-done, s32[]{:T(128)S(6)} %select_n.11), kind=kLoop, calls=%fused_computation | loop fusion | bytes 851972 | tf_op jit(solution)/shard_map/dynamic_update_slice | solution.py:704
  10.9 0.0 copy-start
  10.9 0.0 copy-start.1
  10.9 0.0 copy-start.3
  10.9 0.0 copy-start.4
  10.9 0.0 copy-start.6
  10.9 10.7 %all-to-all-start = ((bf16[32,104,128]{2,1,0:T(8,128)(2,1)}), bf16[32,104,128]{2,1,0:T(8,128)(2,1)S(1)}, u32[]{:S(2)}, u32[]{:S(2)}) async-start(bf16[32,104,128]{2,1,0:T(8,128)(2,1)} %constant_dynamic-update-slice_fusion), calls=%async_computation | async-start | bytes 1703936 | tf_op jit(solution)/shard_map/all_to_all | solution.py:707
  21.6 2.8 %collective-permute-done.2.x_ref = bf16[64,4,16,128]{3,2,1,0:T(8,128)(2,1)} collective-permute-done((bf16[64,4,16,128]{3,2,1,0:T(8,128)(2,1)}, bf16[64,4,16,128]{3,2,1,0:T(8,128)(2,1)}, u32[]{:S(2)}, u32[]{:S(2)}) %collective-permute-start.2) | collective-permute-done | bytes 1048608 | tf_op jit(solution)/shard_map/ppermute | solution.py:671
  24.5 0.0 collective-permute-done.1.core_ref
  24.5 0.0 copy-done.2
  24.5 0.0 copy-done
  24.5 0.0 copy-done.1
  24.5 0.0 copy-done.3
  24.5 0.0 copy-done.4
  24.5 0.0 copy-done.6
  24.5 17.1 %home.1 = (f32[64,416]{1,0:T(8,128)S(1)}, f32[16,64]{1,0:T(8,128)S(1)}, f32[16,64]{1,0:T(8,128)S(1)}, f32[16,64]{1,0:T(8,128)S(1)}, bf16[1,1,128]{2,1,0:T(2,128)(2,1)S(1)}) custom-call(s32[32,64]{1,0:T(8,128)S(1)} %bitcast.3, s32[32,64]{1,0:T(8,128)S(1)} %bitcast.4, f32[3,16]{1,0:T(4,128)S(1)} %copy-done.4, bf16[384,128]{1,0:T(8,128)(2,1)S(1)} %copy-done.6, ...), custom_call_target="tpu_custom_call" | custom-call | flops 10000000000 | bytes 10000000 | tf_op jit(solution)/shard_map/home/pallas_call | solution.py:713
  41.6 1.1 %all-to-all-done = bf16[32,104,128]{2,1,0:T(8,128)(2,1)S(1)} async-done(((bf16[32,104,128]{2,1,0:T(8,128)(2,1)}), bf16[32,104,128]{2,1,0:T(8,128)(2,1)S(1)}, u32[]{:S(2)}, u32[]{:S(2)}) %all-to-all-start) | async-done | bytes 852000 | tf_op jit(solution)/shard_map/all_to_all | solution.py:707
  42.7 0.0 copy-start.5
  42.7 4.2 %collective-permute-start.3 = (bf16[32,104,128]{2,1,0:T(8,128)(2,1)S(1)}, bf16[32,104,128]{2,1,0:T(8,128)(2,1)S(1)}, u32[]{:S(2)}, u32[]{:S(2)}) collective-permute-start(bf16[32,104,128]{2,1,0:T(8,128)(2,1)S(1)} %dynamic_update_slice.7.mine_ref), channel_id=1, source_target_pairs={{0,32},{32,0},{64,96},{96,64},{128,160},{160,128},{192,224},{224,1... | collective-permute-start | bytes 2555912 | tf_op jit(solution)/shard_map/ppermute | solution.py:666
  46.9 2.3 %lookup.1 = (s32[64,128]{1,0:T(8,128)S(1)}, f32[32,384]{1,0:T(8,128)S(1)}, f32[32,384]{1,0:T(8,128)S(1)}) custom-call(f32[3,16]{1,0:T(4,128)S(1)} %copy-done.4, bf16[32,104,128]{2,1,0:T(8,128)(2,1)S(1)} %dynamic_update_slice.7.mine_ref, f32[4,16384]{1,0:T(4,128)S(1)} %copy-done.3, s32[16,16384]{1,0:T(8,128)S(1)} %copy-done.1), custom_call_target="tpu_custom_call" | custom-call | flops 1000000000 | bytes 10000000 | tf_op jit(solution)/shard_map/lookup/pallas_call | solution.py:752
  49.2 0.0 collective-permute-done.3.other_ref
  49.2 0.0 copy-done.5
  49.2 11.5 %task.1.order_ref = f32[32,2,128]{2,1,0:T(2,128)} custom-call(s32[64,128]{1,0:T(8,128)S(1)} %get-tuple-element.21.id_rows, f32[32,384]{1,0:T(8,128)S(1)} %get-tuple-element.22.found_ref, f32[32,384]{1,0:T(8,128)S(1)} %get-tuple-element.23.own_terms, bf16[32,104,128]{2,1,0:T(8,128)(2,1)S(1)} %dynamic_update_slice.7.mine_ref, ...), custom_call_target="tpu_custom_call" | custom-call | flops 10000000000 | bytes 10000000 | tf_op jit(solution)/shard_map/task/pallas_call | solution.py:770
  60.7 5.1 %all-to-all-start.1 = ((f32[32,2,128]{2,1,0:T(2,128)}), f32[32,2,128]{2,1,0:T(2,128)S(1)}, u32[]{:S(2)}, u32[]{:S(2)}) async-start(f32[32,2,128]{2,1,0:T(2,128)} %task.1.order_ref), calls=%async_computation.1 | async-start | bytes 65536 | tf_op jit(solution)/shard_map/all_to_all | solution.py:789
  65.8 0.4 collective-permute-start.5
  66.2 3.2 %collective-permute-start.6 = (f32[16,64]{1,0:T(8,128)S(1)}, f32[16,64]{1,0:T(8,128)S(1)}, u32[]{:S(2)}, u32[]{:S(2)}) collective-permute-start(f32[16,64]{1,0:T(8,128)S(1)} %get-tuple-element.27), channel_id=1, source_target_pairs={{32,64},{64,32},{96,128},{128,96},{160,192},{192,160},{33,65},{65,... | collective-permute-start | bytes 12296 | tf_op jit(solution)/shard_map/ppermute | solution.py:671
  69.4 5.2 %all-to-all-done.1.kept_ref = f32[32,2,128]{2,1,0:T(2,128)S(1)} async-done(((f32[32,2,128]{2,1,0:T(2,128)}), f32[32,2,128]{2,1,0:T(2,128)S(1)}, u32[]{:S(2)}, u32[]{:S(2)}) %all-to-all-start.1) | async-done | bytes 32800 | tf_op jit(solution)/shard_map/all_to_all | solution.py:789
  74.6 1.4 %collective-permute-start.4 = (f32[32,2,128]{2,1,0:T(2,128)S(1)}, f32[32,2,128]{2,1,0:T(2,128)S(1)}, u32[]{:S(2)}, u32[]{:S(2)}) collective-permute-start(f32[32,2,128]{2,1,0:T(2,128)S(1)} %all-to-all-done.1.kept_ref), channel_id=1, source_target_pairs={{0,32},{32,0},{64,96},{96,64},{128,160},{160,128},{192,224},{224,1... | collective-permute-start | bytes 98312 | tf_op jit(solution)/shard_map/ppermute | solution.py:666
  76.0 0.0 collective-permute-done.5.core_ref
  76.0 0.0 collective-permute-done.6.x_ref
  76.0 0.8 gather.1
  76.8 0.1 collective-permute-done.4.got_ref
  76.9 1.4 %final.1 = (f32[64,512]{1,0:T(8,128)}, f32[4,64]{1,0:T(4,128)}) custom-call(f32[32,2,128]{2,1,0:T(2,128)S(1)} %all-to-all-done.1.kept_ref, f32[32,2,128]{2,1,0:T(2,128)S(1)} %collective-permute-done.4.got_ref, f32[64,128]{1,0:T(8,128)S(1)} %get-tuple-element.28.last_ref, f32[16,64]{1,0:T(8,128)S(1)} %get-tuple-element.29.sums_ref, ...), custom_call_target="tpu_custom_call", output_to_operand_aliasing={{0}: (5, {})} | custom-call | tf_op jit(solution)/shard_map/final/pallas_call | solution.py:805
  (1 shorter events, 0.0 us)
Async XLA Ops:
  4.8 5.3 %collective-permute-start = (bf16[16,104,128]{2,1,0:T(8,128)(2,1)}, bf16[16,104,128]{2,1,0:T(8,128)(2,1)S(1)}, u32[]{:S(2)}, u32[]{:S(2)}) collective-permute-start(bf16[16,104,128]{2,1,0:T(8,128)(2,1)} %get-tuple-element.18), channel_id=1, source_target_pairs={{0,32},{32,0},{64,96},{96,64},{128,160},{160,128},{192,224},{224,1... | collective-permute-start | bytes 1277960 | tf_op jit(solution)/shard_map/ppermute | solution.py:666
  8.0 16.4 %collective-permute-start.2 = (bf16[64,4,16,128]{3,2,1,0:T(8,128)(2,1)}, bf16[64,4,16,128]{3,2,1,0:T(8,128)(2,1)}, u32[]{:S(2)}, u32[]{:S(2)}) collective-permute-start(bf16[64,4,16,128]{3,2,1,0:T(8,128)(2,1)} %get-tuple-element.19.own_ref), channel_id=1, source_target_pairs={{32,64},{64,32},{96,128},{128,96},{160,192},{192,160},{33,65},{65,... | collective-permute-start | bytes 3145736 | tf_op jit(solution)/shard_map/ppermute | solution.py:671
  10.0 14.5 %collective-permute-start.1 = (bf16[64,4,16,128]{3,2,1,0:T(8,128)(2,1)}, bf16[64,4,16,128]{3,2,1,0:T(8,128)(2,1)}, u32[]{:S(2)}, u32[]{:S(2)}) collective-permute-start(bf16[64,4,16,128]{3,2,1,0:T(8,128)(2,1)} %get-tuple-element.19.own_ref), channel_id=1, source_target_pairs={{0,32},{32,0},{64,96},{96,64},{128,160},{160,128},{192,224},{224,1... | collective-permute-start | bytes 3145736 | tf_op jit(solution)/shard_map/ppermute | solution.py:666
  10.1 14.4 %copy-start.2 = (bf16[64,4,16,128]{3,2,1,0:T(8,128)(2,1)S(1)}, bf16[64,4,16,128]{3,2,1,0:T(8,128)(2,1)}, u32[]{:S(2)}) copy-start(bf16[64,4,16,128]{3,2,1,0:T(8,128)(2,1)} %get-tuple-element.19.own_ref) | copy-start | bytes 3145732
  10.9 13.6 %copy-start = (s32[64,32]{0,1:T(8,128)S(1)}, s32[64,32]{0,1:T(8,128)}, u32[]{:S(2)}) copy-start(s32[64,32]{0,1:T(8,128)} %param.9) | copy-start | bytes 24580
  10.9 13.6 %copy-start.1 = (s32[16,16384]{1,0:T(8,128)S(1)}, s32[16,16384]{1,0:T(8,128)}, u32[]{:S(2)}) copy-start(s32[16,16384]{1,0:T(8,128)} %masks_ref.3) | copy-start | bytes 3145732
  10.9 13.6 %copy-start.3 = (f32[4,16384]{1,0:T(4,128)S(1)}, f32[4,16384]{1,0:T(4,128)}, u32[]{:S(2)}) copy-start(f32[4,16384]{1,0:T(4,128)} %locations_ref.5) | copy-start | bytes 786436
  10.9 13.6 %copy-start.4 = (f32[3,16]{1,0:T(4,128)S(1)}, f32[3,16]{1,0:T(4,128)}, u32[]{:S(2)}) copy-start(f32[3,16]{1,0:T(4,128)} %stations_ref.5) | copy-start | bytes 580
  10.9 13.6 %copy-start.6 = (bf16[384,128]{1,0:T(8,128)(2,1)S(1)}, bf16[384,128]{1,0:T(8,128)(2,1)}, u32[]{:S(2)}) copy-start(bf16[384,128]{1,0:T(8,128)(2,1)} %constant.33.clone.inverse_ref) | copy-start | bytes 294916
  10.9 31.7 %all-to-all-start = ((bf16[32,104,128]{2,1,0:T(8,128)(2,1)}), bf16[32,104,128]{2,1,0:T(8,128)(2,1)S(1)}, u32[]{:S(2)}, u32[]{:S(2)}) async-start(bf16[32,104,128]{2,1,0:T(8,128)(2,1)} %constant_dynamic-update-slice_fusion), calls=%async_computation | async-start | bytes 1703936 | tf_op jit(solution)/shard_map/all_to_all | solution.py:707
  42.7 6.5 %copy-start.5 = (bf16[128,384]{1,0:T(8,128)(2,1)S(1)}, bf16[128,384]{1,0:T(8,128)(2,1)}, u32[]{:S(2)}) copy-start(bf16[128,384]{1,0:T(8,128)(2,1)} %constant.34.clone.turned_ref) | copy-start | bytes 294916
  42.7 6.5 %collective-permute-start.3 = (bf16[32,104,128]{2,1,0:T(8,128)(2,1)S(1)}, bf16[32,104,128]{2,1,0:T(8,128)(2,1)S(1)}, u32[]{:S(2)}, u32[]{:S(2)}) collective-permute-start(bf16[32,104,128]{2,1,0:T(8,128)(2,1)S(1)} %dynamic_update_slice.7.mine_ref), channel_id=1, source_target_pairs={{0,32},{32,0},{64,96},{96,64},{128,160},{160,128},{192,224},{224,1... | collective-permute-start | bytes 2555912 | tf_op jit(solution)/shard_map/ppermute | solution.py:666
  60.7 13.8 %all-to-all-start.1 = ((f32[32,2,128]{2,1,0:T(2,128)}), f32[32,2,128]{2,1,0:T(2,128)S(1)}, u32[]{:S(2)}, u32[]{:S(2)}) async-start(f32[32,2,128]{2,1,0:T(2,128)} %task.1.order_ref), calls=%async_computation.1 | async-start | bytes 65536 | tf_op jit(solution)/shard_map/all_to_all | solution.py:789
  65.8 10.2 %collective-permute-start.5 = (f32[16,64]{1,0:T(8,128)S(1)}, f32[16,64]{1,0:T(8,128)S(1)}, u32[]{:S(2)}, u32[]{:S(2)}) collective-permute-start(f32[16,64]{1,0:T(8,128)S(1)} %get-tuple-element.26), channel_id=1, source_target_pairs={{0,32},{32,0},{64,96},{96,64},{128,160},{160,128},{192,224},{224,1... | collective-permute-start | bytes 12296 | tf_op jit(solution)/shard_map/ppermute | solution.py:666
  66.2 9.8 %collective-permute-start.6 = (f32[16,64]{1,0:T(8,128)S(1)}, f32[16,64]{1,0:T(8,128)S(1)}, u32[]{:S(2)}, u32[]{:S(2)}) collective-permute-start(f32[16,64]{1,0:T(8,128)S(1)} %get-tuple-element.27), channel_id=1, source_target_pairs={{32,64},{64,32},{96,128},{128,96},{160,192},{192,160},{33,65},{65,... | collective-permute-start | bytes 12296 | tf_op jit(solution)/shard_map/ppermute | solution.py:671
  74.6 2.3 %collective-permute-start.4 = (f32[32,2,128]{2,1,0:T(2,128)S(1)}, f32[32,2,128]{2,1,0:T(2,128)S(1)}, u32[]{:S(2)}, u32[]{:S(2)}) collective-permute-start(f32[32,2,128]{2,1,0:T(2,128)S(1)} %all-to-all-done.1.kept_ref), channel_id=1, source_target_pairs={{0,32},{32,0},{64,96},{96,64},{128,160},{160,128},{192,224},{224,1... | collective-permute-start | bytes 98312 | tf_op jit(solution)/shard_map/ppermute | solution.py:666
